TPU v7x, 768 devices: a whole 4x8x12 slice. The times are simulated.
768 devices in a mesh: graph: 32 (over y, z_hi), feat: 24 (over x, z_lo, core).
Axes of the slice: x: 4, y: 8, z: 12 (z_hi: 4, z_lo: 3; z = z_hi * 3 + z_lo), core: 2. Of those that a mesh axis runs over, the one named last changes fastest.
Arguments:
- features: bfloat16 [98304, 576], P('graph', 'feat'), may hold values from -6 to 6
- adjacency: bfloat16 [98304, 384], P('graph'), may hold values from 0 to 3, as said below
- w_self: bfloat16 [576, 512], replicated, may hold values from -0.25 to 0.25
- w_neigh: bfloat16 [576, 512], replicated, may hold values from -0.5 to 0.5
- bias_out: float32 [512], replicated, may hold values from -3 to 3
- cotangent: bfloat16 [98304, 512], P(('graph', 'feat')), may hold values from -6 to 6
Outputs:
- activation: bfloat16 [98304, 512], P(('graph', 'feat'))
- grad_self: float32 [576, 512], replicated
- grad_neigh: float32 [576, 512], replicated
- grad_bias: float32 [512], replicated
- grad_feat: float32 [98304, 576], P('graph', 'feat')
Inputs may be any that keep to these rules, and one draw needn't show every extreme that they name: adjacency holds whole numbers and is the band of a symmetric matrix with a zero diagonal: adjacency[i, c] equals the entry of node (i // 128 - 1) * 128 + c for node i, and it is zero where that node lies outside 0 to 98303.
All inputs are finite; a program needn't handle non-finite values.
Results may differ from a plain program's by a relative error of at most 0.007.
Values may be sent and summed in bfloat16 or wider, within the bound.
No kernel may reach another device: no remote copies, remote signals or barrier semaphores. Data moves between devices by JAX's collectives and lax.ppermute only.
A program may use at most 32 MiB of HBM per device.

v0:
```python
import jax
import jax.numpy as jnp
from jax import lax
from jax.sharding import PartitionSpec as P

TILE = 128


def extended(block, sides, width):
    for axis, dim in sides:
        count = lax.axis_size(axis)
        forward = [(i, i + 1) for i in range(count - 1)]
        backward = [(target, source) for source, target in forward]
        low = lax.ppermute(
            lax.slice_in_dim(block, block.shape[dim] - width, None, axis=dim), axis, forward
        )
        high = lax.ppermute(lax.slice_in_dim(block, 0, width, axis=dim), axis, backward)
        block = jnp.concatenate([low, block, high], axis=dim)
    return block


def band_product(band_values, padded):
    tile_count = band_values.shape[0] // TILE
    columns = padded.shape[1]
    stacked = padded.reshape(tile_count + 2, TILE, columns)
    blocks = band_values.reshape(tile_count, TILE, 3, TILE)
    summed = jnp.zeros((tile_count, TILE, columns), jnp.float32)
    for offset in range(3):
        summed = summed + jnp.einsum(
            "tic,tcf->tif",
            blocks[:, :, offset, :],
            stacked[offset : offset + tile_count],
            preferred_element_type=jnp.float32,
        )
    return summed.reshape(tile_count * TILE, columns)


def local(features, adjacency, w_self, w_neigh, bias_out, cotangent):
    degree = 1.0 + jnp.sum(adjacency.astype(jnp.float32), axis=1, keepdims=True)
    padded = extended(features, (("graph", 0),), TILE)
    means = (band_product(adjacency, padded) / degree).astype(jnp.bfloat16)
    feat_rows, mean_rows = (
        lax.all_to_all(features, "feat", split_axis=0, concat_axis=1, tiled=True),
        lax.all_to_all(means, "feat", split_axis=0, concat_axis=1, tiled=True),
    )
    preact = (
        jnp.dot(feat_rows, w_self, preferred_element_type=jnp.float32)
        + jnp.dot(mean_rows, w_neigh, preferred_element_type=jnp.float32)
        + bias_out
    )
    sigmoid_z = jax.nn.sigmoid(preact)
    activation = (preact * sigmoid_z).astype(jnp.bfloat16)
    grad_pre = (
        cotangent.astype(jnp.float32) * sigmoid_z * (1.0 + preact * (1.0 - sigmoid_z))
    ).astype(jnp.bfloat16)
    part_self = jnp.einsum("rf,ro->fo", feat_rows, grad_pre, preferred_element_type=jnp.float32)
    part_neigh = jnp.einsum("rf,ro->fo", mean_rows, grad_pre, preferred_element_type=jnp.float32)
    part_bias = jnp.sum(grad_pre.astype(jnp.float32), axis=0)
    summed_self, summed_neigh, summed_bias = lax.psum(
        (part_self, part_neigh, part_bias), ("graph", "feat")
    )
    total_rows = features.shape[0] * lax.axis_size("graph")
    loss_scale = total_rows ** (-0.5)
    grad_self = summed_self * loss_scale
    grad_neigh = summed_neigh * loss_scale
    grad_bias = summed_bias * loss_scale
    back_self = jnp.einsum(
        "ro,fo->rf", grad_pre, w_self, preferred_element_type=jnp.float32
    ).astype(jnp.bfloat16)
    back_means = jnp.einsum(
        "ro,fo->rf", grad_pre, w_neigh, preferred_element_type=jnp.float32
    ).astype(jnp.bfloat16)
    self_cols, mean_cols = (
        lax.all_to_all(back_self, "feat", split_axis=1, concat_axis=0, tiled=True),
        lax.all_to_all(back_means, "feat", split_axis=1, concat_axis=0, tiled=True),
    )
    scaled_back = (mean_cols.astype(jnp.float32) / degree).astype(jnp.bfloat16)
    back_padded = extended(scaled_back, (("graph", 0),), TILE)
    grad_feat = self_cols.astype(jnp.float32) + band_product(adjacency, back_padded)
    return (activation, grad_self, grad_neigh, grad_bias, grad_feat)


def solution(mesh):
    in_specs = (P("graph", "feat"), P("graph", None), P(), P(), P(), P(("graph", "feat"), None))
    out_specs = (P(("graph", "feat"), None), P(), P(), P(), P("graph", "feat"))
    return jax.shard_map(local, mesh=mesh, in_specs=in_specs, out_specs=out_specs, check_vma=False)
```

profile of v0, /device:TPU:1, one launch (start us, length us, event | category | flops | bytes accessed | tf_op | source)
XLA Modules:
  0.0 581.8 jit_solution(5021688081671921797)
XLA Ops:
  7.2 0.0 copy-start
  7.2 0.8 fusion.30
  8.0 8.4 %collective-permute-start = (bf16[128,24]{0,1:T(8,128)(2,1)S(1)}, bf16[128,24]{0,1:T(8,128)(2,1)S(1)}, u32[]{:S(2)}, u32[]{:S(2)}) collective-permute-start(bf16[128,24]{0,1:T(8,128)(2,1)S(1)} %get-tuple-element.20), channel_id=1, source_target_pairs={{0,24},{24,48},{48,72},{72,96},{96,120},{120,144},{144,168},{168,1... | collective-permute-start | bytes 18440 | tf_op jit(solution)/shard_map/ppermute | solution.py:14
  16.4 1.3 collective-permute-start.1
  17.7 1.6 copy_bitcast_fusion.10
  19.3 10.2 %all-to-all-start = ((bf16[24,128,24]{1,2,0:T(8,128)(2,1)}), bf16[24,128,24]{1,2,0:T(8,128)(2,1)S(1)}, u32[]{:S(2)}, u32[]{:S(2)}) async-start(bf16[24,128,24]{1,2,0:T(8,128)(2,1)} %copy_bitcast_fusion.10), calls=%async_computation | async-start | bytes 294912 | tf_op jit(solution)/shard_map/all_to_all | solution.py:43
  29.4 0.0 copy-start.1
  29.5 7.2 %reshape.62 = bf16[24,128,3,128]{3,2,1,0:T(4,128)(2,1)} reshape(bf16[3072,384]{1,0:T(8,128)(2,1)} %param.7) | data formatting | bytes 4718592 | tf_op jit(solution)/shard_map/reshape | solution.py:26
  36.7 0.0 copy-done.1
  36.7 0.5 convert_reduce_fusion
  37.2 0.0 copy-start.7
  37.2 8.0 %fusion.28 = (bf16[24,128,1,128]{3,2,1,0:T(2,128)(2,1)S(1)}, bf16[24,128,1,128]{3,2,1,0:T(2,128)(2,1)S(1)}, bf16[24,128,1,128]{3,2,1,0:T(2,128)(2,1)S(1)}) fusion(bf16[24,128,3,128]{3,2,1,0:T(4,128)(2,1)} %reshape.62), kind=kLoop, calls=%fused_computation.56 | loop fusion | bytes 4718592 | tf_op jit(solution)/shard_map/slice | solution.py:31
  45.2 0.0 copy-start.5
  45.2 0.0 copy-start.2
  45.2 0.0 copy-done.7
  45.2 0.5 fusion.9
  45.7 0.0 collective-permute-done
  45.7 0.0 collective-permute-done.1
  45.8 0.0 copy-start.4
  45.8 0.5 fusion
  46.3 0.0 copy-done.5
  46.3 0.5 copy-done.2
  46.8 0.0 copy-start.8
  46.8 1.2 fusion.7
  48.0 0.0 all-to-all-done
  48.0 6.7 %all-to-all-start.1 = ((bf16[24,128,24]{1,2,0:T(8,128)(2,1)}), bf16[24,128,24]{1,2,0:T(8,128)(2,1)S(1)}, u32[]{:S(2)}, u32[]{:S(2)}) async-start(bf16[24,128,24]{1,2,0:T(8,128)(2,1)} %fusion.7), calls=%async_computation.1 | async-start | bytes 294912 | tf_op jit(solution)/shard_map/all_to_all | solution.py:44
  54.7 0.0 copy-done.4
  54.7 0.3 fusion.31
  55.0 7.3 %all-to-all-done.1 = bf16[24,128,24]{1,2,0:T(8,128)(2,1)S(1)} async-done(((bf16[24,128,24]{1,2,0:T(8,128)(2,1)}), bf16[24,128,24]{1,2,0:T(8,128)(2,1)S(1)}, u32[]{:S(2)}, u32[]{:S(2)}) %all-to-all-start.1) | async-done | bytes 147488 | tf_op jit(solution)/shard_map/all_to_all | solution.py:44
  62.3 0.0 copy-done
  62.3 0.0 copy-done.8
  62.3 2.0 convert_reduce_fusion.1
  64.3 1.0 convolution_convert_fusion
  65.3 1.3 fusion.32
  66.6 3.9 all-to-all-start.3
  70.5 0.0 all-reduce.3.cloned.1.call-start
  70.6 1.3 convolution_bitcast_fusion
  71.9 0.0 all-reduce.3.cloned.1.call-update
  71.9 117.9 %psum.23 = f32[512]{0:T(512)S(1)} all-reduce(f32[512]{0:T(512)S(1)} %get-tuple-element.7), channel_id=1, replica_groups=mesh['graph'=32,'feat'=24] {'graph','feat'}, use_global_device_ids=true, to_apply=%region_4.0 | all-reduce | flops 512 | bytes 4096 | tf_op jit(solution)/shard_map/psum | solution.py:59
  189.8 1.0 convolution_convert_fusion.1
  190.8 0.0 all-to-all-done.3
  190.8 4.1 all-to-all-start.2
  194.9 0.0 copy-start.6
  195.0 3.7 collective-permute-start.2
  198.7 1.3 collective-permute-start.3
  200.0 0.6 broadcast_multiply_fusion.2
  200.6 0.0 collective-permute-done.2
  200.6 4.5 collective-permute-done.3
  205.1 0.5 fusion.8
  205.7 0.0 copy-done.6
  205.7 0.0 copy-start.3
  205.7 0.5 convolution_add_fusion.1
  206.2 0.0 all-to-all-done.2
  206.2 0.9 copy-done.3
  207.1 0.5 fusion.4
  207.6 0.7 copy.87
  208.4 363.3 %all-reduce.3.cloned.1.call-done = (f32[576,512]{1,0:T(8,128)}, f32[576,512]{1,0:T(8,128)}) async-done(((f32[576,512]{1,0:T(8,128)}, f32[576,512]{1,0:T(8,128)}), (f32[576,512]{1,0:T(8,128)}, f32[576,512]{1,0:T(8,128)})) %all-reduce.3.cloned.1.call-update) | async-done | bytes 2359312 | tf_op jit(solution)/shard_map/psum | solution.py:59
  571.7 3.3 broadcast_multiply_fusion
  (5 shorter events, 0.1 us)
Async XLA Ops:
  7.2 55.2 %copy-start = (bf16[576,512]{1,0:T(8,128)(2,1)S(1)}, bf16[576,512]{1,0:T(8,128)(2,1)}, u32[]{:S(2)}) copy-start(bf16[576,512]{1,0:T(8,128)(2,1)} %param.9) | copy-start | bytes 1769476
  8.0 37.8 %collective-permute-start = (bf16[128,24]{0,1:T(8,128)(2,1)S(1)}, bf16[128,24]{0,1:T(8,128)(2,1)S(1)}, u32[]{:S(2)}, u32[]{:S(2)}) collective-permute-start(bf16[128,24]{0,1:T(8,128)(2,1)S(1)} %get-tuple-element.20), channel_id=1, source_target_pairs={{0,24},{24,48},{48,72},{72,96},{96,120},{120,144},{144,168},{168,1... | collective-permute-start | bytes 18440 | tf_op jit(solution)/shard_map/ppermute | solution.py:14
  16.4 29.3 %collective-permute-start.1 = (bf16[128,24]{0,1:T(8,128)(2,1)S(1)}, bf16[128,24]{0,1:T(8,128)(2,1)S(1)}, u32[]{:S(2)}, u32[]{:S(2)}) collective-permute-start(bf16[128,24]{0,1:T(8,128)(2,1)S(1)} %get-tuple-element.19), channel_id=1, source_target_pairs={{24,0},{48,24},{72,48},{96,72},{120,96},{144,120},{168,144},{192,1... | collective-permute-start | bytes 18440 | tf_op jit(solution)/shard_map/ppermute | solution.py:17
  19.3 28.7 %all-to-all-start = ((bf16[24,128,24]{1,2,0:T(8,128)(2,1)}), bf16[24,128,24]{1,2,0:T(8,128)(2,1)S(1)}, u32[]{:S(2)}, u32[]{:S(2)}) async-start(bf16[24,128,24]{1,2,0:T(8,128)(2,1)} %copy_bitcast_fusion.10), calls=%async_computation | async-start | bytes 294912 | tf_op jit(solution)/shard_map/all_to_all | solution.py:43
  29.4 7.2 %copy-start.1 = (bf16[3072,384]{1,0:T(8,128)(2,1)S(1)}, bf16[3072,384]{1,0:T(8,128)(2,1)}, u32[]{:S(2)}) copy-start(bf16[3072,384]{1,0:T(8,128)(2,1)} %param.7) | copy-start | bytes 7077892
  37.2 8.0 %copy-start.7 = (bf16[3072,24]{0,1:T(8,128)(2,1)S(1)}, bf16[3072,24]{0,1:T(8,128)(2,1)}, u32[]{:S(2)}) copy-start(bf16[3072,24]{0,1:T(8,128)(2,1)} %param.6) | copy-start | bytes 442372
  45.2 1.2 copy-start.5
  45.2 1.6 copy-start.2
  45.8 8.9 %copy-start.4 = (bf16[576,512]{1,0:T(8,128)(2,1)S(1)}, bf16[576,512]{1,0:T(8,128)(2,1)}, u32[]{:S(2)}) copy-start(bf16[576,512]{1,0:T(8,128)(2,1)} %param.8) | copy-start | bytes 1769476
  46.8 15.5 %copy-start.8 = (f32[512]{0:T(512)S(1)}, f32[512]{0:T(512)}, u32[]{:S(2)}) copy-start(f32[512]{0:T(512)} %param.10) | copy-start | bytes 6148
  48.0 14.3 %all-to-all-start.1 = ((bf16[24,128,24]{1,2,0:T(8,128)(2,1)}), bf16[24,128,24]{1,2,0:T(8,128)(2,1)S(1)}, u32[]{:S(2)}, u32[]{:S(2)}) async-start(bf16[24,128,24]{1,2,0:T(8,128)(2,1)} %fusion.7), calls=%async_computation.1 | async-start | bytes 294912 | tf_op jit(solution)/shard_map/all_to_all | solution.py:44
  66.6 124.2 %all-to-all-start.3 = ((bf16[128,24,24]{0,2,1:T(8,128)(2,1)}), bf16[128,24,24]{0,2,1:T(8,128)(2,1)S(1)}, u32[]{:S(2)}, u32[]{:S(2)}) async-start(bf16[128,24,24]{0,2,1:T(8,128)(2,1)} %bitcast.15), calls=%async_computation.3 | async-start | bytes 294912 | tf_op jit(solution)/shard_map/all_to_all | solution.py:75
  70.5 501.2 %all-reduce.3.cloned.1.call-start = ((), (), s32[]{:S(2)}) async-start(), calls=%async_computation.4 | async-start | bytes 4718592 | tf_op jit(solution)/shard_map/psum | solution.py:59
  190.8 15.4 %all-to-all-start.2 = ((bf16[128,24,24]{0,2,1:T(8,128)(2,1)}), bf16[128,24,24]{0,2,1:T(8,128)(2,1)S(1)}, u32[]{:S(2)}, u32[]{:S(2)}) async-start(bf16[128,24,24]{0,2,1:T(8,128)(2,1)} %bitcast.13), calls=%async_computation.2 | async-start | bytes 294912 | tf_op jit(solution)/shard_map/all_to_all | solution.py:74
  194.9 10.7 %copy-start.6 = (bf16[24,128,1,128]{3,2,1,0:T(2,128)(2,1)S(1)}, bf16[24,128,1,128]{3,2,1,0:T(2,128)(2,1)}, u32[]{:S(2)}) copy-start(bf16[24,128,1,128]{3,2,1,0:T(2,128)(2,1)} %copy-done.5) | copy-start | bytes 2359300
  195.0 5.6 collective-permute-start.2
  198.7 6.4 %collective-permute-start.3 = (bf16[128,24]{0,1:T(8,128)(2,1)S(1)}, bf16[128,24]{0,1:T(8,128)(2,1)S(1)}, u32[]{:S(2)}, u32[]{:S(2)}) collective-permute-start(bf16[128,24]{0,1:T(8,128)(2,1)S(1)} %get-tuple-element.15), channel_id=1, source_target_pairs={{24,0},{48,24},{72,48},{96,72},{120,96},{144,120},{168,144},{192,1... | collective-permute-start | bytes 18440 | tf_op jit(solution)/shard_map/ppermute | solution.py:17
  205.7 1.4 copy-start.3
Sparse Core Ops, SparseCore 0:
  77.5 494.0 all-reduce.2
where the time goes:
time: 583 us; the launch traced here: 582 us
  waiting for transfers between devices  375 us (64%)
  blocking collectives  118 us (20%)
  starting transfers between devices  39.6 us (7%)
  local copies, waits for them, and re-layouts  19.7 us (3%)
  between operations  14.3 us (2%)
  matrix products  10.6 us (2%)
    psum x1, waiting for transfers between devices, local(): lax.psum((part_self, part_neigh, part_bias), ('graph', 'feat'))  363 us
    psum x1, blocking collectives, local(): lax.psum((part_self, part_neigh, part_bias), ('graph', 'feat'))  118 us
    ppermute x2, starting transfers between devices, extended(): lax.ppermute(lax.slice_in_dim(block, block.shape[dim] - width, None, axis...  12.1 us
  transfers between devices with their start and end apart: 9, of which 3 were waited for; matrix products, arithmetic and copies ran while one was open for 4% of the time, Pallas kernels for 0%

commit v1 on v0

v1 whole, which is shorter than its diff:
```python
import jax
import jax.numpy as jnp
from jax import lax
from jax.experimental import pallas as pl
from jax.experimental.pallas import tpu as pltpu
from jax.sharding import Mesh, PartitionSpec as P

TILE = 128
BF16 = jnp.bfloat16
F32 = jnp.float32
AXES = ("y", "zh", "x", "zl", "c")
SIZES = (8, 4, 4, 3, 2)
GRAPH = ("y", "zh")
FEAT = ("x", "zl", "c")
PLANE = ("y", "x")
LINE = ("zh", "zl")
N_PLANE = 32
N_LINE = 12
N_FEAT = 24
ROWS = 72
VMEM = pl.BlockSpec(memory_space=pltpu.VMEM)
PARAMS = pltpu.CompilerParams(vmem_limit_bytes=40 * 1024 * 1024)


def dot(a, b, da, db):
    return lax.dot_general(a, b, (((da,), (db,)), ((), ())), preferred_element_type=F32)


def call(kernel, outs, n_in):
    return pl.pallas_call(
        kernel,
        out_shape=outs,
        in_specs=[VMEM] * n_in,
        out_specs=jax.tree.map(lambda _: VMEM, outs),
        compiler_params=PARAMS,
    )


def band(parts, adj):
    total = dot(parts[0], adj[:, :TILE], 1, 1)
    total += dot(parts[1], adj[:, TILE : 2 * TILE], 1, 1)
    return total + dot(parts[2], adj[:, 2 * TILE :], 1, 1)


def degrees(adj):
    return (1.0 + dot(jnp.ones((8, 3 * TILE), BF16), adj, 1, 1))[:1]


def forward_kernel(core, low, own, high, adj, ws, wn, bias, cot, act, grad, means, keep, send):
    a = adj[...]
    m = (band((low[...], own[...], high[...]), a) / degrees(a)).astype(BF16)
    means[...] = m
    x = own[...]
    pre = dot(x, ws[...], 0, 0) + dot(m, wn[...], 0, 0) + bias[...]
    s = 1.0 / (1.0 + jnp.exp(-pre))
    act[...] = (pre * s).astype(BF16)
    g = (cot[...].astype(F32) * s * (1.0 + pre * (1.0 - s))).astype(BF16)
    grad[...] = g
    first = core[0] == 0
    keep[...] = jnp.where(first, x, m)
    send[:576] = jnp.where(first, m, x)
    for b in range(4):
        send[576 + b * TILE : 576 + (b + 1) * TILE] = g[:, b * TILE : (b + 1) * TILE]


def back_kernel(grad, adj, ws, wn, back, scaled):
    g = grad[...]
    back[...] = dot(ws[...], g, 1, 1).astype(BF16)
    rounded = dot(wn[...], g, 1, 1).astype(BF16).astype(F32)
    scaled[...] = (rounded / degrees(adj[...])).astype(BF16)


def partial_kernel(keep, grad, recv, out):
    other = recv[:576]
    for b in range(4):
        g0 = grad[:, b * TILE : (b + 1) * TILE]
        g1 = recv[576 + b * TILE : 576 + (b + 1) * TILE]
        block = dot(keep[...], g0, 1, 0) + dot(other, g1, 1, 0)
        for k in range(8):
            out[b * 8 + k, :ROWS] = block[k * ROWS : (k + 1) * ROWS].astype(BF16)
    sums = [
        jnp.sum(grad[:, b * TILE : (b + 1) * TILE].astype(F32), axis=0, keepdims=True)
        + jnp.sum(recv[576 + b * TILE : 576 + (b + 1) * TILE].astype(F32), axis=0, keepdims=True)
        for b in range(4)
    ]
    tail = jnp.concatenate(sums + [jnp.zeros((4, TILE), F32)], axis=0).astype(BF16)
    for d in range(N_PLANE):
        out[d, ROWS:] = tail


def plane_kernel(recv, out):
    total = recv[0].astype(F32)
    for d in range(1, N_PLANE):
        total += recv[d].astype(F32)
    rounded = total.astype(BF16)
    for d in range(N_LINE):
        out[d] = rounded


def line_kernel(scale, recv, out, bias):
    total = recv[0].astype(F32)
    for d in range(1, N_LINE):
        total += recv[d].astype(F32)
    total *= scale
    bias[...] = total[ROWS:]
    rounded = total[:ROWS].astype(BF16)
    for d in range(N_PLANE):
        out[d] = rounded


def unpack_kernel(core, own, other, gs, gn):
    first = core[0] == 0
    for b in range(4):
        o = own[b * 576 : (b + 1) * 576].astype(F32)
        t = other[b * 576 : (b + 1) * 576].astype(F32)
        gs[:, b * TILE : (b + 1) * TILE] = jnp.where(first, o, t)
        gn[:, b * TILE : (b + 1) * TILE] = jnp.where(first, t, o)


def feat_kernel(low, own, high, adj, back, out):
    total = back[...].astype(F32) + band((low[...], own[...], high[...]), adj[...])
    out[...] = total.astype(BF16)


def split_kernel(x, out):
    for t in range(N_FEAT):
        out[t] = x[:, t * TILE : (t + 1) * TILE]


def join_kernel(x, out):
    for t in range(N_FEAT):
        out[:, t * TILE : (t + 1) * TILE] = x[t].astype(F32)


def exchange(x, axis):
    return lax.all_to_all(x, axis, split_axis=0, concat_axis=0, tiled=False)


def halos(x):
    n = 768
    low = lax.ppermute(x, AXES, [(i, i + 1) for i in range(n - 1)])
    high = lax.ppermute(x, AXES, [(i + 1, i) for i in range(n - 1)])
    return low, high


def swap(x):
    return lax.ppermute(x, "c", [(0, 1), (1, 0)])


def sds(shape, dtype=BF16):
    return jax.ShapeDtypeStruct(shape, dtype)


def local(features, adjacency, w_self, w_neigh, bias_out, cotangent):
    n_rows = features.shape[0]
    width = features.shape[1]
    f_in = width * N_FEAT
    f_out = w_self.shape[1]
    scale = (n_rows * 32) ** -0.5
    core = lax.axis_index("c").astype(jnp.int32).reshape(1)
    tile = lax.axis_index(FEAT)
    adj = lax.dynamic_slice_in_dim(adjacency, tile * TILE, TILE, axis=0)
    bias = bias_out.reshape(1, f_out)
    smem = pl.BlockSpec(memory_space=pltpu.SMEM)

    pieces = call(split_kernel, sds((N_FEAT, width, TILE)), 1)(features.T)
    own = exchange(pieces, FEAT).reshape(f_in, TILE)
    low, high = halos(own)
    act, grad, means, keep, send = pl.pallas_call(
        forward_kernel,
        out_shape=(
            sds((TILE, f_out)),
            sds((TILE, f_out)),
            sds((f_in, TILE)),
            sds((f_in, TILE)),
            sds((f_in + f_out, TILE)),
        ),
        in_specs=[smem] + [VMEM] * 8,
        out_specs=(VMEM,) * 5,
        compiler_params=PARAMS,
    )(core, low, own, high, adj, w_self, w_neigh, bias, cotangent)
    recv = swap(send)
    back, scaled = call(back_kernel, (sds((f_in, TILE)), sds((f_in, TILE))), 4)(grad, adj, w_self, w_neigh)
    partial = call(partial_kernel, sds((N_PLANE, ROWS + 8, TILE)), 3)(keep, grad, recv)
    from_plane = exchange(partial, PLANE)
    s_low, s_high = halos(scaled)
    to_line = call(plane_kernel, sds((N_LINE, ROWS + 8, TILE)), 1)(from_plane)
    from_line = exchange(to_line, LINE)
    feat_t = call(feat_kernel, sds((f_in, TILE)), 5)(s_low, scaled, s_high, adj, back)
    feat_back = exchange(feat_t.reshape(N_FEAT, width, TILE), FEAT)
    to_plane, bias_sum = call(
        lambda r, o, b: line_kernel(scale, r, o, b),
        (sds((N_PLANE, ROWS, TILE)), sds((8, TILE), F32)),
        1,
    )(from_line)
    half = exchange(to_plane, PLANE).reshape(N_PLANE * ROWS, TILE)
    other = swap(half)
    grad_self, grad_neigh = pl.pallas_call(
        unpack_kernel,
        out_shape=(sds((f_in, f_out), F32), sds((f_in, f_out), F32)),
        in_specs=[smem, VMEM, VMEM],
        out_specs=(VMEM, VMEM),
        compiler_params=PARAMS,
    )(core, half, other)
    grad_bias = bias_sum[:4].reshape(f_out)
    grad_feat = call(join_kernel, sds((width, n_rows), F32), 1)(feat_back).T
    return act, grad_self, grad_neigh, grad_bias, grad_feat


def solution(mesh):
    grid = Mesh(mesh.devices.reshape(SIZES), AXES)
    in_specs = (P(GRAPH, FEAT), P(GRAPH, None), P(), P(), P(), P(GRAPH + FEAT, None))
    out_specs = (P(GRAPH + FEAT, None), P(), P(), P(), P(GRAPH, FEAT))
    return jax.shard_map(local, mesh=grid, in_specs=in_specs, out_specs=out_specs, check_vma=False)
```

time: 583 us -> 142 us (0.24)
  waiting for transfers between devices: 375 us -> 17 us
  blocking collectives: 118 us -> 72.8 us
  between operations: 14.3 us -> 0.83 us
  local copies, waits for them, and re-layouts: 19.7 us -> 8.64 us
  matrix products: 10.6 us -> 0 us
  Pallas kernels: 0 us -> 7.34 us
    psum x1 -> x0, waiting for transfers between devices: 363 us -> none  [local(): lax.psum((part_self, part_neigh, part_bias), ('graph', 'feat'))]
    psum x1 -> x0, blocking collectives: 118 us -> none  [local(): lax.psum((part_self, part_neigh, part_bias), ('graph', 'feat'))]
    all_to_all x0 -> x3, blocking collectives: none -> 72.8 us  [exchange(): return lax.all_to_all(x, axis, split_axis=0, concat_axis=0, tiled=False)]
    dot_general x12 -> x0, matrix products: 10.6 us -> none  [the longest x6 3.79 us: band_product(): jnp.einsum('tic,tcf->tif', blocks[:, :, offset, :], stacked[offset:offset...]
    slice x3 -> x0, local copies, waits for them, and re-layouts: 8.75 us -> none  [the longest x1 7.98 us: band_product(): blocks[:, :, offset, :]]
    all_to_all x4 -> x2, starting transfers between devices: 24.9 us -> 17 us  [exchange(): return lax.all_to_all(x, axis, split_axis=0, concat_axis=0, tiled=False)]
    pallas_call x0 -> x9, Pallas kernels: none -> 7.34 us  [the longest x1 2.79 us: local(): pl.pallas_call(unpack_kernel, out_shape=(sds((f_in, f_out), F32), sds((f_...]
    ppermute x4 -> x6, waiting for transfers between devices: 4.55 us -> 11.5 us  [the longest x2 9.69 us: halos(): high = lax.ppermute(x, AXES, [(i + 1, i) for i in range(n - 1)])]
  transfers between devices with their start and end apart: 9 -> 8, of which waited for: 3 -> 6; matrix products, arithmetic and copies ran while one was open for 4% -> 0% of each run, Pallas kernels for 0% -> 2%
where the time goes in v1:
time: 142 us; the launch traced here: 141 us
  blocking collectives  72.8 us (51%)
  starting transfers between devices  34.4 us (24%)
  waiting for transfers between devices  17 us (12%)
  local copies, waits for them, and re-layouts  8.64 us (6%)
  Pallas kernels  7.34 us (5%)
    all_to_all x3, blocking collectives, exchange(): return lax.all_to_all(x, axis, split_axis=0, concat_axis=0, tiled=False)  72.8 us
    all_to_all x2, starting transfers between devices, exchange(): return lax.all_to_all(x, axis, split_axis=0, concat_axis=0, tiled=False)  17 us
    ppermute x2, waiting for transfers between devices, halos(): high = lax.ppermute(x, AXES, [(i + 1, i) for i in range(n - 1)])  9.69 us
    ppermute x2, starting transfers between devices, halos(): low = lax.ppermute(x, AXES, [(i, i + 1) for i in range(n - 1)])  9.55 us
    unnamed x26, local copies, waits for them, and re-layouts  8.04 us
    all_to_all x2, waiting for transfers between devices, exchange(): return lax.all_to_all(x, axis, split_axis=0, concat_axis=0, tiled=False)  5.53 us
    ppermute x2, starting transfers between devices, swap(): return lax.ppermute(x, 'c', [(0, 1), (1, 0)])  4 us
    ppermute x2, starting transfers between devices, halos(): high = lax.ppermute(x, AXES, [(i + 1, i) for i in range(n - 1)])  3.84 us
  transfers between devices with their start and end apart: 8, of which 6 were waited for; matrix products, arithmetic and copies ran while one was open for 0% of the time, Pallas kernels for 2%

profile of v1, /device:TPU:1, one launch (start us, length us, event | category | flops | bytes accessed | tf_op | source)
XLA Modules:
  0.0 140.9 jit_solution(6600618505056967253)
XLA Ops:
  0.6 0.0 copy-start
  0.6 0.0 copy-start.10
  0.7 1.1 copy-done.10
  1.7 20.9 %all_to_all.25 = bf16[24,24,128]{2,1,0:T(8,128)(2,1)S(1)} all-to-all(bf16[24,24,128]{2,1,0:T(8,128)(2,1)S(1)} %shard_map.101), channel_id=1, replica_groups=mesh['y'=8,'zh'=4,'x'=4,'zl'=3,'c'=2] {'x','zl','c'}, dimensions={0} | all-to-all | bytes 294912 | tf_op jit(solution)/shard_map/all_to_all | solution.py:136
  22.6 3.0 %collective-permute-start = (bf16[576,128]{1,0:T(8,128)(2,1)S(1)}, bf16[576,128]{1,0:T(8,128)(2,1)S(1)}, u32[]{:S(2)}, u32[]{:S(2)}) collective-permute-start(bf16[576,128]{1,0:T(8,128)(2,1)S(1)} %bitcast.9), channel_id=1, source_target_pairs={{0,1},{1,2},{2,3},{3,4},{4,5},{5,6},{6,7},{7,8},{8,9},{9,10},{10,1... | collective-permute-start | bytes 442376 | tf_op jit(solution)/shard_map/ppermute | solution.py:141
  25.6 1.9 %collective-permute-start.1 = (bf16[576,128]{1,0:T(8,128)(2,1)S(1)}, bf16[576,128]{1,0:T(8,128)(2,1)S(1)}, u32[]{:S(2)}, u32[]{:S(2)}) collective-permute-start(bf16[576,128]{1,0:T(8,128)(2,1)S(1)} %bitcast.10), channel_id=1, source_target_pairs={{1,0},{2,1},{3,2},{4,3},{5,4},{6,5},{7,6},{8,7},{9,8},{10,9},{11,1... | collective-permute-start | bytes 442376 | tf_op jit(solution)/shard_map/ppermute | solution.py:142
  27.6 0.0 copy-done
  27.6 0.0 copy-start.5
  27.6 0.1 collective-permute-done.low
  27.7 4.4 %collective-permute-done.1.high = bf16[576,128]{1,0:T(8,128)(2,1)S(1)} collective-permute-done((bf16[576,128]{1,0:T(8,128)(2,1)S(1)}, bf16[576,128]{1,0:T(8,128)(2,1)S(1)}, u32[]{:S(2)}, u32[]{:S(2)}) %collective-permute-start.1) | collective-permute-done | bytes 147488 | tf_op jit(solution)/shard_map/ppermute | solution.py:142
  32.1 0.0 copy-start.1
  32.1 1.1 copy-done.1
  33.2 0.0 copy-start.3
  33.2 1.1 copy-done.3
  34.2 0.0 copy-start.11
  34.2 0.9 copy-done.11
  35.1 0.0 copy-start.12
  35.1 0.7 copy-done.12
  35.8 1.7 %shard_map.102 = (bf16[128,512]{1,0:T(8,128)(2,1)}, bf16[128,512]{1,0:T(8,128)(2,1)S(1)}, bf16[576,128]{1,0:T(8,128)(2,1)}, bf16[576,128]{1,0:T(8,128)(2,1)S(1)}, bf16[1088,128]{1,0:T(8,128)(2,1)S(1)}) custom-call(s32[1]{0:T(128)} %bitcast.core, bf16[576,128]{1,0:T(8,128)(2,1)S(1)} %collective-permute-done.low, bf16[576,128]{1,0:T(8,128)(2,1)S(1)} %bitcast.11, ...), custom_call_target="tpu_custom_call" | custom-call | tf_op jit(solution)/shard_map/pallas_call | solution.py:169
  37.5 1.9 %collective-permute-start.2 = (bf16[1088,128]{1,0:T(8,128)(2,1)S(1)}, bf16[1088,128]{1,0:T(8,128)(2,1)S(1)}, u32[]{:S(2)}, u32[]{:S(2)}) collective-permute-start(bf16[1088,128]{1,0:T(8,128)(2,1)S(1)} %get-tuple-element.18), channel_id=1, source_target_pairs={{0,1},{1,0},{2,3},{3,2},{4,5},{5,4},{6,7},{7,6},{8,9},{9,8},{10,11... | collective-permute-start | bytes 835592 | tf_op jit(solution)/shard_map/ppermute | solution.py:147
  39.5 1.5 %collective-permute-done.2.recv = bf16[1088,128]{1,0:T(8,128)(2,1)S(1)} collective-permute-done((bf16[1088,128]{1,0:T(8,128)(2,1)S(1)}, bf16[1088,128]{1,0:T(8,128)(2,1)S(1)}, u32[]{:S(2)}, u32[]{:S(2)}) %collective-permute-start.2) | collective-permute-done | bytes 278560 | tf_op jit(solution)/shard_map/ppermute | solution.py:147
  41.0 0.0 copy-done.5
  41.0 0.5 shard_map.103
  41.4 0.0 copy-start.8
  41.5 0.6 copy-done.8
  42.1 0.0 copy-start.2
  42.1 0.0 copy-start.4
  42.1 28.7 %all_to_all.26.recv = bf16[32,80,128]{2,1,0:T(8,128)(2,1)S(1)} all-to-all(bf16[32,80,128]{2,1,0:T(8,128)(2,1)S(1)} %shard_map.103), channel_id=1, replica_groups=mesh['y'=8,'zh'=4,'x'=4,'zl'=3,'c'=2] {'y','x'}, dimensions={0} | all-to-all | bytes 1310720 | tf_op jit(solution)/shard_map/all_to_all | solution.py:136
  70.8 0.1 shard_map.104
  70.9 23.2 %all_to_all.27.r = bf16[12,80,128]{2,1,0:T(8,128)(2,1)S(1)} all-to-all(bf16[12,80,128]{2,1,0:T(8,128)(2,1)S(1)} %shard_map.104), channel_id=1, replica_groups=mesh['y'=8,'zh'=4,'x'=4,'zl'=3,'c'=2] {'zh','zl'}, dimensions={0} | all-to-all | bytes 491520 | tf_op jit(solution)/shard_map/all_to_all | solution.py:136
  94.1 0.1 shard_map.105
  94.1 0.0 copy-start.7
  94.2 0.8 copy-done.7
  95.0 7.2 %all-to-all-start.3 = ((bf16[32,72,128]{2,1,0:T(8,128)(2,1)}), bf16[32,72,128]{2,1,0:T(8,128)(2,1)}, u32[]{:S(2)}, u32[]{:S(2)}) async-start(bf16[32,72,128]{2,1,0:T(8,128)(2,1)} %copy-done.7), calls=%async_computation.3 | async-start | bytes 1179648 | tf_op jit(solution)/shard_map/all_to_all | solution.py:136
  102.2 0.0 copy-done.2
  102.2 0.0 copy-done.4
  102.2 0.0 copy-start.6
  102.2 0.9 copy-done.6
  103.1 0.0 copy-start.9
  103.1 0.9 copy-done.9
  104.0 0.5 shard_map.107
  104.5 6.6 %collective-permute-start.4 = (bf16[576,128]{1,0:T(8,128)(2,1)S(1)}, bf16[576,128]{1,0:T(8,128)(2,1)S(1)}, u32[]{:S(2)}, u32[]{:S(2)}) collective-permute-start(bf16[576,128]{1,0:T(8,128)(2,1)S(1)} %get-tuple-element.23.own), channel_id=1, source_target_pairs={{0,1},{1,2},{2,3},{3,4},{4,5},{5,6},{6,7},{7,8},{8,9},{9,10},{10,1... | collective-permute-start | bytes 442376 | tf_op jit(solution)/shard_map/ppermute | solution.py:141
  111.1 1.9 %collective-permute-start.5 = (bf16[576,128]{1,0:T(8,128)(2,1)S(1)}, bf16[576,128]{1,0:T(8,128)(2,1)S(1)}, u32[]{:S(2)}, u32[]{:S(2)}) collective-permute-start(bf16[576,128]{1,0:T(8,128)(2,1)S(1)} %get-tuple-element.23.own), channel_id=1, source_target_pairs={{1,0},{2,1},{3,2},{4,3},{5,4},{6,5},{7,6},{8,7},{9,8},{10,9},{11,1... | collective-permute-start | bytes 442376 | tf_op jit(solution)/shard_map/ppermute | solution.py:142
  113.0 0.2 collective-permute-done.4.low
  113.2 5.3 %collective-permute-done.5.high = bf16[576,128]{1,0:T(8,128)(2,1)S(1)} collective-permute-done((bf16[576,128]{1,0:T(8,128)(2,1)S(1)}, bf16[576,128]{1,0:T(8,128)(2,1)S(1)}, u32[]{:S(2)}, u32[]{:S(2)}) %collective-permute-start.5) | collective-permute-done | bytes 147488 | tf_op jit(solution)/shard_map/ppermute | solution.py:142
  118.5 0.9 shard_map.108
  119.4 0.0 all-to-all-done.3
  119.4 9.8 %all-to-all-start.4 = ((bf16[24,24,128]{2,1,0:T(8,128)(2,1)}), bf16[24,24,128]{2,1,0:T(8,128)(2,1)S(1)}, u32[]{:S(2)}, u32[]{:S(2)}) async-start(bf16[24,24,128]{2,1,0:T(8,128)(2,1)} %bitcast.6), calls=%async_computation.4 | async-start | bytes 294912 | tf_op jit(solution)/shard_map/all_to_all | solution.py:136
  129.2 2.1 %collective-permute-start.3 = (bf16[2304,128]{1,0:T(8,128)(2,1)}, bf16[2304,128]{1,0:T(8,128)(2,1)S(1)}, u32[]{:S(2)}, u32[]{:S(2)}) collective-permute-start(bf16[2304,128]{1,0:T(8,128)(2,1)} %bitcast.4.own), channel_id=1, source_target_pairs={{0,1},{1,0},{2,3},{3,2},{4,5},{5,4},{6,7},{7,6},{8,9},{9,8},{10,11... | collective-permute-start | bytes 1769480 | tf_op jit(solution)/shard_map/ppermute | solution.py:147
  131.3 5.5 %all-to-all-done.4.x = bf16[24,24,128]{2,1,0:T(8,128)(2,1)S(1)} async-done(((bf16[24,24,128]{2,1,0:T(8,128)(2,1)}), bf16[24,24,128]{2,1,0:T(8,128)(2,1)S(1)}, u32[]{:S(2)}, u32[]{:S(2)}) %all-to-all-start.4) | async-done | bytes 147488 | tf_op jit(solution)/shard_map/all_to_all | solution.py:136
  136.8 0.7 shard_map.109
  137.6 0.6 slice_bitcast_fusion
  138.2 0.0 collective-permute-done.3.other
  138.2 2.8 %shard_map.106 = (f32[576,512]{1,0:T(8,128)}, f32[576,512]{1,0:T(8,128)}) custom-call(s32[1]{0:T(128)} %bitcast.core, bf16[2304,128]{1,0:T(8,128)(2,1)} %bitcast.4.own, bf16[2304,128]{1,0:T(8,128)(2,1)S(1)} %collective-permute-done.3.other), custom_call_target="tpu_custom_call" | custom-call | tf_op jit(solution)/shard_map/pallas_call | solution.py:198
  (2 shorter events, 0.0 us)
Async XLA Ops:
  0.6 26.9 %copy-start = (bf16[3072,384]{1,0:T(8,128)(2,1)S(1)}, bf16[3072,384]{1,0:T(8,128)(2,1)}, u32[]{:S(2)}) copy-start(bf16[3072,384]{1,0:T(8,128)(2,1)} %param.7) | copy-start | bytes 7077892
  0.6 1.1 copy-start.10
  22.6 5.1 %collective-permute-start = (bf16[576,128]{1,0:T(8,128)(2,1)S(1)}, bf16[576,128]{1,0:T(8,128)(2,1)S(1)}, u32[]{:S(2)}, u32[]{:S(2)}) collective-permute-start(bf16[576,128]{1,0:T(8,128)(2,1)S(1)} %bitcast.9), channel_id=1, source_target_pairs={{0,1},{1,2},{2,3},{3,4},{4,5},{5,6},{6,7},{7,8},{8,9},{9,10},{10,1... | collective-permute-start | bytes 442376 | tf_op jit(solution)/shard_map/ppermute | solution.py:141
  25.6 6.5 %collective-permute-start.1 = (bf16[576,128]{1,0:T(8,128)(2,1)S(1)}, bf16[576,128]{1,0:T(8,128)(2,1)S(1)}, u32[]{:S(2)}, u32[]{:S(2)}) collective-permute-start(bf16[576,128]{1,0:T(8,128)(2,1)S(1)} %bitcast.10), channel_id=1, source_target_pairs={{1,0},{2,1},{3,2},{4,3},{5,4},{6,5},{7,6},{8,7},{9,8},{10,9},{11,1... | collective-permute-start | bytes 442376 | tf_op jit(solution)/shard_map/ppermute | solution.py:142
  27.6 13.4 %copy-start.5 = (bf16[128,384]{1,0:T(8,128)(2,1)}, bf16[128,384]{1,0:T(8,128)(2,1)S(1)}, u32[]{:S(2)}) copy-start(bf16[128,384]{1,0:T(8,128)(2,1)S(1)} %constant_dynamic-slice_fusion.adj) | copy-start | bytes 294916
  32.1 1.1 copy-start.1
  33.2 1.1 copy-start.3
  34.2 0.9 copy-start.11
  35.1 0.7 copy-start.12
  37.5 3.4 %collective-permute-start.2 = (bf16[1088,128]{1,0:T(8,128)(2,1)S(1)}, bf16[1088,128]{1,0:T(8,128)(2,1)S(1)}, u32[]{:S(2)}, u32[]{:S(2)}) collective-permute-start(bf16[1088,128]{1,0:T(8,128)(2,1)S(1)} %get-tuple-element.18), channel_id=1, source_target_pairs={{0,1},{1,0},{2,3},{3,2},{4,5},{5,4},{6,7},{7,6},{8,9},{9,8},{10,11... | collective-permute-start | bytes 835592 | tf_op jit(solution)/shard_map/ppermute | solution.py:147
  41.4 0.7 copy-start.8
  42.1 60.1 %copy-start.2 = (bf16[576,512]{1,0:T(8,128)(2,1)S(1)}, bf16[576,512]{1,0:T(8,128)(2,1)}, u32[]{:S(2)}) copy-start(bf16[576,512]{1,0:T(8,128)(2,1)} %ws.3) | copy-start | bytes 1769476
  42.1 60.1 %copy-start.4 = (bf16[576,512]{1,0:T(8,128)(2,1)S(1)}, bf16[576,512]{1,0:T(8,128)(2,1)}, u32[]{:S(2)}) copy-start(bf16[576,512]{1,0:T(8,128)(2,1)} %wn.3) | copy-start | bytes 1769476
  94.1 0.8 copy-start.7
  95.0 24.5 %all-to-all-start.3 = ((bf16[32,72,128]{2,1,0:T(8,128)(2,1)}), bf16[32,72,128]{2,1,0:T(8,128)(2,1)}, u32[]{:S(2)}, u32[]{:S(2)}) async-start(bf16[32,72,128]{2,1,0:T(8,128)(2,1)} %copy-done.7), calls=%async_computation.3 | async-start | bytes 1179648 | tf_op jit(solution)/shard_map/all_to_all | solution.py:136
  102.2 0.9 copy-start.6
  103.1 0.9 copy-start.9
  104.5 8.7 %collective-permute-start.4 = (bf16[576,128]{1,0:T(8,128)(2,1)S(1)}, bf16[576,128]{1,0:T(8,128)(2,1)S(1)}, u32[]{:S(2)}, u32[]{:S(2)}) collective-permute-start(bf16[576,128]{1,0:T(8,128)(2,1)S(1)} %get-tuple-element.23.own), channel_id=1, source_target_pairs={{0,1},{1,2},{2,3},{3,4},{4,5},{5,6},{6,7},{7,8},{8,9},{9,10},{10,1... | collective-permute-start | bytes 442376 | tf_op jit(solution)/shard_map/ppermute | solution.py:141
  111.1 7.4 %collective-permute-start.5 = (bf16[576,128]{1,0:T(8,128)(2,1)S(1)}, bf16[576,128]{1,0:T(8,128)(2,1)S(1)}, u32[]{:S(2)}, u32[]{:S(2)}) collective-permute-start(bf16[576,128]{1,0:T(8,128)(2,1)S(1)} %get-tuple-element.23.own), channel_id=1, source_target_pairs={{1,0},{2,1},{3,2},{4,3},{5,4},{6,5},{7,6},{8,7},{9,8},{10,9},{11,1... | collective-permute-start | bytes 442376 | tf_op jit(solution)/shard_map/ppermute | solution.py:142
  119.4 17.4 %all-to-all-start.4 = ((bf16[24,24,128]{2,1,0:T(8,128)(2,1)}), bf16[24,24,128]{2,1,0:T(8,128)(2,1)S(1)}, u32[]{:S(2)}, u32[]{:S(2)}) async-start(bf16[24,24,128]{2,1,0:T(8,128)(2,1)} %bitcast.6), calls=%async_computation.4 | async-start | bytes 294912 | tf_op jit(solution)/shard_map/all_to_all | solution.py:136
  129.2 8.9 %collective-permute-start.3 = (bf16[2304,128]{1,0:T(8,128)(2,1)}, bf16[2304,128]{1,0:T(8,128)(2,1)S(1)}, u32[]{:S(2)}, u32[]{:S(2)}) collective-permute-start(bf16[2304,128]{1,0:T(8,128)(2,1)} %bitcast.4.own), channel_id=1, source_target_pairs={{0,1},{1,0},{2,3},{3,2},{4,5},{5,4},{6,7},{7,6},{8,9},{9,8},{10,11... | collective-permute-start | bytes 1769480 | tf_op jit(solution)/shard_map/ppermute | solution.py:147

commit v2 on v1

v2 whole, which is shorter than its diff:
```python
import jax
import jax.numpy as jnp
from jax import lax
from jax.experimental import pallas as pl
from jax.experimental.pallas import tpu as pltpu
from jax.sharding import Mesh, PartitionSpec as P

TILE = 128
BF16 = jnp.bfloat16
F32 = jnp.float32
AXES = ("y", "zh", "x", "zl", "c")
SIZES = (8, 4, 4, 3, 2)
GRAPH = ("y", "zh")
FEAT = ("x", "zl", "c")
BLOCK = ("x", "zl")
N_BLOCK = 12
N_Y = 8
N_ZH = 4
N_FEAT = 24
ROWS = 192
TAIL = 8
SMEM = pl.BlockSpec(memory_space=pltpu.SMEM)
ANY = pl.BlockSpec(memory_space=pl.ANY)
VMEM = pl.BlockSpec(memory_space=pltpu.VMEM)
PARAMS = pltpu.CompilerParams(vmem_limit_bytes=32 * 1024 * 1024)


def dot(a, b, da, db):
    return lax.dot_general(a, b, (((da,), (db,)), ((), ())), preferred_element_type=F32)


def call(kernel, specs, outs, scratch=(), **kw):
    return pl.pallas_call(
        kernel,
        out_shape=outs,
        in_specs=list(specs),
        out_specs=kw.pop("out_specs", jax.tree.map(lambda _: VMEM, outs)),
        scratch_shapes=list(scratch),
        compiler_params=PARAMS,
        **kw,
    )


def sds(shape, dtype=BF16):
    return jax.ShapeDtypeStruct(shape, dtype)


def lanes(b):
    return slice(b * TILE, (b + 1) * TILE)


def band(parts, adj):
    total = dot(parts[0], adj[:, lanes(0)], 1, 1)
    total += dot(parts[1], adj[:, lanes(1)], 1, 1)
    return total + dot(parts[2], adj[:, lanes(2)], 1, 1)


def prepare_kernel(tile, feats, adjacency, out, adj, held, sems):
    rows = pl.ds(pl.multiple_of(tile[0] * TILE, TILE), TILE)
    copies = (
        pltpu.make_async_copy(feats, held, sems.at[0]),
        pltpu.make_async_copy(adjacency.at[rows], adj, sems.at[1]),
    )
    for c in copies:
        c.start()
    copies[0].wait()
    for t in range(N_FEAT):
        out[t] = held[:, lanes(t)]
    copies[1].wait()


def forward_kernel(
    core, low, own, high, adj, ws_hbm, wn_hbm, bias_hbm, cot_hbm,
    act, grad, keep, send, back, scaled,
    ws, wn, bias, cot, sems,
):
    pairs = ((ws_hbm, ws), (wn_hbm, wn), (bias_hbm, bias), (cot_hbm, cot))
    copies = [pltpu.make_async_copy(s, d, sems.at[i]) for i, (s, d) in enumerate(pairs)]
    for c in copies:
        c.start()
    a = adj[...]
    degree = (1.0 + dot(jnp.ones((8, 3 * TILE), BF16), a, 1, 1))[:1]
    m = (band((low[...], own[...], high[...]), a) / degree).astype(BF16)
    x = own[...]
    for c in copies:
        c.wait()
    pre = dot(x, ws[...], 0, 0) + dot(m, wn[...], 0, 0) + bias[...]
    s = 1.0 / (1.0 + jnp.exp(-pre))
    act[...] = (pre * s).astype(BF16)
    g = (cot[...].astype(F32) * s * (1.0 + pre * (1.0 - s))).astype(BF16)
    grad[...] = g
    first = core[0] == 0
    keep[...] = jnp.where(first, x, m)
    send[:576] = jnp.where(first, m, x)
    for b in range(4):
        send[576 + b * TILE : 576 + (b + 1) * TILE] = g[:, lanes(b)]
    back[...] = dot(ws[...], g, 1, 1).astype(BF16)
    rounded = dot(wn[...], g, 1, 1).astype(BF16).astype(F32)
    scaled[...] = (rounded / degree).astype(BF16)


def partial_kernel(keep, grad, recv, out):
    other = recv[:576]
    sums = []
    for b in range(4):
        g0 = grad[:, lanes(b)]
        g1 = recv[576 + b * TILE : 576 + (b + 1) * TILE]
        block = dot(keep[...], g0, 1, 0) + dot(other, g1, 1, 0)
        for k in range(3):
            out[b * 3 + k, :ROWS] = block[k * ROWS : (k + 1) * ROWS].astype(BF16)
        sums.append(
            jnp.sum(g0.astype(F32), axis=0, keepdims=True)
            + jnp.sum(g1.astype(F32), axis=0, keepdims=True)
        )
    tail = jnp.concatenate(sums + [jnp.zeros((TAIL - 4, TILE), F32)], axis=0).astype(BF16)
    for d in range(N_BLOCK):
        out[d, ROWS:] = tail


def sum_kernel(recv, out):
    total = recv[0].astype(F32)
    for d in range(1, recv.shape[0]):
        total += recv[d].astype(F32)
    rounded = total.astype(BF16)
    for d in range(out.shape[0]):
        out[d] = rounded


def last_sum_kernel(scale, core, recv, keep, other, out, bias):
    total = recv[0].astype(F32)
    for d in range(1, N_ZH):
        total += recv[d].astype(F32)
    total *= scale
    bias[...] = total[ROWS:]
    rounded = total[:ROWS].astype(BF16)
    first = core[0] == 0
    for d in range(N_BLOCK):
        out[d, :ROWS] = rounded
        k = keep[d].astype(F32)
        o = other[d].astype(F32)
        pair = jnp.concatenate([jnp.where(first, k, o), jnp.where(first, o, k)], axis=0)
        out[d, ROWS:] = pair.astype(BF16)


def halves(block, held):
    for d in range(N_BLOCK):
        rows = slice((d % 3) * ROWS, (d % 3 + 1) * ROWS)
        held[rows, lanes(d // 3)] = block[d, :ROWS].astype(F32)


def own_kernel(core, block, gs, gn, gf, held, sem):
    halves(block, held)
    first = core[0] == 0

    @pl.when(first)
    def _():
        pltpu.make_async_copy(held, gs, sem).start()

    @pl.when(jnp.logical_not(first))
    def _():
        pltpu.make_async_copy(held, gn, sem).start()

    width = gf.shape[0]
    for d in range(N_BLOCK):
        pair = block[d, ROWS:].astype(F32)
        gf[:, lanes(2 * d)] = pair[:width]
        gf[:, lanes(2 * d + 1)] = pair[width:]
    pltpu.make_async_copy(held, gs, sem).wait()


def other_kernel(core, block, gs_in, gn_in, gs, gn, held, sem):
    halves(block, held)
    first = core[0] == 0

    @pl.when(first)
    def _():
        pltpu.make_async_copy(held, gn, sem).start()

    @pl.when(jnp.logical_not(first))
    def _():
        pltpu.make_async_copy(held, gs, sem).start()

    pltpu.make_async_copy(held, gs, sem).wait()


def feat_kernel(core, low, own, high, adj, back, keep, send):
    total = back[...].astype(F32) + band((low[...], own[...], high[...]), adj[...])
    first = core[0] == 0
    width = total.shape[0] // N_FEAT
    for d in range(N_BLOCK):
        even = total[2 * d * width : (2 * d + 1) * width]
        odd = total[(2 * d + 1) * width : (2 * d + 2) * width]
        keep[d] = jnp.where(first, even, odd).astype(BF16)
        send[d] = jnp.where(first, odd, even).astype(BF16)


def exchange(x, axis):
    return lax.all_to_all(x, axis, split_axis=0, concat_axis=0, tiled=False)


def halos(x):
    n = 768
    low = lax.ppermute(x, AXES, [(i, i + 1) for i in range(n - 1)])
    high = lax.ppermute(x, AXES, [(i + 1, i) for i in range(n - 1)])
    return low, high


def swap(x):
    return lax.ppermute(x, "c", [(0, 1), (1, 0)])


def local(features, adjacency, w_self, w_neigh, bias_out, cotangent):
    n_rows, width = features.shape
    f_in, f_out = w_self.shape
    scale = (n_rows * 32) ** -0.5
    core = lax.axis_index("c").astype(jnp.int32).reshape(1)
    tile = lax.axis_index(FEAT).astype(jnp.int32).reshape(1)
    dma = pltpu.SemaphoreType.DMA
    wide = sds((f_in, TILE))
    weight = sds((f_in, f_out), F32)

    pieces, adj = call(
        prepare_kernel,
        [SMEM, ANY, ANY],
        (sds((N_FEAT, width, TILE)), sds((TILE, 3 * TILE))),
        [pltpu.VMEM((width, n_rows), BF16), dma((2,))],
    )(tile, features.T, adjacency)
    own = exchange(pieces, FEAT).reshape(f_in, TILE)
    low, high = halos(own)
    act, grad, keep, send, back, scaled = call(
        forward_kernel,
        [SMEM] + [VMEM] * 4 + [ANY] * 4,
        (sds((TILE, f_out)), sds((TILE, f_out)), wide, sds((f_in + f_out, TILE)), wide, wide),
        [
            pltpu.VMEM((f_in, f_out), BF16),
            pltpu.VMEM((f_in, f_out), BF16),
            pltpu.VMEM((1, f_out), F32),
            pltpu.VMEM((TILE, f_out), BF16),
            dma((4,)),
        ],
    )(core, low, own, high, adj, w_self, w_neigh, bias_out.reshape(1, f_out), cotangent)
    recv = swap(send)
    s_low, s_high = halos(scaled)
    partial = call(partial_kernel, [VMEM] * 3, sds((N_BLOCK, ROWS + TAIL, TILE)))(keep, grad, recv)
    from_block = exchange(partial, BLOCK)
    slab = sds((N_BLOCK, width, TILE))
    from_block, s_low, s_high = lax.optimization_barrier((from_block, s_low, s_high))
    f_keep, f_send = call(feat_kernel, [SMEM] + [VMEM] * 5, (slab, slab))(
        core, s_low, scaled, s_high, adj, back
    )
    f_recv = swap(f_send)
    from_y = exchange(call(sum_kernel, [VMEM], sds((N_Y, ROWS + TAIL, TILE)))(from_block), "y")
    from_y, f_recv = lax.optimization_barrier((from_y, f_recv))
    from_zh = exchange(call(sum_kernel, [VMEM], sds((N_ZH, ROWS + TAIL, TILE)))(from_y), "zh")
    to_block, bias_sum = call(
        lambda *refs: last_sum_kernel(scale, *refs),
        [SMEM] + [VMEM] * 3,
        (sds((N_BLOCK, ROWS + 2 * width, TILE)), sds((TAIL, TILE), F32)),
    )(core, from_zh, f_keep, f_recv)
    block = exchange(to_block, BLOCK)
    other = swap(block)
    held = [pltpu.VMEM((f_in, f_out), F32), dma]
    gs, gn, gf = call(
        own_kernel,
        [SMEM, VMEM],
        (weight, weight, sds((width, n_rows), F32)),
        held,
        out_specs=(ANY, ANY, VMEM),
    )(core, block)
    grad_self, grad_neigh = call(
        other_kernel,
        [SMEM, VMEM, ANY, ANY],
        (weight, weight),
        held,
        out_specs=(ANY, ANY),
        input_output_aliases={2: 0, 3: 1},
    )(core, other, gs, gn)
    return act, grad_self, grad_neigh, bias_sum[:4].reshape(f_out), gf.T


def solution(mesh):
    grid = Mesh(mesh.devices.reshape(SIZES), AXES)
    in_specs = (P(GRAPH, FEAT), P(GRAPH, None), P(), P(), P(), P(GRAPH + FEAT, None))
    out_specs = (P(GRAPH + FEAT, None), P(), P(), P(), P(GRAPH, FEAT))
    return jax.shard_map(local, mesh=grid, in_specs=in_specs, out_specs=out_specs, check_vma=False)
```

time: 142 us -> 137 us (0.965)
  blocking collectives: 72.8 us -> 59.5 us
  starting transfers between devices: 34.4 us -> 43.8 us
  local copies, waits for them, and re-layouts: 8.64 us -> 3.16 us
  waiting for transfers between devices: 17 us -> 21.2 us
    all_to_all x3, blocking collectives: 72.8 us -> 59.5 us  [exchange(): return lax.all_to_all(x, axis, split_axis=0, concat_axis=0, tiled=False)]
    ppermute x2 -> x3, starting transfers between devices: 4 us -> 10.1 us  [swap(): return lax.ppermute(x, 'c', [(0, 1), (1, 0)])]
    unnamed x26 -> x12, local copies, waits for them, and re-layouts: 8.04 us -> 2.58 us
    all_to_all x2, starting transfers between devices: 17 us -> 22 us  [exchange(): return lax.all_to_all(x, axis, split_axis=0, concat_axis=0, tiled=False)]
    ppermute x2, starting transfers between devices: 9.55 us -> 6.76 us  [halos(): low = lax.ppermute(x, AXES, [(i, i + 1) for i in range(n - 1)])]
    all_to_all x2, waiting for transfers between devices: 5.53 us -> 7.93 us  [exchange(): return lax.all_to_all(x, axis, split_axis=0, concat_axis=0, tiled=False)]
  transfers between devices with their start and end apart: 8 -> 9, of which waited for: 6 -> 6; matrix products, arithmetic and copies ran while one was open for 0% -> 0% of each run, Pallas kernels for 2% -> 2%
where the time goes in v2:
time: 137 us
  blocking collectives  59.5 us (43%)
  starting transfers between devices  43.8 us (32%)
  waiting for transfers between devices  21.2 us (15%)
  Pallas kernels  8.4 us (6%)
  local copies, waits for them, and re-layouts  3.16 us (2%)
    all_to_all x3, blocking collectives, exchange(): return lax.all_to_all(x, axis, split_axis=0, concat_axis=0, tiled=False)  59.5 us
    all_to_all x2, starting transfers between devices, exchange(): return lax.all_to_all(x, axis, split_axis=0, concat_axis=0, tiled=False)  22 us
    ppermute x3, starting transfers between devices, swap(): return lax.ppermute(x, 'c', [(0, 1), (1, 0)])  10.1 us
    ppermute x2, waiting for transfers between devices, halos(): high = lax.ppermute(x, AXES, [(i + 1, i) for i in range(n - 1)])  9.62 us
    all_to_all x2, waiting for transfers between devices, exchange(): return lax.all_to_all(x, axis, split_axis=0, concat_axis=0, tiled=False)  7.93 us
    ppermute x2, starting transfers between devices, halos(): low = lax.ppermute(x, AXES, [(i, i + 1) for i in range(n - 1)])  6.76 us
    ppermute x2, starting transfers between devices, halos(): high = lax.ppermute(x, AXES, [(i + 1, i) for i in range(n - 1)])  4.85 us
  transfers between devices with their start and end apart: 9, of which 6 were waited for; matrix products, arithmetic and copies ran while one was open for 0% of the time, Pallas kernels for 2%

profile of v2, /device:TPU:1, one launch (start us, length us, event | category | flops | bytes accessed | tf_op | source)
XLA Modules:
  0.0 136.8 jit_solution(6695892191485298477)
XLA Ops:
  0.6 0.0 copy-start
  0.7 1.7 %copy-done = bf16[3072,384]{1,0:T(8,128)(2,1)S(1)} copy-done((bf16[3072,384]{1,0:T(8,128)(2,1)S(1)}, bf16[3072,384]{1,0:T(8,128)(2,1)}, u32[]{:S(2)}) %copy-start) | copy-done | bytes 2359320
  2.3 0.0 copy-start.3
  2.3 0.9 copy-done.3
  3.2 0.0 copy-start.1
  3.2 0.0 copy-start.2
  3.2 0.0 copy-start.4
  3.2 0.0 copy-start.5
  3.2 0.4 shard_map.101
  3.6 21.0 %all_to_all.25 = bf16[24,24,128]{2,1,0:T(8,128)(2,1)S(1)} all-to-all(bf16[24,24,128]{2,1,0:T(8,128)(2,1)S(1)} %get-tuple-element.27), channel_id=1, replica_groups=mesh['y'=8,'zh'=4,'x'=4,'zl'=3,'c'=2] {'x','zl','c'}, dimensions={0} | all-to-all | bytes 294912 | tf_op jit(solution)/shard_map/all_to_all | solution.py:198
  24.6 2.3 %collective-permute-start.1 = (bf16[576,128]{1,0:T(8,128)(2,1)S(1)}, bf16[576,128]{1,0:T(8,128)(2,1)S(1)}, u32[]{:S(2)}, u32[]{:S(2)}) collective-permute-start(bf16[576,128]{1,0:T(8,128)(2,1)S(1)} %bitcast.8), channel_id=1, source_target_pairs={{1,0},{2,1},{3,2},{4,3},{5,4},{6,5},{7,6},{8,7},{9,8},{10,9},{11,1... | collective-permute-start | bytes 442376 | tf_op jit(solution)/shard_map/ppermute | solution.py:204
  26.9 3.3 %collective-permute-start = (bf16[576,128]{1,0:T(8,128)(2,1)S(1)}, bf16[576,128]{1,0:T(8,128)(2,1)S(1)}, u32[]{:S(2)}, u32[]{:S(2)}) collective-permute-start(bf16[576,128]{1,0:T(8,128)(2,1)S(1)} %bitcast.9), channel_id=1, source_target_pairs={{0,1},{1,2},{2,3},{3,4},{4,5},{5,6},{6,7},{7,8},{8,9},{9,10},{10,1... | collective-permute-start | bytes 442376 | tf_op jit(solution)/shard_map/ppermute | solution.py:203
  30.2 0.9 collective-permute-done.1.high
  31.1 1.2 collective-permute-done.low
  32.3 0.0 copy-done.1
  32.3 0.0 copy-done.2
  32.3 0.0 copy-done.4
  32.3 0.0 copy-done.5
  32.3 2.4 %shard_map.102 = (bf16[128,512]{1,0:T(8,128)(2,1)}, bf16[128,512]{1,0:T(8,128)(2,1)S(1)}, bf16[576,128]{1,0:T(8,128)(2,1)S(1)}, bf16[1088,128]{1,0:T(8,128)(2,1)...) custom-call(s32[1]{0:T(128)} %bitcast.core.refs_0_, bf16[576,128]{1,0:T(8,128)(2,1)S(1)} %collective-permute-done.low, ...), custom_call_target="tpu_custom_call" | custom-call | tf_op jit(solution)/shard_map/pallas_call | solution.py:230
  34.8 1.9 %collective-permute-start.2 = (bf16[1088,128]{1,0:T(8,128)(2,1)S(1)}, bf16[1088,128]{1,0:T(8,128)(2,1)S(1)}, u32[]{:S(2)}, u32[]{:S(2)}) collective-permute-start(bf16[1088,128]{1,0:T(8,128)(2,1)S(1)} %get-tuple-element.32), channel_id=1, source_target_pairs={{0,1},{1,0},{2,3},{3,2},{4,5},{5,4},{6,7},{7,6},{8,9},{9,8},{10,11... | collective-permute-start | bytes 835592 | tf_op jit(solution)/shard_map/ppermute | solution.py:209
  36.7 1.5 %collective-permute-done.2.recv = bf16[1088,128]{1,0:T(8,128)(2,1)S(1)} collective-permute-done((bf16[1088,128]{1,0:T(8,128)(2,1)S(1)}, bf16[1088,128]{1,0:T(8,128)(2,1)S(1)}, u32[]{:S(2)}, u32[]{:S(2)}) %collective-permute-start.2) | collective-permute-done | bytes 278560 | tf_op jit(solution)/shard_map/ppermute | solution.py:209
  38.2 1.3 shard_map.103
  39.5 6.5 %all-to-all-start.1 = ((bf16[12,200,128]{2,1,0:T(8,128)(2,1)}), bf16[12,200,128]{2,1,0:T(8,128)(2,1)S(1)}, u32[]{:S(2)}, u32[]{:S(2)}) async-start(bf16[12,200,128]{2,1,0:T(8,128)(2,1)} %shard_map.103), calls=%async_computation.1 | async-start | bytes 1228800 | tf_op jit(solution)/shard_map/all_to_all | solution.py:198
  46.0 2.6 %collective-permute-start.4 = (bf16[576,128]{1,0:T(8,128)(2,1)S(1)}, bf16[576,128]{1,0:T(8,128)(2,1)S(1)}, u32[]{:S(2)}, u32[]{:S(2)}) collective-permute-start(bf16[576,128]{1,0:T(8,128)(2,1)S(1)} %get-tuple-element.33.own), channel_id=1, source_target_pairs={{1,0},{2,1},{3,2},{4,3},{5,4},{6,5},{7,6},{8,7},{9,8},{10,9},{11,1... | collective-permute-start | bytes 442376 | tf_op jit(solution)/shard_map/ppermute | solution.py:204
  48.5 3.5 %collective-permute-start.3 = (bf16[576,128]{1,0:T(8,128)(2,1)S(1)}, bf16[576,128]{1,0:T(8,128)(2,1)S(1)}, u32[]{:S(2)}, u32[]{:S(2)}) collective-permute-start(bf16[576,128]{1,0:T(8,128)(2,1)S(1)} %get-tuple-element.33.own), channel_id=1, source_target_pairs={{0,1},{1,2},{2,3},{3,4},{4,5},{5,6},{6,7},{7,8},{8,9},{9,10},{10,1... | collective-permute-start | bytes 442376 | tf_op jit(solution)/shard_map/ppermute | solution.py:203
  52.0 8.7 %collective-permute-done.4.high = bf16[576,128]{1,0:T(8,128)(2,1)S(1)} collective-permute-done((bf16[576,128]{1,0:T(8,128)(2,1)S(1)}, bf16[576,128]{1,0:T(8,128)(2,1)S(1)}, u32[]{:S(2)}, u32[]{:S(2)}) %collective-permute-start.4) | collective-permute-done | bytes 147488 | tf_op jit(solution)/shard_map/ppermute | solution.py:204
  60.8 0.0 collective-permute-done.3.low
  60.8 0.0 all-to-all-done.1.recv
  60.8 0.8 shard_map.104
  61.6 15.6 %all-to-all-start.2 = ((bf16[8,200,128]{2,1,0:T(8,128)(2,1)}), bf16[8,200,128]{2,1,0:T(8,128)(2,1)S(1)}, u32[]{:S(2)}, u32[]{:S(2)}) async-start(bf16[8,200,128]{2,1,0:T(8,128)(2,1)} %shard_map.104), calls=%async_computation.2 | async-start | bytes 819200 | tf_op jit(solution)/shard_map/all_to_all | solution.py:198
  77.2 0.3 shard_map.105
  77.5 3.7 %collective-permute-start.5 = (bf16[12,24,128]{2,1,0:T(8,128)(2,1)S(1)}, bf16[12,24,128]{2,1,0:T(8,128)(2,1)S(1)}, u32[]{:S(2)}, u32[]{:S(2)}) collective-permute-start(bf16[12,24,128]{2,1,0:T(8,128)(2,1)S(1)} %get-tuple-element.38), channel_id=1, source_target_pairs={{0,1},{1,0},{2,3},{3,2},{4,5},{5,4},{6,7},{7,6},{8,9},{9,8},{10,11... | collective-permute-start | bytes 221192 | tf_op jit(solution)/shard_map/ppermute | solution.py:209
  81.2 0.9 collective-permute-done.5.refs_3_
  82.1 7.9 %all-to-all-done.2.recv = bf16[8,200,128]{2,1,0:T(8,128)(2,1)S(1)} async-done(((bf16[8,200,128]{2,1,0:T(8,128)(2,1)}), bf16[8,200,128]{2,1,0:T(8,128)(2,1)S(1)}, u32[]{:S(2)}, u32[]{:S(2)}) %all-to-all-start.2) | async-done | bytes 409632 | tf_op jit(solution)/shard_map/all_to_all | solution.py:198
  90.0 0.1 shard_map.106
  90.0 12.6 %all_to_all.26.refs_1_ = bf16[4,200,128]{2,1,0:T(8,128)(2,1)S(1)} all-to-all(bf16[4,200,128]{2,1,0:T(8,128)(2,1)S(1)} %shard_map.106), channel_id=1, replica_groups=mesh['y'=8,'zh'=4,'x'=4,'zl'=3,'c'=2] {'zh'}, dimensions={0} | all-to-all | bytes 409600 | tf_op jit(solution)/shard_map/all_to_all | solution.py:198
  102.6 0.1 shard_map.107
  102.7 25.8 %all_to_all.27.block = bf16[12,240,128]{2,1,0:T(8,128)(2,1)S(1)} all-to-all(bf16[12,240,128]{2,1,0:T(8,128)(2,1)S(1)} %get-tuple-element.42), channel_id=1, replica_groups=mesh['y'=8,'zh'=4,'x'=4,'zl'=3,'c'=2] {'x','zl'}, dimensions={0} | all-to-all | bytes 1474560 | tf_op jit(solution)/shard_map/all_to_all | solution.py:198
  128.6 4.5 %collective-permute-start.6 = (bf16[12,240,128]{2,1,0:T(8,128)(2,1)S(1)}, bf16[12,240,128]{2,1,0:T(8,128)(2,1)S(1)}, u32[]{:S(2)}, u32[]{:S(2)}) collective-permute-start(bf16[12,240,128]{2,1,0:T(8,128)(2,1)S(1)} %all_to_all.27.block), channel_id=1, source_target_pairs={{0,1},{1,0},{2,3},{3,2},{4,5},{5,4},{6,7},{7,6},{8,9},{9,8},{10,11... | collective-permute-start | bytes 2211848 | tf_op jit(solution)/shard_map/ppermute | solution.py:209
  133.1 0.6 slice_bitcast_fusion
  133.7 1.9 %shard_map.108 = (f32[576,512]{1,0:T(8,128)}, f32[576,512]{1,0:T(8,128)}, f32[24,3072]{1,0:T(8,128)}) custom-call(s32[1]{0:T(128)} %bitcast.core.refs_0_, bf16[12,240,128]{2,1,0:T(8,128)(2,1)S(1)} %all_to_all.27.block), custom_call_target="tpu_custom_call" | custom-call | tf_op jit(solution)/shard_map/pallas_call | solution.py:263
  135.6 0.0 collective-permute-done.6.block
  135.6 1.2 shard_map.109
Async XLA Ops:
  0.6 1.7 %copy-start = (bf16[3072,384]{1,0:T(8,128)(2,1)S(1)}, bf16[3072,384]{1,0:T(8,128)(2,1)}, u32[]{:S(2)}) copy-start(bf16[3072,384]{1,0:T(8,128)(2,1)} %adjacency.1) | copy-start | bytes 7077892
  2.3 0.9 copy-start.3
  3.2 29.1 %copy-start.1 = (bf16[576,512]{1,0:T(8,128)(2,1)S(1)}, bf16[576,512]{1,0:T(8,128)(2,1)}, u32[]{:S(2)}) copy-start(bf16[576,512]{1,0:T(8,128)(2,1)} %ws_hbm.1) | copy-start | bytes 1769476
  3.2 29.1 %copy-start.2 = (bf16[576,512]{1,0:T(8,128)(2,1)S(1)}, bf16[576,512]{1,0:T(8,128)(2,1)}, u32[]{:S(2)}) copy-start(bf16[576,512]{1,0:T(8,128)(2,1)} %wn_hbm.1) | copy-start | bytes 1769476
  3.2 29.1 %copy-start.4 = (bf16[128,512]{1,0:T(8,128)(2,1)S(1)}, bf16[128,512]{1,0:T(8,128)(2,1)}, u32[]{:S(2)}) copy-start(bf16[128,512]{1,0:T(8,128)(2,1)} %cot_hbm.1) | copy-start | bytes 393220
  3.2 29.1 %copy-start.5 = (f32[512]{0:T(512)S(1)}, f32[512]{0:T(512)}, u32[]{:S(2)}) copy-start(f32[512]{0:T(512)} %param.10) | copy-start | bytes 6148
  24.6 6.5 %collective-permute-start.1 = (bf16[576,128]{1,0:T(8,128)(2,1)S(1)}, bf16[576,128]{1,0:T(8,128)(2,1)S(1)}, u32[]{:S(2)}, u32[]{:S(2)}) collective-permute-start(bf16[576,128]{1,0:T(8,128)(2,1)S(1)} %bitcast.8), channel_id=1, source_target_pairs={{1,0},{2,1},{3,2},{4,3},{5,4},{6,5},{7,6},{8,7},{9,8},{10,9},{11,1... | collective-permute-start | bytes 442376 | tf_op jit(solution)/shard_map/ppermute | solution.py:204
  26.9 5.3 %collective-permute-start = (bf16[576,128]{1,0:T(8,128)(2,1)S(1)}, bf16[576,128]{1,0:T(8,128)(2,1)S(1)}, u32[]{:S(2)}, u32[]{:S(2)}) collective-permute-start(bf16[576,128]{1,0:T(8,128)(2,1)S(1)} %bitcast.9), channel_id=1, source_target_pairs={{0,1},{1,2},{2,3},{3,4},{4,5},{5,6},{6,7},{7,8},{8,9},{9,10},{10,1... | collective-permute-start | bytes 442376 | tf_op jit(solution)/shard_map/ppermute | solution.py:203
  34.8 3.5 %collective-permute-start.2 = (bf16[1088,128]{1,0:T(8,128)(2,1)S(1)}, bf16[1088,128]{1,0:T(8,128)(2,1)S(1)}, u32[]{:S(2)}, u32[]{:S(2)}) collective-permute-start(bf16[1088,128]{1,0:T(8,128)(2,1)S(1)} %get-tuple-element.32), channel_id=1, source_target_pairs={{0,1},{1,0},{2,3},{3,2},{4,5},{5,4},{6,7},{7,6},{8,9},{9,8},{10,11... | collective-permute-start | bytes 835592 | tf_op jit(solution)/shard_map/ppermute | solution.py:209
  39.5 21.3 %all-to-all-start.1 = ((bf16[12,200,128]{2,1,0:T(8,128)(2,1)}), bf16[12,200,128]{2,1,0:T(8,128)(2,1)S(1)}, u32[]{:S(2)}, u32[]{:S(2)}) async-start(bf16[12,200,128]{2,1,0:T(8,128)(2,1)} %shard_map.103), calls=%async_computation.1 | async-start | bytes 1228800 | tf_op jit(solution)/shard_map/all_to_all | solution.py:198
  46.0 14.8 %collective-permute-start.4 = (bf16[576,128]{1,0:T(8,128)(2,1)S(1)}, bf16[576,128]{1,0:T(8,128)(2,1)S(1)}, u32[]{:S(2)}, u32[]{:S(2)}) collective-permute-start(bf16[576,128]{1,0:T(8,128)(2,1)S(1)} %get-tuple-element.33.own), channel_id=1, source_target_pairs={{1,0},{2,1},{3,2},{4,3},{5,4},{6,5},{7,6},{8,7},{9,8},{10,9},{11,1... | collective-permute-start | bytes 442376 | tf_op jit(solution)/shard_map/ppermute | solution.py:204
  48.5 12.2 %collective-permute-start.3 = (bf16[576,128]{1,0:T(8,128)(2,1)S(1)}, bf16[576,128]{1,0:T(8,128)(2,1)S(1)}, u32[]{:S(2)}, u32[]{:S(2)}) collective-permute-start(bf16[576,128]{1,0:T(8,128)(2,1)S(1)} %get-tuple-element.33.own), channel_id=1, source_target_pairs={{0,1},{1,2},{2,3},{3,4},{4,5},{5,6},{6,7},{7,8},{8,9},{9,10},{10,1... | collective-permute-start | bytes 442376 | tf_op jit(solution)/shard_map/ppermute | solution.py:203
  61.6 28.4 %all-to-all-start.2 = ((bf16[8,200,128]{2,1,0:T(8,128)(2,1)}), bf16[8,200,128]{2,1,0:T(8,128)(2,1)S(1)}, u32[]{:S(2)}, u32[]{:S(2)}) async-start(bf16[8,200,128]{2,1,0:T(8,128)(2,1)} %shard_map.104), calls=%async_computation.2 | async-start | bytes 819200 | tf_op jit(solution)/shard_map/all_to_all | solution.py:198
  77.5 4.6 %collective-permute-start.5 = (bf16[12,24,128]{2,1,0:T(8,128)(2,1)S(1)}, bf16[12,24,128]{2,1,0:T(8,128)(2,1)S(1)}, u32[]{:S(2)}, u32[]{:S(2)}) collective-permute-start(bf16[12,24,128]{2,1,0:T(8,128)(2,1)S(1)} %get-tuple-element.38), channel_id=1, source_target_pairs={{0,1},{1,0},{2,3},{3,2},{4,5},{5,4},{6,7},{7,6},{8,9},{9,8},{10,11... | collective-permute-start | bytes 221192 | tf_op jit(solution)/shard_map/ppermute | solution.py:209
  128.6 7.0 %collective-permute-start.6 = (bf16[12,240,128]{2,1,0:T(8,128)(2,1)S(1)}, bf16[12,240,128]{2,1,0:T(8,128)(2,1)S(1)}, u32[]{:S(2)}, u32[]{:S(2)}) collective-permute-start(bf16[12,240,128]{2,1,0:T(8,128)(2,1)S(1)} %all_to_all.27.block), channel_id=1, source_target_pairs={{0,1},{1,0},{2,3},{3,2},{4,5},{5,4},{6,7},{7,6},{8,9},{9,8},{10,11... | collective-permute-start | bytes 2211848 | tf_op jit(solution)/shard_map/ppermute | solution.py:209

commit v3 on v2

v3 whole, which is shorter than its diff:
```python
import jax
import jax.numpy as jnp
from jax import lax
from jax.experimental import pallas as pl
from jax.experimental.pallas import tpu as pltpu
from jax.sharding import Mesh, PartitionSpec as P

TILE = 128
BF16 = jnp.bfloat16
F32 = jnp.float32
AXES = ("y", "zh", "x", "zl", "c")
SIZES = (8, 4, 4, 3, 2)
GRAPH = ("y", "zh")
FEAT = ("x", "zl", "c")
LINE = ("zh", "zl")
N_X = 4
N_Y = 8
N_LINE = 12
N_FEAT = 24
ROWS = 72
TAIL = 8
SMEM = pl.BlockSpec(memory_space=pltpu.SMEM)
ANY = pl.BlockSpec(memory_space=pl.ANY)
VMEM = pl.BlockSpec(memory_space=pltpu.VMEM)
PARAMS = pltpu.CompilerParams(vmem_limit_bytes=32 * 1024 * 1024)


def dot(a, b, da, db):
    return lax.dot_general(a, b, (((da,), (db,)), ((), ())), preferred_element_type=F32)


def call(kernel, specs, outs, scratch=(), **kw):
    return pl.pallas_call(
        kernel,
        out_shape=outs,
        in_specs=list(specs),
        out_specs=kw.pop("out_specs", jax.tree.map(lambda _: VMEM, outs)),
        scratch_shapes=list(scratch),
        compiler_params=kw.pop("params", PARAMS),
        **kw,
    )


def sds(shape, dtype=BF16):
    return jax.ShapeDtypeStruct(shape, dtype)


def lanes(b):
    return slice(b * TILE, (b + 1) * TILE)


def band(parts, adj):
    return dot(jnp.concatenate(parts, axis=1), adj, 1, 1)


def prepare_kernel(feats, out):
    for t in range(N_FEAT):
        out[t] = feats[:, lanes(t)]


def load_kernel(tile, adjacency, *refs):
    rows = pl.ds(pl.multiple_of(tile[0] * TILE, TILE), TILE)
    sems = refs[-1]
    sources = (adjacency.at[rows],) + refs[:4]
    copies = [
        pltpu.make_async_copy(s, d, sems.at[i])
        for i, (s, d) in enumerate(zip(sources, refs[4:-1], strict=True))
    ]
    for c in copies:
        c.start()
    for c in copies:
        c.wait()


def forward_kernel(
    core, low, own, high, adj, ws, wn, bias, cot, act, grad, keep, send, back, scaled
):
    a = adj[...]
    degree = (1.0 + dot(jnp.ones((8, 3 * TILE), BF16), a, 1, 1))[:1]
    m = (band((low[...], own[...], high[...]), a) / degree).astype(BF16)
    x = own[...]
    pre = dot(x, ws[...], 0, 0) + dot(m, wn[...], 0, 0) + bias[...]
    s = 1.0 / (1.0 + jnp.exp(-pre))
    act[...] = (pre * s).astype(BF16)
    g = (cot[...].astype(F32) * s * (1.0 + pre * (1.0 - s))).astype(BF16)
    grad[...] = g
    first = core[0] == 0
    keep[...] = jnp.where(first, x, m)
    send[:576] = jnp.where(first, m, x)
    for b in range(4):
        send[576 + b * TILE : 576 + (b + 1) * TILE] = g[:, lanes(b)]
    back[...] = dot(ws[...], g, 1, 1).astype(BF16)
    rounded = dot(wn[...], g, 1, 1).astype(BF16).astype(F32)
    scaled[...] = (rounded / degree).astype(BF16)


def partial_kernel(keep, grad, recv, out):
    f_in = keep.shape[0]
    rows = [recv[f_in + b * TILE : f_in + (b + 1) * TILE] for b in range(N_X)]
    g = jnp.concatenate([grad[...], jnp.concatenate(rows, axis=1)], axis=0)
    total = dot(jnp.concatenate([keep[...], recv[:f_in]], axis=1), g, 1, 0)
    sums = jnp.sum(g.astype(F32), axis=0, keepdims=True)
    parts = [sums[:, lanes(b)] for b in range(N_X)]
    tail = jnp.concatenate(parts + [jnp.zeros((TAIL - N_X, TILE), F32)], axis=0)
    for b in range(N_X):
        out[b] = jnp.concatenate([total[:, lanes(b)], tail], axis=0).astype(BF16)


def summed(recv):
    total = recv[0].astype(F32)
    for d in range(1, recv.shape[0]):
        total += recv[d].astype(F32)
    return total


def x_kernel(recv, out):
    total = summed(recv)
    tail = total[N_Y * ROWS :]
    for d in range(N_Y):
        out[d] = jnp.concatenate([total[d * ROWS : (d + 1) * ROWS], tail], axis=0).astype(BF16)


def y_kernel(recv, out):
    rounded = summed(recv).astype(BF16)
    for d in range(N_LINE):
        out[d] = rounded


def line_kernel(scale, recv, out, bias):
    total = summed(recv) * scale
    bias[...] = jnp.concatenate([total[ROWS + b : ROWS + b + 1] for b in range(N_X)], axis=1)
    rounded = total[:ROWS].astype(BF16)
    for d in range(N_Y):
        out[d] = rounded


def feat_kernel(core, low, own, high, adj, back, keep, send):
    total = back[...].astype(F32) + band((low[...], own[...], high[...]), adj[...])
    first = core[0] == 0
    width = total.shape[0] // N_FEAT
    for d in range(N_LINE):
        even = total[2 * d * width : (2 * d + 1) * width]
        odd = total[(2 * d + 1) * width : (2 * d + 2) * width]
        keep[d % 3, d // 3] = jnp.where(first, even, odd).astype(BF16)
        send[d % 3, d // 3] = jnp.where(first, odd, even).astype(BF16)


def pair_kernel(core, zl, keep, other, stay, up, down):
    first = core[0] == 0
    for shift, out in enumerate((stay, up, down)):
        at = lax.rem(zl[0] + shift, 3)
        for d in range(N_X):
            k = keep[at, d].astype(F32)
            o = other[at, d].astype(F32)
            pair = jnp.concatenate([jnp.where(first, k, o), jnp.where(first, o, k)], axis=0)
            out[d] = pair.astype(BF16)


def join_kernel(zl, grads, stay, low, high, out):
    f_in = grads.shape[0]
    pair = stay.shape[1]
    whole = grads[...]
    place = zl[0]
    for d in range(N_X):
        out[d, :f_in] = whole
        for p in range(3):
            far = jnp.where(place == (p + 1) % 3, low[d], high[d])
            out[d, f_in + p * pair : f_in + (p + 1) * pair] = jnp.where(place == p, stay[d], far)


def halves(block, held, copies):
    for d in range(N_X):
        held[:, lanes(d)] = block[d, : held.shape[0]].astype(F32)
        copies(d)


def send_half(held, sems, first, yes, no):
    def copies(d):
        @pl.when(first)
        def _():
            pltpu.make_async_copy(held.at[:, lanes(d)], yes.at[:, lanes(d)], sems.at[d]).start()

        @pl.when(jnp.logical_not(first))
        def _():
            pltpu.make_async_copy(held.at[:, lanes(d)], no.at[:, lanes(d)], sems.at[d]).start()

    return copies


def finish(held, sems, out):
    for d in range(N_X):
        pltpu.make_async_copy(held.at[:, lanes(d)], out.at[:, lanes(d)], sems.at[d]).wait()


def own_kernel(core, block, gs, gn, gf, held, sems):
    halves(block, held, send_half(held, sems, core[0] == 0, gs, gn))
    f_in = held.shape[0]
    width = gf.shape[0]
    for d in range(N_X):
        part = block[d, f_in:].astype(F32)
        for k in range(6):
            gf[:, lanes(6 * d + k)] = part[k * width : (k + 1) * width]
    finish(held, sems, gs)


def other_kernel(core, block, gs_in, gn_in, gs, gn, held, sems):
    halves(block, held, send_half(held, sems, core[0] == 0, gn, gs))
    finish(held, sems, gs)


def exchange(x, axis):
    return lax.all_to_all(x, axis, split_axis=0, concat_axis=0, tiled=False)


def halos(x):
    n = 768
    low = lax.ppermute(x, AXES, [(i, i + 1) for i in range(n - 1)])
    high = lax.ppermute(x, AXES, [(i + 1, i) for i in range(n - 1)])
    return low, high


def swap(x):
    return lax.ppermute(x, "c", [(0, 1), (1, 0)])


def local(features, adjacency, w_self, w_neigh, bias_out, cotangent):
    n_rows, width = features.shape
    f_in, f_out = w_self.shape
    scale = (n_rows * 32) ** -0.5
    core = lax.axis_index("c").astype(jnp.int32).reshape(1)
    tile = lax.axis_index(FEAT).astype(jnp.int32).reshape(1)
    dma = pltpu.SemaphoreType.DMA
    wide = sds((f_in, TILE))
    weight = sds((f_in, f_out), F32)

    pieces = call(prepare_kernel, [VMEM], sds((N_FEAT, width, TILE)))(features.T)
    own = exchange(pieces, FEAT).reshape(f_in, TILE)
    held = call(
        load_kernel,
        [SMEM] + [ANY] * 5,
        (
            sds((TILE, 3 * TILE)),
            sds((f_in, f_out)),
            sds((f_in, f_out)),
            sds((1, f_out), F32),
            sds((TILE, f_out)),
        ),
        [dma((5,))],
        params=pltpu.CompilerParams(vmem_limit_bytes=52 * 1024 * 1024),
    )(tile, adjacency, w_self, w_neigh, bias_out.reshape(1, f_out), cotangent)
    own, held = lax.optimization_barrier((own, held))
    adj = held[0]
    low, high = halos(own)
    act, grad, keep, send, back, scaled = call(
        forward_kernel,
        [SMEM] + [VMEM] * 8,
        (sds((TILE, f_out)), sds((TILE, f_out)), wide, sds((f_in + f_out, TILE)), wide, wide),
    )(core, low, own, high, *held)
    recv = swap(send)
    s_low, s_high = halos(scaled)
    partial = call(partial_kernel, [VMEM] * 3, sds((N_X, f_in + TAIL, TILE)))(keep, grad, recv)
    from_x = exchange(partial, "x")
    from_x, s_low, s_high = lax.optimization_barrier((from_x, s_low, s_high))
    from_y = exchange(call(x_kernel, [VMEM], sds((N_Y, ROWS + TAIL, TILE)))(from_x), "y")
    slab = sds((3, N_X, width, TILE))
    f_keep, f_send = call(feat_kernel, [SMEM] + [VMEM] * 5, (slab, slab))(
        core, s_low, scaled, s_high, adj, back
    )
    f_recv = swap(f_send)
    from_y, f_recv = lax.optimization_barrier((from_y, f_recv))
    from_line = exchange(call(y_kernel, [VMEM], sds((N_LINE, ROWS + TAIL, TILE)))(from_y), LINE)
    zl = lax.axis_index("zl").astype(jnp.int32).reshape(1)
    pair = sds((N_X, 2 * width, TILE))
    stay, up, down = call(pair_kernel, [SMEM] * 2 + [VMEM] * 2, (pair,) * 3)(core, zl, f_keep, f_recv)
    f_low = lax.ppermute(up, "zl", [(i, (i + 1) % 3) for i in range(3)])
    f_high = lax.ppermute(down, "zl", [(i, (i + 2) % 3) for i in range(3)])
    from_line, f_low, f_high = lax.optimization_barrier((from_line, f_low, f_high))
    to_y, bias_sum = call(
        lambda *refs: line_kernel(scale, *refs),
        [VMEM],
        (sds((N_Y, ROWS, TILE)), sds((1, f_out), F32)),
    )(from_line)
    column = exchange(to_y, "y").reshape(f_in, TILE)
    to_x = call(join_kernel, [SMEM] + [VMEM] * 4, sds((N_X, f_in + 6 * width, TILE)))(
        zl, column, stay, f_low, f_high
    )
    block = exchange(to_x, "x")
    other = swap(block)
    held = [pltpu.VMEM((f_in, f_out), F32), dma((N_X,))]
    gs, gn, gf = call(
        own_kernel,
        [SMEM, VMEM],
        (weight, weight, sds((width, n_rows), F32)),
        held,
        out_specs=(ANY, ANY, VMEM),
    )(core, block)
    grad_self, grad_neigh = call(
        other_kernel,
        [SMEM, VMEM, ANY, ANY],
        (weight, weight),
        held,
        out_specs=(ANY, ANY),
        input_output_aliases={2: 0, 3: 1},
    )(core, other, gs, gn)
    return act, grad_self, grad_neigh, bias_sum.reshape(f_out), gf.T


def solution(mesh):
    grid = Mesh(mesh.devices.reshape(SIZES), AXES)
    in_specs = (P(GRAPH, FEAT), P(GRAPH, None), P(), P(), P(), P(GRAPH + FEAT, None))
    out_specs = (P(GRAPH + FEAT, None), P(), P(), P(), P(GRAPH, FEAT))
    return jax.shard_map(local, mesh=grid, in_specs=in_specs, out_specs=out_specs, check_vma=False)
```

time: 137 us -> 134 us (0.978)
  blocking collectives: 59.5 us -> 24.8 us
  starting transfers between devices: 43.8 us -> 74.3 us
  Pallas kernels: 8.4 us -> 10.2 us
    all_to_all x3 -> x2, blocking collectives: 59.5 us -> 24.8 us  [exchange(): return lax.all_to_all(x, axis, split_axis=0, concat_axis=0, tiled=False)]
    all_to_all x2 -> x4, starting transfers between devices: 22 us -> 39.3 us  [exchange(): return lax.all_to_all(x, axis, split_axis=0, concat_axis=0, tiled=False)]
    ppermute x3, starting transfers between devices: 10.1 us -> 17.7 us  [swap(): return lax.ppermute(x, 'c', [(0, 1), (1, 0)])]
    ppermute x2, waiting for transfers between devices: 9.62 us -> 2.06 us  [halos(): high = lax.ppermute(x, AXES, [(i + 1, i) for i in range(n - 1)])]
    ppermute x0 -> x2, starting transfers between devices: none -> 6.18 us  [the longest x1 3.19 us: local(): f_low = lax.ppermute(up, 'zl', [(i, (i + 1) % 3) for i in range(3)])]
    all_to_all x2 -> x4, waiting for transfers between devices: 7.93 us -> 12.3 us  [exchange(): return lax.all_to_all(x, axis, split_axis=0, concat_axis=0, tiled=False)]
    pallas_call x6 -> x9, Pallas kernels: 5.05 us -> 7.06 us  [the longest x1 1.7 us: local(): call(forward_kernel, [SMEM] + [VMEM] * 8, (sds((TILE, f_out)), sds((TILE,...]
    ppermute x0 -> x2, waiting for transfers between devices: none -> 1.95 us  [the longest x1 1.95 us: local(): f_high = lax.ppermute(down, 'zl', [(i, (i + 2) % 3) for i in range(3)])]
  transfers between devices with their start and end apart: 9 -> 13, of which waited for: 6 -> 11; matrix products, arithmetic and copies ran while one was open for 0% -> 0% of each run, Pallas kernels for 2% -> 3%
where the time goes in v3:
time: 134 us; the launch traced here: 133 us
  starting transfers between devices  74.3 us (55%)
  blocking collectives  24.8 us (19%)
  waiting for transfers between devices  20.8 us (16%)
  Pallas kernels  10.2 us (8%)
  local copies, waits for them, and re-layouts  2.48 us (2%)
    all_to_all x4, starting transfers between devices, exchange(): return lax.all_to_all(x, axis, split_axis=0, concat_axis=0, tiled=False)  39.3 us
    all_to_all x2, blocking collectives, exchange(): return lax.all_to_all(x, axis, split_axis=0, concat_axis=0, tiled=False)  24.8 us
    ppermute x3, starting transfers between devices, swap(): return lax.ppermute(x, 'c', [(0, 1), (1, 0)])  17.7 us
    all_to_all x4, waiting for transfers between devices, exchange(): return lax.all_to_all(x, axis, split_axis=0, concat_axis=0, tiled=False)  12.3 us
    ppermute x2, starting transfers between devices, halos(): low = lax.ppermute(x, AXES, [(i, i + 1) for i in range(n - 1)])  6.27 us
    ppermute x2, starting transfers between devices, halos(): high = lax.ppermute(x, AXES, [(i + 1, i) for i in range(n - 1)])  4.83 us
    ppermute x1, starting transfers between devices, local(): f_low = lax.ppermute(up, 'zl', [(i, (i + 1) % 3) for i in range(3)])  3.19 us
    ppermute x1, starting transfers between devices, local(): f_high = lax.ppermute(down, 'zl', [(i, (i + 2) % 3) for i in range(3)])  2.99 us
  transfers between devices with their start and end apart: 13, of which 11 were waited for; matrix products, arithmetic and copies ran while one was open for 0% of the time, Pallas kernels for 3%

profile of v3, /device:TPU:1, one launch (start us, length us, event | category | flops | bytes accessed | tf_op | source)
XLA Modules:
  0.0 133.4 jit_solution(11496526192897427910)
XLA Ops:
  0.6 0.0 copy-start
  0.6 0.9 copy-done
  1.5 0.7 shard_map.101
  2.2 14.1 %all-to-all-start = ((bf16[24,24,128]{2,1,0:T(8,128)(2,1)}), bf16[24,24,128]{2,1,0:T(8,128)(2,1)S(1)}, u32[]{:S(2)}, u32[]{:S(2)}) async-start(bf16[24,24,128]{2,1,0:T(8,128)(2,1)} %shard_map.101), calls=%async_computation | async-start | bytes 294912 | tf_op jit(solution)/shard_map/all_to_all | solution.py:212
  16.3 0.0 copy-start.1
  16.3 0.9 copy-done.1
  17.2 0.0 copy-start.2
  17.2 0.7 copy-done.2
  17.9 1.3 %shard_map.102 = (bf16[128,384]{1,0:T(8,128)(2,1)S(1)}, bf16[576,512]{1,0:T(8,128)(2,1)S(1)}, bf16[576,512]{1,0:T(8,128)(2,1)S(1)}, f32[1,512]{1,0:T(1,128)S(1)}, bf16[128,512]{1,0:T(8,128)(2,1)S(1)}) custom-call(s32[1]{0:T(128)} %bitcast.3.tile, bf16[3072,384]{1,0:T(8,128)(2,1)} %adjacency.1, bf16[576,512]{1,0:T(8,128)(2,1)} %refs_0_.1, ...), custom_call_target="tpu_custom_call" | custom-call | tf_op jit(solution)/shard_map/pallas_call | solution.py:238
  19.3 4.8 %all-to-all-done = bf16[24,24,128]{2,1,0:T(8,128)(2,1)S(1)} async-done(((bf16[24,24,128]{2,1,0:T(8,128)(2,1)}), bf16[24,24,128]{2,1,0:T(8,128)(2,1)S(1)}, u32[]{:S(2)}, u32[]{:S(2)}) %all-to-all-start) | async-done | bytes 147488 | tf_op jit(solution)/shard_map/all_to_all | solution.py:212
  24.0 2.3 %collective-permute-start.1 = (bf16[576,128]{1,0:T(8,128)(2,1)S(1)}, bf16[576,128]{1,0:T(8,128)(2,1)S(1)}, u32[]{:S(2)}, u32[]{:S(2)}) collective-permute-start(bf16[576,128]{1,0:T(8,128)(2,1)S(1)} %bitcast.9), channel_id=1, source_target_pairs={{1,0},{2,1},{3,2},{4,3},{5,4},{6,5},{7,6},{8,7},{9,8},{10,9},{11,1... | collective-permute-start | bytes 442376 | tf_op jit(solution)/shard_map/ppermute | solution.py:218
  26.3 3.3 %collective-permute-start = (bf16[576,128]{1,0:T(8,128)(2,1)S(1)}, bf16[576,128]{1,0:T(8,128)(2,1)S(1)}, u32[]{:S(2)}, u32[]{:S(2)}) collective-permute-start(bf16[576,128]{1,0:T(8,128)(2,1)S(1)} %bitcast.10), channel_id=1, source_target_pairs={{0,1},{1,2},{2,3},{3,4},{4,5},{5,6},{6,7},{7,8},{8,9},{9,10},{10,1... | collective-permute-start | bytes 442376 | tf_op jit(solution)/shard_map/ppermute | solution.py:217
  29.6 0.9 collective-permute-done.1.high
  30.5 1.2 collective-permute-done.low
  31.7 1.7 %shard_map.103 = (bf16[128,512]{1,0:T(8,128)(2,1)}, bf16[128,512]{1,0:T(8,128)(2,1)S(1)}, bf16[576,128]{1,0:T(8,128)(2,1)S(1)}, bf16[1088,128]{1,0:T(8,128)(2,1)...) custom-call(s32[1]{0:T(128)} %bitcast.core, bf16[576,128]{1,0:T(8,128)(2,1)S(1)} %collective-permute-done.low, ...), custom_call_target="tpu_custom_call" | custom-call | tf_op jit(solution)/shard_map/pallas_call | solution.py:254
  33.4 1.9 %collective-permute-start.2 = (bf16[1088,128]{1,0:T(8,128)(2,1)S(1)}, bf16[1088,128]{1,0:T(8,128)(2,1)S(1)}, u32[]{:S(2)}, u32[]{:S(2)}) collective-permute-start(bf16[1088,128]{1,0:T(8,128)(2,1)S(1)} %get-tuple-element.56), channel_id=1, source_target_pairs={{0,1},{1,0},{2,3},{3,2},{4,5},{5,4},{6,7},{7,6},{8,9},{9,8},{10,11... | collective-permute-start | bytes 835592 | tf_op jit(solution)/shard_map/ppermute | solution.py:223
  35.3 1.5 %collective-permute-done.2.recv = bf16[1088,128]{1,0:T(8,128)(2,1)S(1)} collective-permute-done((bf16[1088,128]{1,0:T(8,128)(2,1)S(1)}, bf16[1088,128]{1,0:T(8,128)(2,1)S(1)}, u32[]{:S(2)}, u32[]{:S(2)}) %collective-permute-start.2) | collective-permute-done | bytes 278560 | tf_op jit(solution)/shard_map/ppermute | solution.py:223
  36.8 1.1 shard_map.104
  37.9 6.4 %all-to-all-start.1 = ((bf16[4,584,128]{2,1,0:T(8,128)(2,1)}), bf16[4,584,128]{2,1,0:T(8,128)(2,1)S(1)}, u32[]{:S(2)}, u32[]{:S(2)}) async-start(bf16[4,584,128]{2,1,0:T(8,128)(2,1)} %shard_map.104), calls=%async_computation.1 | async-start | bytes 1196032 | tf_op jit(solution)/shard_map/all_to_all | solution.py:212
  44.4 2.5 %collective-permute-start.4 = (bf16[576,128]{1,0:T(8,128)(2,1)S(1)}, bf16[576,128]{1,0:T(8,128)(2,1)S(1)}, u32[]{:S(2)}, u32[]{:S(2)}) collective-permute-start(bf16[576,128]{1,0:T(8,128)(2,1)S(1)} %get-tuple-element.57.own), channel_id=1, source_target_pairs={{1,0},{2,1},{3,2},{4,3},{5,4},{6,5},{7,6},{8,7},{9,8},{10,9},{11,1... | collective-permute-start | bytes 442376 | tf_op jit(solution)/shard_map/ppermute | solution.py:218
  46.9 3.0 %collective-permute-start.3 = (bf16[576,128]{1,0:T(8,128)(2,1)S(1)}, bf16[576,128]{1,0:T(8,128)(2,1)S(1)}, u32[]{:S(2)}, u32[]{:S(2)}) collective-permute-start(bf16[576,128]{1,0:T(8,128)(2,1)S(1)} %get-tuple-element.57.own), channel_id=1, source_target_pairs={{0,1},{1,2},{2,3},{3,4},{4,5},{5,6},{6,7},{7,8},{8,9},{9,10},{10,1... | collective-permute-start | bytes 442376 | tf_op jit(solution)/shard_map/ppermute | solution.py:217
  49.9 1.2 collective-permute-done.4.high
  51.1 0.9 collective-permute-done.3.low
  52.0 2.1 %all-to-all-done.1.recv = bf16[4,584,128]{2,1,0:T(8,128)(2,1)S(1)} async-done(((bf16[4,584,128]{2,1,0:T(8,128)(2,1)}), bf16[4,584,128]{2,1,0:T(8,128)(2,1)S(1)}, u32[]{:S(2)}, u32[]{:S(2)}) %all-to-all-start.1) | async-done | bytes 598048 | tf_op jit(solution)/shard_map/all_to_all | solution.py:212
  54.1 0.7 shard_map.105
  54.8 15.3 %all-to-all-start.2 = ((bf16[8,80,128]{2,1,0:T(8,128)(2,1)}), bf16[8,80,128]{2,1,0:T(8,128)(2,1)S(1)}, u32[]{:S(2)}, u32[]{:S(2)}) async-start(bf16[8,80,128]{2,1,0:T(8,128)(2,1)} %shard_map.105), calls=%async_computation.2 | async-start | bytes 327680 | tf_op jit(solution)/shard_map/all_to_all | solution.py:212
  70.1 0.3 shard_map.106
  70.4 6.4 %collective-permute-start.5 = (bf16[3,4,24,128]{3,2,1,0:T(8,128)(2,1)S(1)}, bf16[3,4,24,128]{3,2,1,0:T(8,128)(2,1)S(1)}, u32[]{:S(2)}, u32[]{:S(2)}) collective-permute-start(bf16[3,4,24,128]{3,2,1,0:T(8,128)(2,1)S(1)} %get-tuple-element.62), channel_id=1, source_target_pairs={{0,1},{1,0},{2,3},{3,2},{4,5},{5,4},{6,7},{7,6},{8,9},{9,8},{10,11... | collective-permute-start | bytes 221192 | tf_op jit(solution)/shard_map/ppermute | solution.py:223
  76.8 0.9 collective-permute-done.5.other
  77.7 0.7 all-to-all-done.2.recv
  78.4 0.7 shard_map.107
  79.1 3.5 %all-to-all-start.3 = ((bf16[12,80,128]{2,1,0:T(8,128)(2,1)}), bf16[12,80,128]{2,1,0:T(8,128)(2,1)S(1)}, u32[]{:S(2)}, u32[]{:S(2)}) async-start(bf16[12,80,128]{2,1,0:T(8,128)(2,1)} %shard_map.107), calls=%async_computation.3 | async-start | bytes 491520 | tf_op jit(solution)/shard_map/all_to_all | solution.py:212
  82.7 3.2 %collective-permute-start.6 = (bf16[4,48,128]{2,1,0:T(8,128)(2,1)S(1)}, bf16[4,48,128]{2,1,0:T(8,128)(2,1)S(1)}, u32[]{:S(2)}, u32[]{:S(2)}) collective-permute-start(bf16[4,48,128]{2,1,0:T(8,128)(2,1)S(1)} %get-tuple-element.66), channel_id=1, source_target_pairs={{0,2},{2,4},{4,0},{1,3},{3,5},{5,1},{6,8},{8,10},{10,6},{7,9},{9,1... | collective-permute-start | bytes 147464 | tf_op jit(solution)/shard_map/ppermute | solution.py:275
  85.9 3.0 %collective-permute-start.7 = (bf16[4,48,128]{2,1,0:T(8,128)(2,1)S(1)}, bf16[4,48,128]{2,1,0:T(8,128)(2,1)S(1)}, u32[]{:S(2)}, u32[]{:S(2)}) collective-permute-start(bf16[4,48,128]{2,1,0:T(8,128)(2,1)S(1)} %get-tuple-element.67), channel_id=1, source_target_pairs={{0,4},{2,0},{4,2},{1,5},{3,1},{5,3},{6,10},{8,6},{10,8},{7,11},{9,... | collective-permute-start | bytes 147464 | tf_op jit(solution)/shard_map/ppermute | solution.py:276
  88.9 0.0 collective-permute-done.6.low
  88.9 1.9 %collective-permute-done.7.high = bf16[4,48,128]{2,1,0:T(8,128)(2,1)S(1)} collective-permute-done((bf16[4,48,128]{2,1,0:T(8,128)(2,1)S(1)}, bf16[4,48,128]{2,1,0:T(8,128)(2,1)S(1)}, u32[]{:S(2)}, u32[]{:S(2)}) %collective-permute-start.7) | collective-permute-done | bytes 49184 | tf_op jit(solution)/shard_map/ppermute | solution.py:276
  90.9 4.8 %all-to-all-done.3.refs_0_ = bf16[12,80,128]{2,1,0:T(8,128)(2,1)S(1)} async-done(((bf16[12,80,128]{2,1,0:T(8,128)(2,1)}), bf16[12,80,128]{2,1,0:T(8,128)(2,1)S(1)}, u32[]{:S(2)}, u32[]{:S(2)}) %all-to-all-start.3) | async-done | bytes 245792 | tf_op jit(solution)/shard_map/all_to_all | solution.py:212
  95.7 0.6 shard_map.109
  96.3 14.3 %all_to_all.30 = bf16[8,72,128]{2,1,0:T(8,128)(2,1)S(1)} all-to-all(bf16[8,72,128]{2,1,0:T(8,128)(2,1)S(1)} %get-tuple-element.69), channel_id=1, replica_groups=mesh['y'=8,'zh'=4,'x'=4,'zl'=3,'c'=2] {'y'}, dimensions={0} | all-to-all | bytes 294912 | tf_op jit(solution)/shard_map/all_to_all | solution.py:212
  110.6 0.1 shard_map.110
  110.7 10.5 %all_to_all.31.block = bf16[4,720,128]{2,1,0:T(8,128)(2,1)S(1)} all-to-all(bf16[4,720,128]{2,1,0:T(8,128)(2,1)S(1)} %shard_map.110), channel_id=1, replica_groups=mesh['y'=8,'zh'=4,'x'=4,'zl'=3,'c'=2] {'x'}, dimensions={0} | all-to-all | bytes 1474560 | tf_op jit(solution)/shard_map/all_to_all | solution.py:212
  121.1 9.4 %collective-permute-start.8 = (bf16[4,720,128]{2,1,0:T(8,128)(2,1)S(1)}, bf16[4,720,128]{2,1,0:T(8,128)(2,1)S(1)}, u32[]{:S(2)}, u32[]{:S(2)}) collective-permute-start(bf16[4,720,128]{2,1,0:T(8,128)(2,1)S(1)} %all_to_all.31.block), channel_id=1, source_target_pairs={{0,1},{1,0},{2,3},{3,2},{4,5},{5,4},{6,7},{7,6},{8,9},{9,8},{10,11... | collective-permute-start | bytes 2211848 | tf_op jit(solution)/shard_map/ppermute | solution.py:223
  130.5 1.8 %shard_map.111 = (f32[576,512]{1,0:T(8,128)}, f32[576,512]{1,0:T(8,128)}, f32[24,3072]{1,0:T(8,128)}) custom-call(s32[1]{0:T(128)} %bitcast.core, bf16[4,720,128]{2,1,0:T(8,128)(2,1)S(1)} %all_to_all.31.block), custom_call_target="tpu_custom_call" | custom-call | tf_op jit(solution)/shard_map/pallas_call | solution.py:290
  132.3 0.0 collective-permute-done.8.block
  132.4 1.1 shard_map.112
  (1 shorter events, 0.0 us)
Async XLA Ops:
  0.6 0.9 copy-start
  2.2 21.8 %all-to-all-start = ((bf16[24,24,128]{2,1,0:T(8,128)(2,1)}), bf16[24,24,128]{2,1,0:T(8,128)(2,1)S(1)}, u32[]{:S(2)}, u32[]{:S(2)}) async-start(bf16[24,24,128]{2,1,0:T(8,128)(2,1)} %shard_map.101), calls=%async_computation | async-start | bytes 294912 | tf_op jit(solution)/shard_map/all_to_all | solution.py:212
  16.3 0.9 copy-start.1
  17.2 0.7 copy-start.2
  24.0 6.5 %collective-permute-start.1 = (bf16[576,128]{1,0:T(8,128)(2,1)S(1)}, bf16[576,128]{1,0:T(8,128)(2,1)S(1)}, u32[]{:S(2)}, u32[]{:S(2)}) collective-permute-start(bf16[576,128]{1,0:T(8,128)(2,1)S(1)} %bitcast.9), channel_id=1, source_target_pairs={{1,0},{2,1},{3,2},{4,3},{5,4},{6,5},{7,6},{8,7},{9,8},{10,9},{11,1... | collective-permute-start | bytes 442376 | tf_op jit(solution)/shard_map/ppermute | solution.py:218
  26.3 5.3 %collective-permute-start = (bf16[576,128]{1,0:T(8,128)(2,1)S(1)}, bf16[576,128]{1,0:T(8,128)(2,1)S(1)}, u32[]{:S(2)}, u32[]{:S(2)}) collective-permute-start(bf16[576,128]{1,0:T(8,128)(2,1)S(1)} %bitcast.10), channel_id=1, source_target_pairs={{0,1},{1,2},{2,3},{3,4},{4,5},{5,6},{6,7},{7,8},{8,9},{9,10},{10,1... | collective-permute-start | bytes 442376 | tf_op jit(solution)/shard_map/ppermute | solution.py:217
  33.4 3.4 %collective-permute-start.2 = (bf16[1088,128]{1,0:T(8,128)(2,1)S(1)}, bf16[1088,128]{1,0:T(8,128)(2,1)S(1)}, u32[]{:S(2)}, u32[]{:S(2)}) collective-permute-start(bf16[1088,128]{1,0:T(8,128)(2,1)S(1)} %get-tuple-element.56), channel_id=1, source_target_pairs={{0,1},{1,0},{2,3},{3,2},{4,5},{5,4},{6,7},{7,6},{8,9},{9,8},{10,11... | collective-permute-start | bytes 835592 | tf_op jit(solution)/shard_map/ppermute | solution.py:223
  37.9 16.1 %all-to-all-start.1 = ((bf16[4,584,128]{2,1,0:T(8,128)(2,1)}), bf16[4,584,128]{2,1,0:T(8,128)(2,1)S(1)}, u32[]{:S(2)}, u32[]{:S(2)}) async-start(bf16[4,584,128]{2,1,0:T(8,128)(2,1)} %shard_map.104), calls=%async_computation.1 | async-start | bytes 1196032 | tf_op jit(solution)/shard_map/all_to_all | solution.py:212
  44.4 6.7 %collective-permute-start.4 = (bf16[576,128]{1,0:T(8,128)(2,1)S(1)}, bf16[576,128]{1,0:T(8,128)(2,1)S(1)}, u32[]{:S(2)}, u32[]{:S(2)}) collective-permute-start(bf16[576,128]{1,0:T(8,128)(2,1)S(1)} %get-tuple-element.57.own), channel_id=1, source_target_pairs={{1,0},{2,1},{3,2},{4,3},{5,4},{6,5},{7,6},{8,7},{9,8},{10,9},{11,1... | collective-permute-start | bytes 442376 | tf_op jit(solution)/shard_map/ppermute | solution.py:218
  46.9 5.1 %collective-permute-start.3 = (bf16[576,128]{1,0:T(8,128)(2,1)S(1)}, bf16[576,128]{1,0:T(8,128)(2,1)S(1)}, u32[]{:S(2)}, u32[]{:S(2)}) collective-permute-start(bf16[576,128]{1,0:T(8,128)(2,1)S(1)} %get-tuple-element.57.own), channel_id=1, source_target_pairs={{0,1},{1,2},{2,3},{3,4},{4,5},{5,6},{6,7},{7,8},{8,9},{9,10},{10,1... | collective-permute-start | bytes 442376 | tf_op jit(solution)/shard_map/ppermute | solution.py:217
  54.8 23.6 %all-to-all-start.2 = ((bf16[8,80,128]{2,1,0:T(8,128)(2,1)}), bf16[8,80,128]{2,1,0:T(8,128)(2,1)S(1)}, u32[]{:S(2)}, u32[]{:S(2)}) async-start(bf16[8,80,128]{2,1,0:T(8,128)(2,1)} %shard_map.105), calls=%async_computation.2 | async-start | bytes 327680 | tf_op jit(solution)/shard_map/all_to_all | solution.py:212
  70.4 7.3 %collective-permute-start.5 = (bf16[3,4,24,128]{3,2,1,0:T(8,128)(2,1)S(1)}, bf16[3,4,24,128]{3,2,1,0:T(8,128)(2,1)S(1)}, u32[]{:S(2)}, u32[]{:S(2)}) collective-permute-start(bf16[3,4,24,128]{3,2,1,0:T(8,128)(2,1)S(1)} %get-tuple-element.62), channel_id=1, source_target_pairs={{0,1},{1,0},{2,3},{3,2},{4,5},{5,4},{6,7},{7,6},{8,9},{9,8},{10,11... | collective-permute-start | bytes 221192 | tf_op jit(solution)/shard_map/ppermute | solution.py:223
  79.1 16.6 %all-to-all-start.3 = ((bf16[12,80,128]{2,1,0:T(8,128)(2,1)}), bf16[12,80,128]{2,1,0:T(8,128)(2,1)S(1)}, u32[]{:S(2)}, u32[]{:S(2)}) async-start(bf16[12,80,128]{2,1,0:T(8,128)(2,1)} %shard_map.107), calls=%async_computation.3 | async-start | bytes 491520 | tf_op jit(solution)/shard_map/all_to_all | solution.py:212
  82.7 6.2 %collective-permute-start.6 = (bf16[4,48,128]{2,1,0:T(8,128)(2,1)S(1)}, bf16[4,48,128]{2,1,0:T(8,128)(2,1)S(1)}, u32[]{:S(2)}, u32[]{:S(2)}) collective-permute-start(bf16[4,48,128]{2,1,0:T(8,128)(2,1)S(1)} %get-tuple-element.66), channel_id=1, source_target_pairs={{0,2},{2,4},{4,0},{1,3},{3,5},{5,1},{6,8},{8,10},{10,6},{7,9},{9,1... | collective-permute-start | bytes 147464 | tf_op jit(solution)/shard_map/ppermute | solution.py:275
  85.9 5.0 %collective-permute-start.7 = (bf16[4,48,128]{2,1,0:T(8,128)(2,1)S(1)}, bf16[4,48,128]{2,1,0:T(8,128)(2,1)S(1)}, u32[]{:S(2)}, u32[]{:S(2)}) collective-permute-start(bf16[4,48,128]{2,1,0:T(8,128)(2,1)S(1)} %get-tuple-element.67), channel_id=1, source_target_pairs={{0,4},{2,0},{4,2},{1,5},{3,1},{5,3},{6,10},{8,6},{10,8},{7,11},{9,... | collective-permute-start | bytes 147464 | tf_op jit(solution)/shard_map/ppermute | solution.py:276
  121.1 11.2 %collective-permute-start.8 = (bf16[4,720,128]{2,1,0:T(8,128)(2,1)S(1)}, bf16[4,720,128]{2,1,0:T(8,128)(2,1)S(1)}, u32[]{:S(2)}, u32[]{:S(2)}) collective-permute-start(bf16[4,720,128]{2,1,0:T(8,128)(2,1)S(1)} %all_to_all.31.block), channel_id=1, source_target_pairs={{0,1},{1,0},{2,3},{3,2},{4,5},{5,4},{6,7},{7,6},{8,9},{9,8},{10,11... | collective-permute-start | bytes 2211848 | tf_op jit(solution)/shard_map/ppermute | solution.py:223

commit v4 on v3

--- a/solution.py
+++ b/solution.py
@@ -36,7 +36,7 @@
         in_specs=list(specs),
         out_specs=kw.pop("out_specs", jax.tree.map(lambda _: VMEM, outs)),
         scratch_shapes=list(scratch),
-        compiler_params=kw.pop("params", PARAMS),
+        compiler_params=PARAMS,
         **kw,
     )
 
@@ -53,31 +53,35 @@
     return dot(jnp.concatenate(parts, axis=1), adj, 1, 1)
 
 
-def prepare_kernel(feats, out):
-    for t in range(N_FEAT):
-        out[t] = feats[:, lanes(t)]
-
-
-def load_kernel(tile, adjacency, *refs):
+def prepare_kernel(tile, feats, adjacency, *refs):
+    held, sems = refs[-2:]
     rows = pl.ds(pl.multiple_of(tile[0] * TILE, TILE), TILE)
-    sems = refs[-1]
-    sources = (adjacency.at[rows],) + refs[:4]
-    copies = [
-        pltpu.make_async_copy(s, d, sems.at[i])
-        for i, (s, d) in enumerate(zip(sources, refs[4:-1], strict=True))
-    ]
+    pairs = [(feats, held), (adjacency.at[rows], refs[5])]
+    pairs += [(refs[i], refs[i + 6]) for i in range(4)]
+    out = refs[4]
+    copies = [pltpu.make_async_copy(s, d, sems.at[i]) for i, (s, d) in enumerate(pairs)]
     for c in copies:
         c.start()
-    for c in copies:
+    copies[0].wait()
+    for t in range(N_FEAT):
+        out[t] = held[:, lanes(t)]
+    for c in copies[1:]:
         c.wait()
 
 
+def sides(core, far, near):
+    first = core[0] == 0
+    f, n = far[...], near[...]
+    return jnp.where(first, f, n), jnp.where(first, n, f)
+
+
 def forward_kernel(
-    core, low, own, high, adj, ws, wn, bias, cot, act, grad, keep, send, back, scaled
+    core, near, far, own, adj, ws, wn, bias, cot, act, grad, keep, send, back, scaled
 ):
     a = adj[...]
     degree = (1.0 + dot(jnp.ones((8, 3 * TILE), BF16), a, 1, 1))[:1]
-    m = (band((low[...], own[...], high[...]), a) / degree).astype(BF16)
+    low, high = sides(core, far, near)
+    m = (band((low, own[...], high), a) / degree).astype(BF16)
     x = own[...]
     pre = dot(x, ws[...], 0, 0) + dot(m, wn[...], 0, 0) + bias[...]
     s = 1.0 / (1.0 + jnp.exp(-pre))
@@ -134,25 +138,16 @@
         out[d] = rounded
 
 
-def feat_kernel(core, low, own, high, adj, back, keep, send):
-    total = back[...].astype(F32) + band((low[...], own[...], high[...]), adj[...])
-    first = core[0] == 0
-    width = total.shape[0] // N_FEAT
-    for d in range(N_LINE):
-        even = total[2 * d * width : (2 * d + 1) * width]
-        odd = total[(2 * d + 1) * width : (2 * d + 2) * width]
-        keep[d % 3, d // 3] = jnp.where(first, even, odd).astype(BF16)
-        send[d % 3, d // 3] = jnp.where(first, odd, even).astype(BF16)
-
-
-def pair_kernel(core, zl, keep, other, stay, up, down):
-    first = core[0] == 0
+def feat_kernel(core, zl, near, far, own, adj, back, stay, up, down, parts):
+    low, high = sides(core, far, near)
+    total = back[...].astype(F32) + band((low, own[...], high), adj[...])
+    width = parts.shape[1]
+    for i in range(N_FEAT):
+        parts[i] = total[i * width : (i + 1) * width]
     for shift, out in enumerate((stay, up, down)):
-        at = lax.rem(zl[0] + shift, 3)
+        at = 2 * lax.rem(zl[0] + shift, 3)
         for d in range(N_X):
-            k = keep[at, d].astype(F32)
-            o = other[at, d].astype(F32)
-            pair = jnp.concatenate([jnp.where(first, k, o), jnp.where(first, o, k)], axis=0)
+            pair = jnp.concatenate([parts[6 * d + at], parts[6 * d + at + 1]], axis=0)
             out[d] = pair.astype(BF16)
 
 
@@ -192,20 +187,38 @@
         pltpu.make_async_copy(held.at[:, lanes(d)], out.at[:, lanes(d)], sems.at[d]).wait()
 
 
-def own_kernel(core, block, gs, gn, gf, held, sems):
+def columns(core, source, block, gf, part, sems):
+    width = part.shape[1]
+    f_in = block.shape[1] - 6 * width
+    first = core == 0
+    copies = []
+    for d in range(N_X):
+        rows = block[d, f_in:].astype(F32)
+        for p in range(3):
+            k = 3 * d + p
+            even = rows[2 * p * width : (2 * p + 1) * width]
+            odd = rows[(2 * p + 1) * width : (2 * p + 2) * width]
+            at = pl.ds(pl.multiple_of((2 * k + source) * TILE, TILE), TILE)
+            part[k] = jnp.where(first, even, odd)
+            copies.append(pltpu.make_async_copy(part.at[k], gf.at[:, at], sems.at[k]))
+            copies[-1].start()
+    return copies
+
+
+def own_kernel(core, block, gs, gn, gf, held, sems, part, part_sems):
     halves(block, held, send_half(held, sems, core[0] == 0, gs, gn))
-    f_in = held.shape[0]
-    width = gf.shape[0]
-    for d in range(N_X):
-        part = block[d, f_in:].astype(F32)
-        for k in range(6):
-            gf[:, lanes(6 * d + k)] = part[k * width : (k + 1) * width]
+    copies = columns(core[0], core[0], block, gf, part, part_sems)
     finish(held, sems, gs)
-
-
-def other_kernel(core, block, gs_in, gn_in, gs, gn, held, sems):
+    for c in copies:
+        c.wait()
+
+
+def other_kernel(core, block, gs_in, gn_in, gf_in, gs, gn, gf, held, sems, part, part_sems):
     halves(block, held, send_half(held, sems, core[0] == 0, gn, gs))
+    copies = columns(core[0], 1 - core[0], block, gf, part, part_sems)
     finish(held, sems, gs)
+    for c in copies:
+        c.wait()
 
 
 def exchange(x, axis):
@@ -213,10 +226,10 @@
 
 
 def halos(x):
-    n = 768
-    low = lax.ppermute(x, AXES, [(i, i + 1) for i in range(n - 1)])
-    high = lax.ppermute(x, AXES, [(i + 1, i) for i in range(n - 1)])
-    return low, high
+    pairs = [(2 * k + 1, 2 * k + 2) for k in range(383)]
+    pairs += [(b, a) for a, b in pairs]
+    near = swap(x)
+    return lax.ppermute(x, AXES, pairs), near
 
 
 def swap(x):
@@ -233,45 +246,49 @@
     wide = sds((f_in, TILE))
     weight = sds((f_in, f_out), F32)
 
-    pieces = call(prepare_kernel, [VMEM], sds((N_FEAT, width, TILE)))(features.T)
-    own = exchange(pieces, FEAT).reshape(f_in, TILE)
-    held = call(
-        load_kernel,
-        [SMEM] + [ANY] * 5,
+    pieces, *held = call(
+        prepare_kernel,
+        [SMEM] + [ANY] * 6,
         (
+            sds((N_FEAT, width, TILE)),
             sds((TILE, 3 * TILE)),
             sds((f_in, f_out)),
             sds((f_in, f_out)),
             sds((1, f_out), F32),
             sds((TILE, f_out)),
         ),
-        [dma((5,))],
-        params=pltpu.CompilerParams(vmem_limit_bytes=52 * 1024 * 1024),
-    )(tile, adjacency, w_self, w_neigh, bias_out.reshape(1, f_out), cotangent)
-    own, held = lax.optimization_barrier((own, held))
+        [pltpu.VMEM((width, n_rows), BF16), dma((6,))],
+    )(
+        tile,
+        *(
+            pltpu.with_memory_space_constraint(x, pltpu.HBM)
+            for x in (features.T, adjacency, w_self, w_neigh, bias_out.reshape(1, f_out), cotangent)
+        ),
+    )
     adj = held[0]
-    low, high = halos(own)
+    own = exchange(pieces, FEAT).reshape(f_in, TILE)
+    far, near = halos(own)
     act, grad, keep, send, back, scaled = call(
         forward_kernel,
         [SMEM] + [VMEM] * 8,
         (sds((TILE, f_out)), sds((TILE, f_out)), wide, sds((f_in + f_out, TILE)), wide, wide),
-    )(core, low, own, high, *held)
+    )(core, near, far, own, *held)
     recv = swap(send)
-    s_low, s_high = halos(scaled)
+    s_far, s_near = halos(scaled)
     partial = call(partial_kernel, [VMEM] * 3, sds((N_X, f_in + TAIL, TILE)))(keep, grad, recv)
     from_x = exchange(partial, "x")
-    from_x, s_low, s_high = lax.optimization_barrier((from_x, s_low, s_high))
-    from_y = exchange(call(x_kernel, [VMEM], sds((N_Y, ROWS + TAIL, TILE)))(from_x), "y")
-    slab = sds((3, N_X, width, TILE))
-    f_keep, f_send = call(feat_kernel, [SMEM] + [VMEM] * 5, (slab, slab))(
-        core, s_low, scaled, s_high, adj, back
-    )
-    f_recv = swap(f_send)
-    from_y, f_recv = lax.optimization_barrier((from_y, f_recv))
-    from_line = exchange(call(y_kernel, [VMEM], sds((N_LINE, ROWS + TAIL, TILE)))(from_y), LINE)
+    from_x, s_far, s_near = lax.optimization_barrier((from_x, s_far, s_near))
     zl = lax.axis_index("zl").astype(jnp.int32).reshape(1)
     pair = sds((N_X, 2 * width, TILE))
-    stay, up, down = call(pair_kernel, [SMEM] * 2 + [VMEM] * 2, (pair,) * 3)(core, zl, f_keep, f_recv)
+    stay, up, down = call(
+        feat_kernel,
+        [SMEM] * 2 + [VMEM] * 5,
+        (pair,) * 3,
+        [pltpu.VMEM((N_FEAT, width, TILE), F32)],
+    )(core, zl, s_near, s_far, scaled, adj, back)
+    from_x, stay, up, down = lax.optimization_barrier((from_x, stay, up, down))
+    from_y = exchange(call(x_kernel, [VMEM], sds((N_Y, ROWS + TAIL, TILE)))(from_x), "y")
+    from_line = exchange(call(y_kernel, [VMEM], sds((N_LINE, ROWS + TAIL, TILE)))(from_y), LINE)
     f_low = lax.ppermute(up, "zl", [(i, (i + 1) % 3) for i in range(3)])
     f_high = lax.ppermute(down, "zl", [(i, (i + 2) % 3) for i in range(3)])
     from_line, f_low, f_high = lax.optimization_barrier((from_line, f_low, f_high))
@@ -286,22 +303,24 @@
     )
     block = exchange(to_x, "x")
     other = swap(block)
-    held = [pltpu.VMEM((f_in, f_out), F32), dma((N_X,))]
-    gs, gn, gf = call(
-        own_kernel,
-        [SMEM, VMEM],
-        (weight, weight, sds((width, n_rows), F32)),
-        held,
-        out_specs=(ANY, ANY, VMEM),
+    whole = sds((width, n_rows), F32)
+    room = [
+        pltpu.VMEM((f_in, f_out), F32),
+        dma((N_X,)),
+        pltpu.VMEM((N_LINE, width, TILE), F32),
+        dma((N_LINE,)),
+    ]
+    partly = call(
+        own_kernel, [SMEM, VMEM], (weight, weight, whole), room, out_specs=(ANY,) * 3
     )(core, block)
-    grad_self, grad_neigh = call(
+    grad_self, grad_neigh, gf = call(
         other_kernel,
-        [SMEM, VMEM, ANY, ANY],
-        (weight, weight),
-        held,
-        out_specs=(ANY, ANY),
-        input_output_aliases={2: 0, 3: 1},
-    )(core, other, gs, gn)
+        [SMEM, VMEM] + [ANY] * 3,
+        (weight, weight, whole),
+        room,
+        out_specs=(ANY,) * 3,
+        input_output_aliases={2: 0, 3: 1, 4: 2},
+    )(core, other, *partly)
     return act, grad_self, grad_neigh, bias_sum.reshape(f_out), gf.T
 
 

time: 134 us -> 129 us (0.963)
  blocking collectives: 24.8 us -> 60.4 us
  starting transfers between devices: 74.3 us -> 42.8 us
  waiting for transfers between devices: 20.8 us -> 15.8 us
  local copies, waits for them, and re-layouts: 2.48 us -> 0 us
  Pallas kernels: 10.2 us -> 8.55 us
    all_to_all x2 -> x4, blocking collectives: 24.8 us -> 60.4 us  [exchange(): return lax.all_to_all(x, axis, split_axis=0, concat_axis=0, tiled=False)]
    all_to_all x4 -> x2, starting transfers between devices: 39.3 us -> 14.3 us  [exchange(): return lax.all_to_all(x, axis, split_axis=0, concat_axis=0, tiled=False)]
    all_to_all x4 -> x2, waiting for transfers between devices: 12.3 us -> 2.23 us  [exchange(): return lax.all_to_all(x, axis, split_axis=0, concat_axis=0, tiled=False)]
    ppermute x4 -> x2, starting transfers between devices: 11.1 us -> 5.16 us  [halos(): return (lax.ppermute(x, AXES, pairs), near)]
    ppermute x4 -> x2, waiting for transfers between devices: 4.16 us -> 7.1 us  [halos(): return (lax.ppermute(x, AXES, pairs), near)]
    unnamed x6 -> x0, local copies, waits for them, and re-layouts: 2.48 us -> none
    ppermute x1, waiting for transfers between devices: 1.95 us -> 3.74 us  [local(): f_high = lax.ppermute(down, 'zl', [(i, (i + 2) % 3) for i in range(3)])]
    pallas_call x6 -> x4, Pallas kernels: 5.23 us -> 4.23 us  [the longest x1 1.46 us: local(): call(prepare_kernel, [SMEM] + [ANY] * 6, (sds((N_FEAT, width, TILE)), sds...]
  transfers between devices with their start and end apart: 13 -> 10, of which waited for: 11 -> 8; matrix products, arithmetic and copies ran while one was open for 0% -> 0% of each run, Pallas kernels for 3% -> 1%
where the time goes in v4:
time: 129 us; the launch traced here: 128 us
  blocking collectives  60.4 us (47%)
  starting transfers between devices  42.8 us (33%)
  waiting for transfers between devices  15.8 us (12%)
  Pallas kernels  8.55 us (7%)
    all_to_all x4, blocking collectives, exchange(): return lax.all_to_all(x, axis, split_axis=0, concat_axis=0, tiled=False)  60.4 us
    ppermute x4, starting transfers between devices, swap(): return lax.ppermute(x, 'c', [(0, 1), (1, 0)])  17.1 us
    all_to_all x2, starting transfers between devices, exchange(): return lax.all_to_all(x, axis, split_axis=0, concat_axis=0, tiled=False)  14.3 us
    ppermute x2, waiting for transfers between devices, halos(): return (lax.ppermute(x, AXES, pairs), near)  7.1 us
    ppermute x2, starting transfers between devices, halos(): return (lax.ppermute(x, AXES, pairs), near)  5.16 us
    ppermute x1, waiting for transfers between devices, local(): f_high = lax.ppermute(down, 'zl', [(i, (i + 2) % 3) for i in range(3)])  3.74 us
    ppermute x1, starting transfers between devices, local(): f_low = lax.ppermute(up, 'zl', [(i, (i + 1) % 3) for i in range(3)])  3.32 us
    ppermute x1, starting transfers between devices, local(): f_high = lax.ppermute(down, 'zl', [(i, (i + 2) % 3) for i in range(3)])  2.86 us
  transfers between devices with their start and end apart: 10, of which 8 were waited for; matrix products, arithmetic and copies ran while one was open for 0% of the time, Pallas kernels for 1%

profile of v4, /device:TPU:1, one launch (start us, length us, event | category | flops | bytes accessed | tf_op | source)
XLA Modules:
  0.0 128.2 jit_solution(15209433942991048794)
XLA Ops:
  0.7 1.5 %shard_map.101 = (bf16[24,24,128]{2,1,0:T(8,128)(2,1)S(1)}, bf16[128,384]{1,0:T(8,128)(2,1)S(1)}, bf16[576,512]{1,0:T(8,128)(2,1)S(1)}, bf16[576,512]{1,0:T(8,12...) custom-call(s32[1]{0:T(128)} %bitcast.1.tile, bf16[24,3072]{1,0:T(8,128)(2,1)} %bitcast.14, ...), custom_call_target="tpu_custom_call" | custom-call | tf_op jit(solution)/shard_map/pallas_call | solution.py:249
  2.1 20.9 %all_to_all.30 = bf16[24,24,128]{2,1,0:T(8,128)(2,1)S(1)} all-to-all(bf16[24,24,128]{2,1,0:T(8,128)(2,1)S(1)} %get-tuple-element.38), channel_id=1, replica_groups=mesh['y'=8,'zh'=4,'x'=4,'zl'=3,'c'=2] {'x','zl','c'}, dimensions={0} | all-to-all | bytes 294912 | tf_op jit(solution)/shard_map/all_to_all | solution.py:225
  23.0 3.0 %collective-permute-start.1 = (bf16[576,128]{1,0:T(8,128)(2,1)S(1)}, bf16[576,128]{1,0:T(8,128)(2,1)S(1)}, u32[]{:S(2)}, u32[]{:S(2)}) collective-permute-start(bf16[576,128]{1,0:T(8,128)(2,1)S(1)} %bitcast.9), channel_id=1, source_target_pairs={{1,2},{3,4},{5,6},{7,8},{9,10},{11,12},{13,14},{15,16},{17,18},{19... | collective-permute-start | bytes 442376 | tf_op jit(solution)/shard_map/ppermute | solution.py:232
  26.0 1.9 %collective-permute-start = (bf16[576,128]{1,0:T(8,128)(2,1)S(1)}, bf16[576,128]{1,0:T(8,128)(2,1)S(1)}, u32[]{:S(2)}, u32[]{:S(2)}) collective-permute-start(bf16[576,128]{1,0:T(8,128)(2,1)S(1)} %bitcast.10), channel_id=1, source_target_pairs={{0,1},{1,0},{2,3},{3,2},{4,5},{5,4},{6,7},{7,6},{8,9},{9,8},{10,11... | collective-permute-start | bytes 442376 | tf_op jit(solution)/shard_map/ppermute | solution.py:236
  27.9 2.5 %collective-permute-done.1.far = bf16[576,128]{1,0:T(8,128)(2,1)S(1)} collective-permute-done((bf16[576,128]{1,0:T(8,128)(2,1)S(1)}, bf16[576,128]{1,0:T(8,128)(2,1)S(1)}, u32[]{:S(2)}, u32[]{:S(2)}) %collective-permute-start.1) | collective-permute-done | bytes 147488 | tf_op jit(solution)/shard_map/ppermute | solution.py:232
  30.5 0.0 collective-permute-done.near
  30.5 1.7 %shard_map.102 = (bf16[128,512]{1,0:T(8,128)(2,1)}, bf16[128,512]{1,0:T(8,128)(2,1)S(1)}, bf16[576,128]{1,0:T(8,128)(2,1)S(1)}, bf16[1088,128]{1,0:T(8,128)(2,1)...) custom-call(s32[1]{0:T(128)} %bitcast.core, bf16[576,128]{1,0:T(8,128)(2,1)S(1)} %collective-permute-done.near, ...), custom_call_target="tpu_custom_call" | custom-call | tf_op jit(solution)/shard_map/pallas_call | solution.py:271
  32.2 1.9 %collective-permute-start.2 = (bf16[1088,128]{1,0:T(8,128)(2,1)S(1)}, bf16[1088,128]{1,0:T(8,128)(2,1)S(1)}, u32[]{:S(2)}, u32[]{:S(2)}) collective-permute-start(bf16[1088,128]{1,0:T(8,128)(2,1)S(1)} %get-tuple-element.47), channel_id=1, source_target_pairs={{0,1},{1,0},{2,3},{3,2},{4,5},{5,4},{6,7},{7,6},{8,9},{9,8},{10,11... | collective-permute-start | bytes 835592 | tf_op jit(solution)/shard_map/ppermute | solution.py:236
  34.1 1.5 %collective-permute-done.2.recv = bf16[1088,128]{1,0:T(8,128)(2,1)S(1)} collective-permute-done((bf16[1088,128]{1,0:T(8,128)(2,1)S(1)}, bf16[1088,128]{1,0:T(8,128)(2,1)S(1)}, u32[]{:S(2)}, u32[]{:S(2)}) %collective-permute-start.2) | collective-permute-done | bytes 278560 | tf_op jit(solution)/shard_map/ppermute | solution.py:236
  35.6 1.1 shard_map.103
  36.7 3.7 %all-to-all-start.1 = ((bf16[4,584,128]{2,1,0:T(8,128)(2,1)}), bf16[4,584,128]{2,1,0:T(8,128)(2,1)S(1)}, u32[]{:S(2)}, u32[]{:S(2)}) async-start(bf16[4,584,128]{2,1,0:T(8,128)(2,1)} %shard_map.103), calls=%async_computation.1 | async-start | bytes 1196032 | tf_op jit(solution)/shard_map/all_to_all | solution.py:225
  40.4 2.5 %collective-permute-start.4 = (bf16[576,128]{1,0:T(8,128)(2,1)S(1)}, bf16[576,128]{1,0:T(8,128)(2,1)S(1)}, u32[]{:S(2)}, u32[]{:S(2)}) collective-permute-start(bf16[576,128]{1,0:T(8,128)(2,1)S(1)} %get-tuple-element.48.own), channel_id=1, source_target_pairs={{0,1},{1,0},{2,3},{3,2},{4,5},{5,4},{6,7},{7,6},{8,9},{9,8},{10,11... | collective-permute-start | bytes 442376 | tf_op jit(solution)/shard_map/ppermute | solution.py:236
  43.0 2.2 %collective-permute-start.3 = (bf16[576,128]{1,0:T(8,128)(2,1)S(1)}, bf16[576,128]{1,0:T(8,128)(2,1)S(1)}, u32[]{:S(2)}, u32[]{:S(2)}) collective-permute-start(bf16[576,128]{1,0:T(8,128)(2,1)S(1)} %get-tuple-element.48.own), channel_id=1, source_target_pairs={{1,2},{3,4},{5,6},{7,8},{9,10},{11,12},{13,14},{15,16},{17,18},{19... | collective-permute-start | bytes 442376 | tf_op jit(solution)/shard_map/ppermute | solution.py:232
  45.1 0.0 collective-permute-done.4.near
  45.2 4.6 %collective-permute-done.3.far = bf16[576,128]{1,0:T(8,128)(2,1)S(1)} collective-permute-done((bf16[576,128]{1,0:T(8,128)(2,1)S(1)}, bf16[576,128]{1,0:T(8,128)(2,1)S(1)}, u32[]{:S(2)}, u32[]{:S(2)}) %collective-permute-start.3) | collective-permute-done | bytes 147488 | tf_op jit(solution)/shard_map/ppermute | solution.py:232
  49.7 0.4 all-to-all-done.1.recv
  50.1 0.3 shard_map.104
  50.4 0.1 shard_map.105
  50.5 18.5 %all_to_all.31.recv = bf16[8,80,128]{2,1,0:T(8,128)(2,1)S(1)} all-to-all(bf16[8,80,128]{2,1,0:T(8,128)(2,1)S(1)} %shard_map.105), channel_id=1, replica_groups=mesh['y'=8,'zh'=4,'x'=4,'zl'=3,'c'=2] {'y'}, dimensions={0} | all-to-all | bytes 327680 | tf_op jit(solution)/shard_map/all_to_all | solution.py:225
  69.0 0.7 shard_map.106
  69.7 10.7 %all-to-all-start.3 = ((bf16[12,80,128]{2,1,0:T(8,128)(2,1)}), bf16[12,80,128]{2,1,0:T(8,128)(2,1)S(1)}, u32[]{:S(2)}, u32[]{:S(2)}) async-start(bf16[12,80,128]{2,1,0:T(8,128)(2,1)} %shard_map.106), calls=%async_computation.3 | async-start | bytes 491520 | tf_op jit(solution)/shard_map/all_to_all | solution.py:225
  80.4 3.3 %collective-permute-start.5 = (bf16[4,48,128]{2,1,0:T(8,128)(2,1)S(1)}, bf16[4,48,128]{2,1,0:T(8,128)(2,1)S(1)}, u32[]{:S(2)}, u32[]{:S(2)}) collective-permute-start(bf16[4,48,128]{2,1,0:T(8,128)(2,1)S(1)} %get-tuple-element.57), channel_id=1, source_target_pairs={{0,2},{2,4},{4,0},{1,3},{3,5},{5,1},{6,8},{8,10},{10,6},{7,9},{9,1... | collective-permute-start | bytes 147464 | tf_op jit(solution)/shard_map/ppermute | solution.py:292
  83.7 2.9 %collective-permute-start.6 = (bf16[4,48,128]{2,1,0:T(8,128)(2,1)S(1)}, bf16[4,48,128]{2,1,0:T(8,128)(2,1)S(1)}, u32[]{:S(2)}, u32[]{:S(2)}) collective-permute-start(bf16[4,48,128]{2,1,0:T(8,128)(2,1)S(1)} %get-tuple-element.58), channel_id=1, source_target_pairs={{0,4},{2,0},{4,2},{1,5},{3,1},{5,3},{6,10},{8,6},{10,8},{7,11},{9,... | collective-permute-start | bytes 147464 | tf_op jit(solution)/shard_map/ppermute | solution.py:293
  86.6 0.6 collective-permute-done.5.low
  87.2 3.7 %collective-permute-done.6.high = bf16[4,48,128]{2,1,0:T(8,128)(2,1)S(1)} collective-permute-done((bf16[4,48,128]{2,1,0:T(8,128)(2,1)S(1)}, bf16[4,48,128]{2,1,0:T(8,128)(2,1)S(1)}, u32[]{:S(2)}, u32[]{:S(2)}) %collective-permute-start.6) | collective-permute-done | bytes 49184 | tf_op jit(solution)/shard_map/ppermute | solution.py:293
  91.0 1.8 %all-to-all-done.3.refs_0_ = bf16[12,80,128]{2,1,0:T(8,128)(2,1)S(1)} async-done(((bf16[12,80,128]{2,1,0:T(8,128)(2,1)}), bf16[12,80,128]{2,1,0:T(8,128)(2,1)S(1)}, u32[]{:S(2)}, u32[]{:S(2)}) %all-to-all-start.3) | async-done | bytes 245792 | tf_op jit(solution)/shard_map/all_to_all | solution.py:225
  92.8 0.6 shard_map.107
  93.4 10.5 %all_to_all.32 = bf16[8,72,128]{2,1,0:T(8,128)(2,1)S(1)} all-to-all(bf16[8,72,128]{2,1,0:T(8,128)(2,1)S(1)} %get-tuple-element.60), channel_id=1, replica_groups=mesh['y'=8,'zh'=4,'x'=4,'zl'=3,'c'=2] {'y'}, dimensions={0} | all-to-all | bytes 294912 | tf_op jit(solution)/shard_map/all_to_all | solution.py:225
  103.9 0.1 shard_map.108
  104.0 10.5 %all_to_all.33.block = bf16[4,720,128]{2,1,0:T(8,128)(2,1)S(1)} all-to-all(bf16[4,720,128]{2,1,0:T(8,128)(2,1)S(1)} %shard_map.108), channel_id=1, replica_groups=mesh['y'=8,'zh'=4,'x'=4,'zl'=3,'c'=2] {'x'}, dimensions={0} | all-to-all | bytes 1474560 | tf_op jit(solution)/shard_map/all_to_all | solution.py:225
  114.4 10.8 %collective-permute-start.7 = (bf16[4,720,128]{2,1,0:T(8,128)(2,1)S(1)}, bf16[4,720,128]{2,1,0:T(8,128)(2,1)S(1)}, u32[]{:S(2)}, u32[]{:S(2)}) collective-permute-start(bf16[4,720,128]{2,1,0:T(8,128)(2,1)S(1)} %all_to_all.33.block), channel_id=1, source_target_pairs={{0,1},{1,0},{2,3},{3,2},{4,5},{5,4},{6,7},{7,6},{8,9},{9,8},{10,11... | collective-permute-start | bytes 2211848 | tf_op jit(solution)/shard_map/ppermute | solution.py:236
  125.2 1.2 shard_map.109
  126.4 0.6 collective-permute-done.7.block
  127.0 1.2 shard_map.110
Async XLA Ops:
  23.0 7.5 %collective-permute-start.1 = (bf16[576,128]{1,0:T(8,128)(2,1)S(1)}, bf16[576,128]{1,0:T(8,128)(2,1)S(1)}, u32[]{:S(2)}, u32[]{:S(2)}) collective-permute-start(bf16[576,128]{1,0:T(8,128)(2,1)S(1)} %bitcast.9), channel_id=1, source_target_pairs={{1,2},{3,4},{5,6},{7,8},{9,10},{11,12},{13,14},{15,16},{17,18},{19... | collective-permute-start | bytes 442376 | tf_op jit(solution)/shard_map/ppermute | solution.py:232
  26.0 4.5 %collective-permute-start = (bf16[576,128]{1,0:T(8,128)(2,1)S(1)}, bf16[576,128]{1,0:T(8,128)(2,1)S(1)}, u32[]{:S(2)}, u32[]{:S(2)}) collective-permute-start(bf16[576,128]{1,0:T(8,128)(2,1)S(1)} %bitcast.10), channel_id=1, source_target_pairs={{0,1},{1,0},{2,3},{3,2},{4,5},{5,4},{6,7},{7,6},{8,9},{9,8},{10,11... | collective-permute-start | bytes 442376 | tf_op jit(solution)/shard_map/ppermute | solution.py:236
  32.2 3.4 %collective-permute-start.2 = (bf16[1088,128]{1,0:T(8,128)(2,1)S(1)}, bf16[1088,128]{1,0:T(8,128)(2,1)S(1)}, u32[]{:S(2)}, u32[]{:S(2)}) collective-permute-start(bf16[1088,128]{1,0:T(8,128)(2,1)S(1)} %get-tuple-element.47), channel_id=1, source_target_pairs={{0,1},{1,0},{2,3},{3,2},{4,5},{5,4},{6,7},{7,6},{8,9},{9,8},{10,11... | collective-permute-start | bytes 835592 | tf_op jit(solution)/shard_map/ppermute | solution.py:236
  36.7 13.4 %all-to-all-start.1 = ((bf16[4,584,128]{2,1,0:T(8,128)(2,1)}), bf16[4,584,128]{2,1,0:T(8,128)(2,1)S(1)}, u32[]{:S(2)}, u32[]{:S(2)}) async-start(bf16[4,584,128]{2,1,0:T(8,128)(2,1)} %shard_map.103), calls=%async_computation.1 | async-start | bytes 1196032 | tf_op jit(solution)/shard_map/all_to_all | solution.py:225
  40.4 4.7 %collective-permute-start.4 = (bf16[576,128]{1,0:T(8,128)(2,1)S(1)}, bf16[576,128]{1,0:T(8,128)(2,1)S(1)}, u32[]{:S(2)}, u32[]{:S(2)}) collective-permute-start(bf16[576,128]{1,0:T(8,128)(2,1)S(1)} %get-tuple-element.48.own), channel_id=1, source_target_pairs={{0,1},{1,0},{2,3},{3,2},{4,5},{5,4},{6,7},{7,6},{8,9},{9,8},{10,11... | collective-permute-start | bytes 442376 | tf_op jit(solution)/shard_map/ppermute | solution.py:236
  43.0 6.8 %collective-permute-start.3 = (bf16[576,128]{1,0:T(8,128)(2,1)S(1)}, bf16[576,128]{1,0:T(8,128)(2,1)S(1)}, u32[]{:S(2)}, u32[]{:S(2)}) collective-permute-start(bf16[576,128]{1,0:T(8,128)(2,1)S(1)} %get-tuple-element.48.own), channel_id=1, source_target_pairs={{1,2},{3,4},{5,6},{7,8},{9,10},{11,12},{13,14},{15,16},{17,18},{19... | collective-permute-start | bytes 442376 | tf_op jit(solution)/shard_map/ppermute | solution.py:232
  69.7 23.1 %all-to-all-start.3 = ((bf16[12,80,128]{2,1,0:T(8,128)(2,1)}), bf16[12,80,128]{2,1,0:T(8,128)(2,1)S(1)}, u32[]{:S(2)}, u32[]{:S(2)}) async-start(bf16[12,80,128]{2,1,0:T(8,128)(2,1)} %shard_map.106), calls=%async_computation.3 | async-start | bytes 491520 | tf_op jit(solution)/shard_map/all_to_all | solution.py:225
  80.4 6.8 %collective-permute-start.5 = (bf16[4,48,128]{2,1,0:T(8,128)(2,1)S(1)}, bf16[4,48,128]{2,1,0:T(8,128)(2,1)S(1)}, u32[]{:S(2)}, u32[]{:S(2)}) collective-permute-start(bf16[4,48,128]{2,1,0:T(8,128)(2,1)S(1)} %get-tuple-element.57), channel_id=1, source_target_pairs={{0,2},{2,4},{4,0},{1,3},{3,5},{5,1},{6,8},{8,10},{10,6},{7,9},{9,1... | collective-permute-start | bytes 147464 | tf_op jit(solution)/shard_map/ppermute | solution.py:292
  83.7 7.2 %collective-permute-start.6 = (bf16[4,48,128]{2,1,0:T(8,128)(2,1)S(1)}, bf16[4,48,128]{2,1,0:T(8,128)(2,1)S(1)}, u32[]{:S(2)}, u32[]{:S(2)}) collective-permute-start(bf16[4,48,128]{2,1,0:T(8,128)(2,1)S(1)} %get-tuple-element.58), channel_id=1, source_target_pairs={{0,4},{2,0},{4,2},{1,5},{3,1},{5,3},{6,10},{8,6},{10,8},{7,11},{9,... | collective-permute-start | bytes 147464 | tf_op jit(solution)/shard_map/ppermute | solution.py:293
  114.4 12.6 %collective-permute-start.7 = (bf16[4,720,128]{2,1,0:T(8,128)(2,1)S(1)}, bf16[4,720,128]{2,1,0:T(8,128)(2,1)S(1)}, u32[]{:S(2)}, u32[]{:S(2)}) collective-permute-start(bf16[4,720,128]{2,1,0:T(8,128)(2,1)S(1)} %all_to_all.33.block), channel_id=1, source_target_pairs={{0,1},{1,0},{2,3},{3,2},{4,5},{5,4},{6,7},{7,6},{8,9},{9,8},{10,11... | collective-permute-start | bytes 2211848 | tf_op jit(solution)/shard_map/ppermute | solution.py:236

commit v5 on v4

--- a/solution.py
+++ b/solution.py
@@ -277,7 +277,8 @@
     s_far, s_near = halos(scaled)
     partial = call(partial_kernel, [VMEM] * 3, sds((N_X, f_in + TAIL, TILE)))(keep, grad, recv)
     from_x = exchange(partial, "x")
-    from_x, s_far, s_near = lax.optimization_barrier((from_x, s_far, s_near))
+    from_y = exchange(call(x_kernel, [VMEM], sds((N_Y, ROWS + TAIL, TILE)))(from_x), "y")
+    from_y, s_far, s_near = lax.optimization_barrier((from_y, s_far, s_near))
     zl = lax.axis_index("zl").astype(jnp.int32).reshape(1)
     pair = sds((N_X, 2 * width, TILE))
     stay, up, down = call(
@@ -286,12 +287,10 @@
         (pair,) * 3,
         [pltpu.VMEM((N_FEAT, width, TILE), F32)],
     )(core, zl, s_near, s_far, scaled, adj, back)
-    from_x, stay, up, down = lax.optimization_barrier((from_x, stay, up, down))
-    from_y = exchange(call(x_kernel, [VMEM], sds((N_Y, ROWS + TAIL, TILE)))(from_x), "y")
+    from_y, stay, up, down = lax.optimization_barrier((from_y, stay, up, down))
     from_line = exchange(call(y_kernel, [VMEM], sds((N_LINE, ROWS + TAIL, TILE)))(from_y), LINE)
     f_low = lax.ppermute(up, "zl", [(i, (i + 1) % 3) for i in range(3)])
     f_high = lax.ppermute(down, "zl", [(i, (i + 2) % 3) for i in range(3)])
-    from_line, f_low, f_high = lax.optimization_barrier((from_line, f_low, f_high))
     to_y, bias_sum = call(
         lambda *refs: line_kernel(scale, *refs),
         [VMEM],

time: 129 us -> 132 us (1.023)
  blocking collectives: 60.4 us -> 66.4 us
  waiting for transfers between devices: 15.8 us -> 14.1 us
    all_to_all x4, blocking collectives: 60.4 us -> 66.4 us  [exchange(): return lax.all_to_all(x, axis, split_axis=0, concat_axis=0, tiled=False)]
    ppermute x4, starting transfers between devices: 17.1 us -> 13 us  [swap(): return lax.ppermute(x, 'c', [(0, 1), (1, 0)])]
    ppermute x1, starting transfers between devices: 3.32 us -> 5.9 us  [local(): f_low = lax.ppermute(up, 'zl', [(i, (i + 1) % 3) for i in range(3)])]
    all_to_all x2, waiting for transfers between devices: 2.23 us -> 0.01 us  [exchange(): return lax.all_to_all(x, axis, split_axis=0, concat_axis=0, tiled=False)]
    all_to_all x2, starting transfers between devices: 14.3 us -> 16.2 us  [exchange(): return lax.all_to_all(x, axis, split_axis=0, concat_axis=0, tiled=False)]
    ppermute x2, waiting for transfers between devices: 7.1 us -> 8.65 us  [halos(): return (lax.ppermute(x, AXES, pairs), near)]
  transfers between devices with their start and end apart: 10 -> 10, of which waited for: 8 -> 5; matrix products, arithmetic and copies ran while one was open for 0% -> 0% of each run, Pallas kernels for 1% -> 1%
where the time goes in v5:
time: 132 us; the launch traced here: 131 us
  blocking collectives  66.4 us (50%)
  starting transfers between devices  41.9 us (32%)
  waiting for transfers between devices  14.1 us (11%)
  Pallas kernels  7.81 us (6%)
    all_to_all x4, blocking collectives, exchange(): return lax.all_to_all(x, axis, split_axis=0, concat_axis=0, tiled=False)  66.4 us
    all_to_all x2, starting transfers between devices, exchange(): return lax.all_to_all(x, axis, split_axis=0, concat_axis=0, tiled=False)  16.2 us
    ppermute x4, starting transfers between devices, swap(): return lax.ppermute(x, 'c', [(0, 1), (1, 0)])  13 us
    ppermute x2, waiting for transfers between devices, halos(): return (lax.ppermute(x, AXES, pairs), near)  8.65 us
    ppermute x1, starting transfers between devices, local(): f_low = lax.ppermute(up, 'zl', [(i, (i + 1) % 3) for i in range(3)])  5.9 us
    ppermute x2, starting transfers between devices, halos(): return (lax.ppermute(x, AXES, pairs), near)  4.9 us
    ppermute x1, waiting for transfers between devices, local(): f_high = lax.ppermute(down, 'zl', [(i, (i + 2) % 3) for i in range(3)])  3.3 us
  transfers between devices with their start and end apart: 10, of which 5 were waited for; matrix products, arithmetic and copies ran while one was open for 0% of the time, Pallas kernels for 1%

profile of v5, /device:TPU:1, one launch (start us, length us, event | category | flops | bytes accessed | tf_op | source)
XLA Modules:
  0.0 131.0 jit_solution(9481148181354241384)
XLA Ops:
  0.7 1.5 %shard_map.101 = (bf16[24,24,128]{2,1,0:T(8,128)(2,1)S(1)}, bf16[128,384]{1,0:T(8,128)(2,1)S(1)}, bf16[576,512]{1,0:T(8,128)(2,1)S(1)}, bf16[576,512]{1,0:T(8,12...) custom-call(s32[1]{0:T(128)} %bitcast.1.tile, bf16[24,3072]{1,0:T(8,128)(2,1)} %bitcast.14, ...), custom_call_target="tpu_custom_call" | custom-call | tf_op jit(solution)/shard_map/pallas_call | solution.py:249
  2.1 20.9 %all_to_all.30 = bf16[24,24,128]{2,1,0:T(8,128)(2,1)S(1)} all-to-all(bf16[24,24,128]{2,1,0:T(8,128)(2,1)S(1)} %get-tuple-element.35), channel_id=1, replica_groups=mesh['y'=8,'zh'=4,'x'=4,'zl'=3,'c'=2] {'x','zl','c'}, dimensions={0} | all-to-all | bytes 294912 | tf_op jit(solution)/shard_map/all_to_all | solution.py:225
  23.0 3.0 %collective-permute-start.1 = (bf16[576,128]{1,0:T(8,128)(2,1)S(1)}, bf16[576,128]{1,0:T(8,128)(2,1)S(1)}, u32[]{:S(2)}, u32[]{:S(2)}) collective-permute-start(bf16[576,128]{1,0:T(8,128)(2,1)S(1)} %bitcast.10), channel_id=1, source_target_pairs={{1,2},{3,4},{5,6},{7,8},{9,10},{11,12},{13,14},{15,16},{17,18},{19... | collective-permute-start | bytes 442376 | tf_op jit(solution)/shard_map/ppermute | solution.py:232
  26.0 1.9 %collective-permute-start = (bf16[576,128]{1,0:T(8,128)(2,1)S(1)}, bf16[576,128]{1,0:T(8,128)(2,1)S(1)}, u32[]{:S(2)}, u32[]{:S(2)}) collective-permute-start(bf16[576,128]{1,0:T(8,128)(2,1)S(1)} %bitcast.11), channel_id=1, source_target_pairs={{0,1},{1,0},{2,3},{3,2},{4,5},{5,4},{6,7},{7,6},{8,9},{9,8},{10,11... | collective-permute-start | bytes 442376 | tf_op jit(solution)/shard_map/ppermute | solution.py:236
  27.9 2.5 %collective-permute-done.1.far = bf16[576,128]{1,0:T(8,128)(2,1)S(1)} collective-permute-done((bf16[576,128]{1,0:T(8,128)(2,1)S(1)}, bf16[576,128]{1,0:T(8,128)(2,1)S(1)}, u32[]{:S(2)}, u32[]{:S(2)}) %collective-permute-start.1) | collective-permute-done | bytes 147488 | tf_op jit(solution)/shard_map/ppermute | solution.py:232
  30.5 0.0 collective-permute-done.near
  30.5 1.7 %shard_map.102 = (bf16[128,512]{1,0:T(8,128)(2,1)}, bf16[128,512]{1,0:T(8,128)(2,1)S(1)}, bf16[576,128]{1,0:T(8,128)(2,1)S(1)}, bf16[1088,128]{1,0:T(8,128)(2,1)...) custom-call(s32[1]{0:T(128)} %bitcast.core, bf16[576,128]{1,0:T(8,128)(2,1)S(1)} %collective-permute-done.near, ...), custom_call_target="tpu_custom_call" | custom-call | tf_op jit(solution)/shard_map/pallas_call | solution.py:271
  32.2 1.9 %collective-permute-start.2 = (bf16[1088,128]{1,0:T(8,128)(2,1)S(1)}, bf16[1088,128]{1,0:T(8,128)(2,1)S(1)}, u32[]{:S(2)}, u32[]{:S(2)}) collective-permute-start(bf16[1088,128]{1,0:T(8,128)(2,1)S(1)} %get-tuple-element.44), channel_id=1, source_target_pairs={{0,1},{1,0},{2,3},{3,2},{4,5},{5,4},{6,7},{7,6},{8,9},{9,8},{10,11... | collective-permute-start | bytes 835592 | tf_op jit(solution)/shard_map/ppermute | solution.py:236
  34.1 1.5 %collective-permute-done.2.recv = bf16[1088,128]{1,0:T(8,128)(2,1)S(1)} collective-permute-done((bf16[1088,128]{1,0:T(8,128)(2,1)S(1)}, bf16[1088,128]{1,0:T(8,128)(2,1)S(1)}, u32[]{:S(2)}, u32[]{:S(2)}) %collective-permute-start.2) | collective-permute-done | bytes 278560 | tf_op jit(solution)/shard_map/ppermute | solution.py:236
  35.6 0.3 shard_map.103
  35.9 13.2 %all_to_all.31.recv = bf16[4,584,128]{2,1,0:T(8,128)(2,1)S(1)} all-to-all(bf16[4,584,128]{2,1,0:T(8,128)(2,1)S(1)} %shard_map.103), channel_id=1, replica_groups=mesh['y'=8,'zh'=4,'x'=4,'zl'=3,'c'=2] {'x'}, dimensions={0} | all-to-all | bytes 1196032 | tf_op jit(solution)/shard_map/all_to_all | solution.py:225
  49.1 0.7 shard_map.104
  49.8 9.3 %all-to-all-start.2 = ((bf16[8,80,128]{2,1,0:T(8,128)(2,1)}), bf16[8,80,128]{2,1,0:T(8,128)(2,1)S(1)}, u32[]{:S(2)}, u32[]{:S(2)}) async-start(bf16[8,80,128]{2,1,0:T(8,128)(2,1)} %shard_map.104), calls=%async_computation.2 | async-start | bytes 327680 | tf_op jit(solution)/shard_map/all_to_all | solution.py:225
  59.1 3.7 %collective-permute-start.4 = (bf16[576,128]{1,0:T(8,128)(2,1)S(1)}, bf16[576,128]{1,0:T(8,128)(2,1)S(1)}, u32[]{:S(2)}, u32[]{:S(2)}) collective-permute-start(bf16[576,128]{1,0:T(8,128)(2,1)S(1)} %get-tuple-element.45.own), channel_id=1, source_target_pairs={{0,1},{1,0},{2,3},{3,2},{4,5},{5,4},{6,7},{7,6},{8,9},{9,8},{10,11... | collective-permute-start | bytes 442376 | tf_op jit(solution)/shard_map/ppermute | solution.py:236
  62.8 1.9 %collective-permute-start.3 = (bf16[576,128]{1,0:T(8,128)(2,1)S(1)}, bf16[576,128]{1,0:T(8,128)(2,1)S(1)}, u32[]{:S(2)}, u32[]{:S(2)}) collective-permute-start(bf16[576,128]{1,0:T(8,128)(2,1)S(1)} %get-tuple-element.45.own), channel_id=1, source_target_pairs={{1,2},{3,4},{5,6},{7,8},{9,10},{11,12},{13,14},{15,16},{17,18},{19... | collective-permute-start | bytes 442376 | tf_op jit(solution)/shard_map/ppermute | solution.py:232
  64.7 0.0 collective-permute-done.4.near
  64.7 6.1 %collective-permute-done.3.far = bf16[576,128]{1,0:T(8,128)(2,1)S(1)} collective-permute-done((bf16[576,128]{1,0:T(8,128)(2,1)S(1)}, bf16[576,128]{1,0:T(8,128)(2,1)S(1)}, u32[]{:S(2)}, u32[]{:S(2)}) %collective-permute-start.3) | collective-permute-done | bytes 147488 | tf_op jit(solution)/shard_map/ppermute | solution.py:232
  70.8 0.0 all-to-all-done.2.recv
  70.8 0.3 shard_map.105
  71.2 20.8 %all_to_all.32.refs_0_ = bf16[12,80,128]{2,1,0:T(8,128)(2,1)S(1)} all-to-all(bf16[12,80,128]{2,1,0:T(8,128)(2,1)S(1)} %shard_map.106), channel_id=1, replica_groups=mesh['y'=8,'zh'=4,'x'=4,'zl'=3,'c'=2] {'zh','zl'}, dimensions={0} | all-to-all | bytes 491520 | tf_op jit(solution)/shard_map/all_to_all | solution.py:225
  92.0 0.7 shard_map.107
  92.7 6.9 %all-to-all-start.4 = ((bf16[8,72,128]{2,1,0:T(8,128)(2,1)}), bf16[8,72,128]{2,1,0:T(8,128)(2,1)S(1)}, u32[]{:S(2)}, u32[]{:S(2)}) async-start(bf16[8,72,128]{2,1,0:T(8,128)(2,1)} %get-tuple-element.54), calls=%async_computation.4 | async-start | bytes 294912 | tf_op jit(solution)/shard_map/all_to_all | solution.py:225
  99.6 5.9 %collective-permute-start.5 = (bf16[4,48,128]{2,1,0:T(8,128)(2,1)S(1)}, bf16[4,48,128]{2,1,0:T(8,128)(2,1)S(1)}, u32[]{:S(2)}, u32[]{:S(2)}) collective-permute-start(bf16[4,48,128]{2,1,0:T(8,128)(2,1)S(1)} %get-tuple-element.56), channel_id=1, source_target_pairs={{0,2},{2,4},{4,0},{1,3},{3,5},{5,1},{6,8},{8,10},{10,6},{7,9},{9,1... | collective-permute-start | bytes 147464 | tf_op jit(solution)/shard_map/ppermute | solution.py:292
  105.6 1.9 %collective-permute-start.6 = (bf16[4,48,128]{2,1,0:T(8,128)(2,1)S(1)}, bf16[4,48,128]{2,1,0:T(8,128)(2,1)S(1)}, u32[]{:S(2)}, u32[]{:S(2)}) collective-permute-start(bf16[4,48,128]{2,1,0:T(8,128)(2,1)S(1)} %get-tuple-element.57), channel_id=1, source_target_pairs={{0,4},{2,0},{4,2},{1,5},{3,1},{5,3},{6,10},{8,6},{10,8},{7,11},{9,... | collective-permute-start | bytes 147464 | tf_op jit(solution)/shard_map/ppermute | solution.py:293
  107.5 0.0 collective-permute-done.5.low
  107.5 3.3 %collective-permute-done.6.high = bf16[4,48,128]{2,1,0:T(8,128)(2,1)S(1)} collective-permute-done((bf16[4,48,128]{2,1,0:T(8,128)(2,1)S(1)}, bf16[4,48,128]{2,1,0:T(8,128)(2,1)S(1)}, u32[]{:S(2)}, u32[]{:S(2)}) %collective-permute-start.6) | collective-permute-done | bytes 49184 | tf_op jit(solution)/shard_map/ppermute | solution.py:293
  110.8 0.0 all-to-all-done.4
  110.8 0.1 shard_map.108
  110.9 11.5 %all_to_all.33.block = bf16[4,720,128]{2,1,0:T(8,128)(2,1)S(1)} all-to-all(bf16[4,720,128]{2,1,0:T(8,128)(2,1)S(1)} %shard_map.108), channel_id=1, replica_groups=mesh['y'=8,'zh'=4,'x'=4,'zl'=3,'c'=2] {'x'}, dimensions={0} | all-to-all | bytes 1474560 | tf_op jit(solution)/shard_map/all_to_all | solution.py:225
  122.4 5.5 %collective-permute-start.7 = (bf16[4,720,128]{2,1,0:T(8,128)(2,1)S(1)}, bf16[4,720,128]{2,1,0:T(8,128)(2,1)S(1)}, u32[]{:S(2)}, u32[]{:S(2)}) collective-permute-start(bf16[4,720,128]{2,1,0:T(8,128)(2,1)S(1)} %all_to_all.33.block), channel_id=1, source_target_pairs={{0,1},{1,0},{2,3},{3,2},{4,5},{5,4},{6,7},{7,6},{8,9},{9,8},{10,11... | collective-permute-start | bytes 2211848 | tf_op jit(solution)/shard_map/ppermute | solution.py:236
  127.9 1.2 shard_map.109
  129.2 0.6 collective-permute-done.7.block
  129.7 1.2 shard_map.110
  (1 shorter events, 0.0 us)
Async XLA Ops:
  23.0 7.5 %collective-permute-start.1 = (bf16[576,128]{1,0:T(8,128)(2,1)S(1)}, bf16[576,128]{1,0:T(8,128)(2,1)S(1)}, u32[]{:S(2)}, u32[]{:S(2)}) collective-permute-start(bf16[576,128]{1,0:T(8,128)(2,1)S(1)} %bitcast.10), channel_id=1, source_target_pairs={{1,2},{3,4},{5,6},{7,8},{9,10},{11,12},{13,14},{15,16},{17,18},{19... | collective-permute-start | bytes 442376 | tf_op jit(solution)/shard_map/ppermute | solution.py:232
  26.0 4.5 %collective-permute-start = (bf16[576,128]{1,0:T(8,128)(2,1)S(1)}, bf16[576,128]{1,0:T(8,128)(2,1)S(1)}, u32[]{:S(2)}, u32[]{:S(2)}) collective-permute-start(bf16[576,128]{1,0:T(8,128)(2,1)S(1)} %bitcast.11), channel_id=1, source_target_pairs={{0,1},{1,0},{2,3},{3,2},{4,5},{5,4},{6,7},{7,6},{8,9},{9,8},{10,11... | collective-permute-start | bytes 442376 | tf_op jit(solution)/shard_map/ppermute | solution.py:236
  32.2 3.4 %collective-permute-start.2 = (bf16[1088,128]{1,0:T(8,128)(2,1)S(1)}, bf16[1088,128]{1,0:T(8,128)(2,1)S(1)}, u32[]{:S(2)}, u32[]{:S(2)}) collective-permute-start(bf16[1088,128]{1,0:T(8,128)(2,1)S(1)} %get-tuple-element.44), channel_id=1, source_target_pairs={{0,1},{1,0},{2,3},{3,2},{4,5},{5,4},{6,7},{7,6},{8,9},{9,8},{10,11... | collective-permute-start | bytes 835592 | tf_op jit(solution)/shard_map/ppermute | solution.py:236
  49.8 21.0 %all-to-all-start.2 = ((bf16[8,80,128]{2,1,0:T(8,128)(2,1)}), bf16[8,80,128]{2,1,0:T(8,128)(2,1)S(1)}, u32[]{:S(2)}, u32[]{:S(2)}) async-start(bf16[8,80,128]{2,1,0:T(8,128)(2,1)} %shard_map.104), calls=%async_computation.2 | async-start | bytes 327680 | tf_op jit(solution)/shard_map/all_to_all | solution.py:225
  59.1 5.6 %collective-permute-start.4 = (bf16[576,128]{1,0:T(8,128)(2,1)S(1)}, bf16[576,128]{1,0:T(8,128)(2,1)S(1)}, u32[]{:S(2)}, u32[]{:S(2)}) collective-permute-start(bf16[576,128]{1,0:T(8,128)(2,1)S(1)} %get-tuple-element.45.own), channel_id=1, source_target_pairs={{0,1},{1,0},{2,3},{3,2},{4,5},{5,4},{6,7},{7,6},{8,9},{9,8},{10,11... | collective-permute-start | bytes 442376 | tf_op jit(solution)/shard_map/ppermute | solution.py:236
  62.8 8.0 %collective-permute-start.3 = (bf16[576,128]{1,0:T(8,128)(2,1)S(1)}, bf16[576,128]{1,0:T(8,128)(2,1)S(1)}, u32[]{:S(2)}, u32[]{:S(2)}) collective-permute-start(bf16[576,128]{1,0:T(8,128)(2,1)S(1)} %get-tuple-element.45.own), channel_id=1, source_target_pairs={{1,2},{3,4},{5,6},{7,8},{9,10},{11,12},{13,14},{15,16},{17,18},{19... | collective-permute-start | bytes 442376 | tf_op jit(solution)/shard_map/ppermute | solution.py:232
  92.7 18.1 %all-to-all-start.4 = ((bf16[8,72,128]{2,1,0:T(8,128)(2,1)}), bf16[8,72,128]{2,1,0:T(8,128)(2,1)S(1)}, u32[]{:S(2)}, u32[]{:S(2)}) async-start(bf16[8,72,128]{2,1,0:T(8,128)(2,1)} %get-tuple-element.54), calls=%async_computation.4 | async-start | bytes 294912 | tf_op jit(solution)/shard_map/all_to_all | solution.py:225
  99.6 7.8 %collective-permute-start.5 = (bf16[4,48,128]{2,1,0:T(8,128)(2,1)S(1)}, bf16[4,48,128]{2,1,0:T(8,128)(2,1)S(1)}, u32[]{:S(2)}, u32[]{:S(2)}) collective-permute-start(bf16[4,48,128]{2,1,0:T(8,128)(2,1)S(1)} %get-tuple-element.56), channel_id=1, source_target_pairs={{0,2},{2,4},{4,0},{1,3},{3,5},{5,1},{6,8},{8,10},{10,6},{7,9},{9,1... | collective-permute-start | bytes 147464 | tf_op jit(solution)/shard_map/ppermute | solution.py:292
  105.6 5.2 %collective-permute-start.6 = (bf16[4,48,128]{2,1,0:T(8,128)(2,1)S(1)}, bf16[4,48,128]{2,1,0:T(8,128)(2,1)S(1)}, u32[]{:S(2)}, u32[]{:S(2)}) collective-permute-start(bf16[4,48,128]{2,1,0:T(8,128)(2,1)S(1)} %get-tuple-element.57), channel_id=1, source_target_pairs={{0,4},{2,0},{4,2},{1,5},{3,1},{5,3},{6,10},{8,6},{10,8},{7,11},{9,... | collective-permute-start | bytes 147464 | tf_op jit(solution)/shard_map/ppermute | solution.py:293
  122.4 7.3 %collective-permute-start.7 = (bf16[4,720,128]{2,1,0:T(8,128)(2,1)S(1)}, bf16[4,720,128]{2,1,0:T(8,128)(2,1)S(1)}, u32[]{:S(2)}, u32[]{:S(2)}) collective-permute-start(bf16[4,720,128]{2,1,0:T(8,128)(2,1)S(1)} %all_to_all.33.block), channel_id=1, source_target_pairs={{0,1},{1,0},{2,3},{3,2},{4,5},{5,4},{6,7},{7,6},{8,9},{9,8},{10,11... | collective-permute-start | bytes 2211848 | tf_op jit(solution)/shard_map/ppermute | solution.py:236

commit v6 on v4

--- a/solution.py
+++ b/solution.py
@@ -53,25 +53,29 @@
     return dot(jnp.concatenate(parts, axis=1), adj, 1, 1)
 
 
-def prepare_kernel(tile, feats, adjacency, *refs):
-    held, sems = refs[-2:]
+def prepare_kernel(feats, out, held, sem):
+    copy = pltpu.make_async_copy(feats, held, sem)
+    copy.start()
+    copy.wait()
+    for t in range(N_FEAT):
+        out[t] = held[:, lanes(t)]
+
+
+def load_kernel(tile, adjacency, *refs):
     rows = pl.ds(pl.multiple_of(tile[0] * TILE, TILE), TILE)
-    pairs = [(feats, held), (adjacency.at[rows], refs[5])]
-    pairs += [(refs[i], refs[i + 6]) for i in range(4)]
-    out = refs[4]
-    copies = [pltpu.make_async_copy(s, d, sems.at[i]) for i, (s, d) in enumerate(pairs)]
+    sources, targets, sems = (adjacency.at[rows],) + refs[:4], refs[4:-1], refs[-1]
+    copies = [
+        pltpu.make_async_copy(s, d, sems.at[i])
+        for i, (s, d) in enumerate(zip(sources, targets, strict=True))
+    ]
     for c in copies:
         c.start()
-    copies[0].wait()
-    for t in range(N_FEAT):
-        out[t] = held[:, lanes(t)]
-    for c in copies[1:]:
+    for c in copies:
         c.wait()
 
 
-def sides(core, far, near):
+def sides(core, f, n):
     first = core[0] == 0
-    f, n = far[...], near[...]
     return jnp.where(first, f, n), jnp.where(first, n, f)
 
 
@@ -80,7 +84,7 @@
 ):
     a = adj[...]
     degree = (1.0 + dot(jnp.ones((8, 3 * TILE), BF16), a, 1, 1))[:1]
-    low, high = sides(core, far, near)
+    low, high = sides(core, far[...], near[...])
     m = (band((low, own[...], high), a) / degree).astype(BF16)
     x = own[...]
     pre = dot(x, ws[...], 0, 0) + dot(m, wn[...], 0, 0) + bias[...]
@@ -95,10 +99,13 @@
         send[576 + b * TILE : 576 + (b + 1) * TILE] = g[:, lanes(b)]
     back[...] = dot(ws[...], g, 1, 1).astype(BF16)
     rounded = dot(wn[...], g, 1, 1).astype(BF16).astype(F32)
-    scaled[...] = (rounded / degree).astype(BF16)
-
-
-def partial_kernel(keep, grad, recv, out):
+    scale = (rounded / degree).astype(BF16)
+    scaled[...] = scale
+    send[576 + 4 * TILE :] = scale
+
+
+def partial_kernel(keep, grad, recv, act, out, act_out):
+    act_out[...] = act[...]
     f_in = keep.shape[0]
     rows = [recv[f_in + b * TILE : f_in + (b + 1) * TILE] for b in range(N_X)]
     g = jnp.concatenate([grad[...], jnp.concatenate(rows, axis=1)], axis=0)
@@ -138,8 +145,8 @@
         out[d] = rounded
 
 
-def feat_kernel(core, zl, near, far, own, adj, back, stay, up, down, parts):
-    low, high = sides(core, far, near)
+def feat_kernel(core, zl, recv, far, own, adj, back, stay, up, down, parts):
+    low, high = sides(core, far[...], recv[recv.shape[0] - own.shape[0] :])
     total = back[...].astype(F32) + band((low, own[...], high), adj[...])
     width = parts.shape[1]
     for i in range(N_FEAT):
@@ -225,12 +232,10 @@
     return lax.all_to_all(x, axis, split_axis=0, concat_axis=0, tiled=False)
 
 
-def halos(x):
+def across(x):
     pairs = [(2 * k + 1, 2 * k + 2) for k in range(383)]
     pairs += [(b, a) for a, b in pairs]
-    near = swap(x)
-    return lax.ppermute(x, AXES, pairs), near
-
+    return lax.ppermute(x, AXES, pairs)
 
 def swap(x):
     return lax.ppermute(x, "c", [(0, 1), (1, 0)])
@@ -246,38 +251,40 @@
     wide = sds((f_in, TILE))
     weight = sds((f_in, f_out), F32)
 
-    pieces, *held = call(
-        prepare_kernel,
-        [SMEM] + [ANY] * 6,
+    def pinned(x):
+        return pltpu.with_memory_space_constraint(x, pltpu.HBM)
+
+    pieces = call(
+        prepare_kernel, [ANY], sds((N_FEAT, width, TILE)), [pltpu.VMEM((width, n_rows), BF16), dma]
+    )(pinned(features.T))
+    own = exchange(pieces, FEAT).reshape(f_in, TILE)
+    near, far = swap(own), across(own)
+    held = call(
+        load_kernel,
+        [SMEM] + [ANY] * 5,
         (
-            sds((N_FEAT, width, TILE)),
             sds((TILE, 3 * TILE)),
             sds((f_in, f_out)),
             sds((f_in, f_out)),
             sds((1, f_out), F32),
             sds((TILE, f_out)),
         ),
-        [pltpu.VMEM((width, n_rows), BF16), dma((6,))],
-    )(
-        tile,
-        *(
-            pltpu.with_memory_space_constraint(x, pltpu.HBM)
-            for x in (features.T, adjacency, w_self, w_neigh, bias_out.reshape(1, f_out), cotangent)
-        ),
-    )
+        [dma((5,))],
+    )(tile, *map(pinned, (adjacency, w_self, w_neigh, bias_out.reshape(1, f_out), cotangent)))
+    near, far, held = lax.optimization_barrier((near, far, held))
     adj = held[0]
-    own = exchange(pieces, FEAT).reshape(f_in, TILE)
-    far, near = halos(own)
     act, grad, keep, send, back, scaled = call(
         forward_kernel,
         [SMEM] + [VMEM] * 8,
-        (sds((TILE, f_out)), sds((TILE, f_out)), wide, sds((f_in + f_out, TILE)), wide, wide),
+        (sds((TILE, f_out)), sds((TILE, f_out)), wide, sds((2 * f_in + f_out, TILE)), wide, wide),
     )(core, near, far, own, *held)
     recv = swap(send)
-    s_far, s_near = halos(scaled)
-    partial = call(partial_kernel, [VMEM] * 3, sds((N_X, f_in + TAIL, TILE)))(keep, grad, recv)
+    s_far = across(scaled)
+    partial, act = call(
+        partial_kernel, [VMEM] * 4, (sds((N_X, f_in + TAIL, TILE)), sds((TILE, f_out)))
+    )(keep, grad, recv, act)
     from_x = exchange(partial, "x")
-    from_x, s_far, s_near = lax.optimization_barrier((from_x, s_far, s_near))
+    from_x, s_far = lax.optimization_barrier((from_x, s_far))
     zl = lax.axis_index("zl").astype(jnp.int32).reshape(1)
     pair = sds((N_X, 2 * width, TILE))
     stay, up, down = call(
@@ -285,7 +292,7 @@
         [SMEM] * 2 + [VMEM] * 5,
         (pair,) * 3,
         [pltpu.VMEM((N_FEAT, width, TILE), F32)],
-    )(core, zl, s_near, s_far, scaled, adj, back)
+    )(core, zl, recv, s_far, scaled, adj, back)
     from_x, stay, up, down = lax.optimization_barrier((from_x, stay, up, down))
     from_y = exchange(call(x_kernel, [VMEM], sds((N_Y, ROWS + TAIL, TILE)))(from_x), "y")
     from_line = exchange(call(y_kernel, [VMEM], sds((N_LINE, ROWS + TAIL, TILE)))(from_y), LINE)

time: 129 us -> 126 us (0.977)
  starting transfers between devices: 42.8 us -> 36.1 us
  blocking collectives: 60.4 us -> 63.5 us
    all_to_all x2, starting transfers between devices: 14.3 us -> 9.25 us  [exchange(): return lax.all_to_all(x, axis, split_axis=0, concat_axis=0, tiled=False)]
    all_to_all x2, waiting for transfers between devices: 2.23 us -> 6.25 us  [exchange(): return lax.all_to_all(x, axis, split_axis=0, concat_axis=0, tiled=False)]
    all_to_all x4, blocking collectives: 60.4 us -> 63.5 us  [exchange(): return lax.all_to_all(x, axis, split_axis=0, concat_axis=0, tiled=False)]
    ppermute x4 -> x3, starting transfers between devices: 17.1 us -> 15.2 us  [swap(): return lax.ppermute(x, 'c', [(0, 1), (1, 0)])]
    ppermute x2, waiting for transfers between devices: 7.1 us -> 5.43 us  [across(): return lax.ppermute(x, AXES, pairs)]
    ppermute x1, waiting for transfers between devices: 3.74 us -> 2.29 us  [local(): f_high = lax.ppermute(down, 'zl', [(i, (i + 2) % 3) for i in range(3)])]
    pallas_call x2 -> x3, Pallas kernels: 2.58 us -> 3.46 us  [the longest x1 1.38 us: local(): call(load_kernel, [SMEM] + [ANY] * 5, (sds((TILE, 3 * TILE)), sds((f_in,...]
  transfers between devices with their start and end apart: 10 -> 9, of which waited for: 8 -> 7; matrix products, arithmetic and copies ran while one was open for 0% -> 0% of each run, Pallas kernels for 1% -> 2%
where the time goes in v6:
time: 126 us
  blocking collectives  63.5 us (50%)
  starting transfers between devices  36.1 us (29%)
  waiting for transfers between devices  16.3 us (13%)
  Pallas kernels  8.91 us (7%)
    all_to_all x4, blocking collectives, exchange(): return lax.all_to_all(x, axis, split_axis=0, concat_axis=0, tiled=False)  63.5 us
    ppermute x3, starting transfers between devices, swap(): return lax.ppermute(x, 'c', [(0, 1), (1, 0)])  15.2 us
    all_to_all x2, starting transfers between devices, exchange(): return lax.all_to_all(x, axis, split_axis=0, concat_axis=0, tiled=False)  9.25 us
    all_to_all x2, waiting for transfers between devices, exchange(): return lax.all_to_all(x, axis, split_axis=0, concat_axis=0, tiled=False)  6.25 us
    ppermute x2, waiting for transfers between devices, across(): return lax.ppermute(x, AXES, pairs)  5.43 us
    ppermute x2, starting transfers between devices, across(): return lax.ppermute(x, AXES, pairs)  5.43 us
    ppermute x1, starting transfers between devices, local(): f_low = lax.ppermute(up, 'zl', [(i, (i + 1) % 3) for i in range(3)])  3.32 us
    ppermute x1, starting transfers between devices, local(): f_high = lax.ppermute(down, 'zl', [(i, (i + 2) % 3) for i in range(3)])  2.86 us
  transfers between devices with their start and end apart: 9, of which 7 were waited for; matrix products, arithmetic and copies ran while one was open for 0% of the time, Pallas kernels for 2%

profile of v6, /device:TPU:1, one launch (start us, length us, event | category | flops | bytes accessed | tf_op | source)
XLA Modules:
  0.0 125.5 jit_solution(6954478413600901944)
XLA Ops:
  0.6 0.9 shard_map.101
  1.6 20.9 %all_to_all.30 = bf16[24,24,128]{2,1,0:T(8,128)(2,1)S(1)} all-to-all(bf16[24,24,128]{2,1,0:T(8,128)(2,1)S(1)} %shard_map.101), channel_id=1, replica_groups=mesh['y'=8,'zh'=4,'x'=4,'zl'=3,'c'=2] {'x','zl','c'}, dimensions={0} | all-to-all | bytes 294912 | tf_op jit(solution)/shard_map/all_to_all | solution.py:232
  22.5 3.0 %collective-permute-start.1 = (bf16[576,128]{1,0:T(8,128)(2,1)S(1)}, bf16[576,128]{1,0:T(8,128)(2,1)S(1)}, u32[]{:S(2)}, u32[]{:S(2)}) collective-permute-start(bf16[576,128]{1,0:T(8,128)(2,1)S(1)} %bitcast.9), channel_id=1, source_target_pairs={{1,2},{3,4},{5,6},{7,8},{9,10},{11,12},{13,14},{15,16},{17,18},{19... | collective-permute-start | bytes 442376 | tf_op jit(solution)/shard_map/ppermute | solution.py:238
  25.5 1.9 %collective-permute-start = (bf16[576,128]{1,0:T(8,128)(2,1)S(1)}, bf16[576,128]{1,0:T(8,128)(2,1)S(1)}, u32[]{:S(2)}, u32[]{:S(2)}) collective-permute-start(bf16[576,128]{1,0:T(8,128)(2,1)S(1)} %bitcast.10), channel_id=1, source_target_pairs={{0,1},{1,0},{2,3},{3,2},{4,5},{5,4},{6,7},{7,6},{8,9},{9,8},{10,11... | collective-permute-start | bytes 442376 | tf_op jit(solution)/shard_map/ppermute | solution.py:241
  27.4 1.4 %shard_map.102 = (bf16[128,384]{1,0:T(8,128)(2,1)S(1)}, bf16[576,512]{1,0:T(8,128)(2,1)S(1)}, bf16[576,512]{1,0:T(8,128)(2,1)S(1)}, f32[1,512]{1,0:T(1,128)S(1)}, bf16[128,512]{1,0:T(8,128)(2,1)S(1)}) custom-call(s32[1]{0:T(128)} %bitcast.3.tile, bf16[3072,384]{1,0:T(8,128)(2,1)} %adjacency.1, bf16[576,512]{1,0:T(8,128)(2,1)} %refs_0_.1, ...), custom_call_target="tpu_custom_call" | custom-call | tf_op jit(solution)/shard_map/pallas_call | solution.py:262
  28.8 1.1 collective-permute-done.1.far
  29.9 0.0 collective-permute-done.near
  30.0 1.2 shard_map.103
  31.1 1.9 %collective-permute-start.2 = (bf16[1664,128]{1,0:T(8,128)(2,1)S(1)}, bf16[1664,128]{1,0:T(8,128)(2,1)S(1)}, u32[]{:S(2)}, u32[]{:S(2)}) collective-permute-start(bf16[1664,128]{1,0:T(8,128)(2,1)S(1)} %get-tuple-element.59), channel_id=1, source_target_pairs={{0,1},{1,0},{2,3},{3,2},{4,5},{5,4},{6,7},{7,6},{8,9},{9,8},{10,11... | collective-permute-start | bytes 1277960 | tf_op jit(solution)/shard_map/ppermute | solution.py:241
  33.1 1.7 %collective-permute-done.2.recv = bf16[1664,128]{1,0:T(8,128)(2,1)S(1)} collective-permute-done((bf16[1664,128]{1,0:T(8,128)(2,1)S(1)}, bf16[1664,128]{1,0:T(8,128)(2,1)S(1)}, u32[]{:S(2)}, u32[]{:S(2)}) %collective-permute-start.2) | collective-permute-done | bytes 426016 | tf_op jit(solution)/shard_map/ppermute | solution.py:241
  34.8 1.1 shard_map.104
  35.9 3.6 %all-to-all-start.1 = ((bf16[4,584,128]{2,1,0:T(8,128)(2,1)}), bf16[4,584,128]{2,1,0:T(8,128)(2,1)S(1)}, u32[]{:S(2)}, u32[]{:S(2)}) async-start(bf16[4,584,128]{2,1,0:T(8,128)(2,1)} %get-tuple-element.62), calls=%async_computation.1 | async-start | bytes 1196032 | tf_op jit(solution)/shard_map/all_to_all | solution.py:232
  39.6 2.5 %collective-permute-start.3 = (bf16[576,128]{1,0:T(8,128)(2,1)S(1)}, bf16[576,128]{1,0:T(8,128)(2,1)S(1)}, u32[]{:S(2)}, u32[]{:S(2)}) collective-permute-start(bf16[576,128]{1,0:T(8,128)(2,1)S(1)} %get-tuple-element.63.own), channel_id=1, source_target_pairs={{1,2},{3,4},{5,6},{7,8},{9,10},{11,12},{13,14},{15,16},{17,18},{19... | collective-permute-start | bytes 442376 | tf_op jit(solution)/shard_map/ppermute | solution.py:238
  42.0 4.3 %collective-permute-done.3.far = bf16[576,128]{1,0:T(8,128)(2,1)S(1)} collective-permute-done((bf16[576,128]{1,0:T(8,128)(2,1)S(1)}, bf16[576,128]{1,0:T(8,128)(2,1)S(1)}, u32[]{:S(2)}, u32[]{:S(2)}) %collective-permute-start.3) | collective-permute-done | bytes 147488 | tf_op jit(solution)/shard_map/ppermute | solution.py:238
  46.3 3.0 %all-to-all-done.1.recv = bf16[4,584,128]{2,1,0:T(8,128)(2,1)S(1)} async-done(((bf16[4,584,128]{2,1,0:T(8,128)(2,1)}), bf16[4,584,128]{2,1,0:T(8,128)(2,1)S(1)}, u32[]{:S(2)}, u32[]{:S(2)}) %all-to-all-start.1) | async-done | bytes 598048 | tf_op jit(solution)/shard_map/all_to_all | solution.py:232
  49.4 0.3 shard_map.105
  49.7 0.1 shard_map.106
  49.8 21.3 %all_to_all.31.recv = bf16[8,80,128]{2,1,0:T(8,128)(2,1)S(1)} all-to-all(bf16[8,80,128]{2,1,0:T(8,128)(2,1)S(1)} %shard_map.106), channel_id=1, replica_groups=mesh['y'=8,'zh'=4,'x'=4,'zl'=3,'c'=2] {'y'}, dimensions={0} | all-to-all | bytes 327680 | tf_op jit(solution)/shard_map/all_to_all | solution.py:232
  71.0 0.7 shard_map.107
  71.8 5.6 %all-to-all-start.3 = ((bf16[12,80,128]{2,1,0:T(8,128)(2,1)}), bf16[12,80,128]{2,1,0:T(8,128)(2,1)S(1)}, u32[]{:S(2)}, u32[]{:S(2)}) async-start(bf16[12,80,128]{2,1,0:T(8,128)(2,1)} %shard_map.107), calls=%async_computation.3 | async-start | bytes 491520 | tf_op jit(solution)/shard_map/all_to_all | solution.py:232
  77.4 3.3 %collective-permute-start.4 = (bf16[4,48,128]{2,1,0:T(8,128)(2,1)S(1)}, bf16[4,48,128]{2,1,0:T(8,128)(2,1)S(1)}, u32[]{:S(2)}, u32[]{:S(2)}) collective-permute-start(bf16[4,48,128]{2,1,0:T(8,128)(2,1)S(1)} %get-tuple-element.71), channel_id=1, source_target_pairs={{0,2},{2,4},{4,0},{1,3},{3,5},{5,1},{6,8},{8,10},{10,6},{7,9},{9,1... | collective-permute-start | bytes 147464 | tf_op jit(solution)/shard_map/ppermute | solution.py:299
  80.7 2.9 %collective-permute-start.5 = (bf16[4,48,128]{2,1,0:T(8,128)(2,1)S(1)}, bf16[4,48,128]{2,1,0:T(8,128)(2,1)S(1)}, u32[]{:S(2)}, u32[]{:S(2)}) collective-permute-start(bf16[4,48,128]{2,1,0:T(8,128)(2,1)S(1)} %get-tuple-element.72), channel_id=1, source_target_pairs={{0,4},{2,0},{4,2},{1,5},{3,1},{5,3},{6,10},{8,6},{10,8},{7,11},{9,... | collective-permute-start | bytes 147464 | tf_op jit(solution)/shard_map/ppermute | solution.py:300
  83.6 0.0 collective-permute-done.4.low
  83.6 2.3 %collective-permute-done.5.high = bf16[4,48,128]{2,1,0:T(8,128)(2,1)S(1)} collective-permute-done((bf16[4,48,128]{2,1,0:T(8,128)(2,1)S(1)}, bf16[4,48,128]{2,1,0:T(8,128)(2,1)S(1)}, u32[]{:S(2)}, u32[]{:S(2)}) %collective-permute-start.5) | collective-permute-done | bytes 49184 | tf_op jit(solution)/shard_map/ppermute | solution.py:300
  85.9 3.2 %all-to-all-done.3.refs_0_ = bf16[12,80,128]{2,1,0:T(8,128)(2,1)S(1)} async-done(((bf16[12,80,128]{2,1,0:T(8,128)(2,1)}), bf16[12,80,128]{2,1,0:T(8,128)(2,1)S(1)}, u32[]{:S(2)}, u32[]{:S(2)}) %all-to-all-start.3) | async-done | bytes 245792 | tf_op jit(solution)/shard_map/all_to_all | solution.py:232
  89.1 0.6 shard_map.108
  89.7 10.5 %all_to_all.32 = bf16[8,72,128]{2,1,0:T(8,128)(2,1)S(1)} all-to-all(bf16[8,72,128]{2,1,0:T(8,128)(2,1)S(1)} %get-tuple-element.74), channel_id=1, replica_groups=mesh['y'=8,'zh'=4,'x'=4,'zl'=3,'c'=2] {'y'}, dimensions={0} | all-to-all | bytes 294912 | tf_op jit(solution)/shard_map/all_to_all | solution.py:232
  100.2 0.1 shard_map.109
  100.3 10.8 %all_to_all.33.block = bf16[4,720,128]{2,1,0:T(8,128)(2,1)S(1)} all-to-all(bf16[4,720,128]{2,1,0:T(8,128)(2,1)S(1)} %shard_map.109), channel_id=1, replica_groups=mesh['y'=8,'zh'=4,'x'=4,'zl'=3,'c'=2] {'x'}, dimensions={0} | all-to-all | bytes 1474560 | tf_op jit(solution)/shard_map/all_to_all | solution.py:232
  111.1 11.4 %collective-permute-start.6 = (bf16[4,720,128]{2,1,0:T(8,128)(2,1)S(1)}, bf16[4,720,128]{2,1,0:T(8,128)(2,1)S(1)}, u32[]{:S(2)}, u32[]{:S(2)}) collective-permute-start(bf16[4,720,128]{2,1,0:T(8,128)(2,1)S(1)} %all_to_all.33.block), channel_id=1, source_target_pairs={{0,1},{1,0},{2,3},{3,2},{4,5},{5,4},{6,7},{7,6},{8,9},{9,8},{10,11... | collective-permute-start | bytes 2211848 | tf_op jit(solution)/shard_map/ppermute | solution.py:241
  122.5 1.2 shard_map.110
  123.7 0.6 collective-permute-done.6.block
  124.3 1.2 shard_map.111
Async XLA Ops:
  22.5 7.5 %collective-permute-start.1 = (bf16[576,128]{1,0:T(8,128)(2,1)S(1)}, bf16[576,128]{1,0:T(8,128)(2,1)S(1)}, u32[]{:S(2)}, u32[]{:S(2)}) collective-permute-start(bf16[576,128]{1,0:T(8,128)(2,1)S(1)} %bitcast.9), channel_id=1, source_target_pairs={{1,2},{3,4},{5,6},{7,8},{9,10},{11,12},{13,14},{15,16},{17,18},{19... | collective-permute-start | bytes 442376 | tf_op jit(solution)/shard_map/ppermute | solution.py:238
  25.5 4.5 %collective-permute-start = (bf16[576,128]{1,0:T(8,128)(2,1)S(1)}, bf16[576,128]{1,0:T(8,128)(2,1)S(1)}, u32[]{:S(2)}, u32[]{:S(2)}) collective-permute-start(bf16[576,128]{1,0:T(8,128)(2,1)S(1)} %bitcast.10), channel_id=1, source_target_pairs={{0,1},{1,0},{2,3},{3,2},{4,5},{5,4},{6,7},{7,6},{8,9},{9,8},{10,11... | collective-permute-start | bytes 442376 | tf_op jit(solution)/shard_map/ppermute | solution.py:241
  31.1 3.7 %collective-permute-start.2 = (bf16[1664,128]{1,0:T(8,128)(2,1)S(1)}, bf16[1664,128]{1,0:T(8,128)(2,1)S(1)}, u32[]{:S(2)}, u32[]{:S(2)}) collective-permute-start(bf16[1664,128]{1,0:T(8,128)(2,1)S(1)} %get-tuple-element.59), channel_id=1, source_target_pairs={{0,1},{1,0},{2,3},{3,2},{4,5},{5,4},{6,7},{7,6},{8,9},{9,8},{10,11... | collective-permute-start | bytes 1277960 | tf_op jit(solution)/shard_map/ppermute | solution.py:241
  35.9 13.4 %all-to-all-start.1 = ((bf16[4,584,128]{2,1,0:T(8,128)(2,1)}), bf16[4,584,128]{2,1,0:T(8,128)(2,1)S(1)}, u32[]{:S(2)}, u32[]{:S(2)}) async-start(bf16[4,584,128]{2,1,0:T(8,128)(2,1)} %get-tuple-element.62), calls=%async_computation.1 | async-start | bytes 1196032 | tf_op jit(solution)/shard_map/all_to_all | solution.py:232
  39.6 6.7 %collective-permute-start.3 = (bf16[576,128]{1,0:T(8,128)(2,1)S(1)}, bf16[576,128]{1,0:T(8,128)(2,1)S(1)}, u32[]{:S(2)}, u32[]{:S(2)}) collective-permute-start(bf16[576,128]{1,0:T(8,128)(2,1)S(1)} %get-tuple-element.63.own), channel_id=1, source_target_pairs={{1,2},{3,4},{5,6},{7,8},{9,10},{11,12},{13,14},{15,16},{17,18},{19... | collective-permute-start | bytes 442376 | tf_op jit(solution)/shard_map/ppermute | solution.py:238
  71.8 17.3 %all-to-all-start.3 = ((bf16[12,80,128]{2,1,0:T(8,128)(2,1)}), bf16[12,80,128]{2,1,0:T(8,128)(2,1)S(1)}, u32[]{:S(2)}, u32[]{:S(2)}) async-start(bf16[12,80,128]{2,1,0:T(8,128)(2,1)} %shard_map.107), calls=%async_computation.3 | async-start | bytes 491520 | tf_op jit(solution)/shard_map/all_to_all | solution.py:232
  77.4 6.2 %collective-permute-start.4 = (bf16[4,48,128]{2,1,0:T(8,128)(2,1)S(1)}, bf16[4,48,128]{2,1,0:T(8,128)(2,1)S(1)}, u32[]{:S(2)}, u32[]{:S(2)}) collective-permute-start(bf16[4,48,128]{2,1,0:T(8,128)(2,1)S(1)} %get-tuple-element.71), channel_id=1, source_target_pairs={{0,2},{2,4},{4,0},{1,3},{3,5},{5,1},{6,8},{8,10},{10,6},{7,9},{9,1... | collective-permute-start | bytes 147464 | tf_op jit(solution)/shard_map/ppermute | solution.py:299
  80.7 5.2 %collective-permute-start.5 = (bf16[4,48,128]{2,1,0:T(8,128)(2,1)S(1)}, bf16[4,48,128]{2,1,0:T(8,128)(2,1)S(1)}, u32[]{:S(2)}, u32[]{:S(2)}) collective-permute-start(bf16[4,48,128]{2,1,0:T(8,128)(2,1)S(1)} %get-tuple-element.72), channel_id=1, source_target_pairs={{0,4},{2,0},{4,2},{1,5},{3,1},{5,3},{6,10},{8,6},{10,8},{7,11},{9,... | collective-permute-start | bytes 147464 | tf_op jit(solution)/shard_map/ppermute | solution.py:300
  111.1 13.2 %collective-permute-start.6 = (bf16[4,720,128]{2,1,0:T(8,128)(2,1)S(1)}, bf16[4,720,128]{2,1,0:T(8,128)(2,1)S(1)}, u32[]{:S(2)}, u32[]{:S(2)}) collective-permute-start(bf16[4,720,128]{2,1,0:T(8,128)(2,1)S(1)} %all_to_all.33.block), channel_id=1, source_target_pairs={{0,1},{1,0},{2,3},{3,2},{4,5},{5,4},{6,7},{7,6},{8,9},{9,8},{10,11... | collective-permute-start | bytes 2211848 | tf_op jit(solution)/shard_map/ppermute | solution.py:241

commit v7 on v6

--- a/solution.py
+++ b/solution.py
@@ -12,6 +12,7 @@
 SIZES = (8, 4, 4, 3, 2)
 GRAPH = ("y", "zh")
 FEAT = ("x", "zl", "c")
+PLANE = ("y", "x")
 LINE = ("zh", "zl")
 N_X = 4
 N_Y = 8
@@ -113,8 +114,10 @@
     sums = jnp.sum(g.astype(F32), axis=0, keepdims=True)
     parts = [sums[:, lanes(b)] for b in range(N_X)]
     tail = jnp.concatenate(parts + [jnp.zeros((TAIL - N_X, TILE), F32)], axis=0)
-    for b in range(N_X):
-        out[b] = jnp.concatenate([total[:, lanes(b)], tail], axis=0).astype(BF16)
+    for y in range(N_Y):
+        for x in range(N_X):
+            piece = total[y * ROWS : (y + 1) * ROWS, lanes(x)]
+            out[y * N_X + x] = jnp.concatenate([piece, tail], axis=0).astype(BF16)
 
 
 def summed(recv):
@@ -124,14 +127,7 @@
     return total
 
 
-def x_kernel(recv, out):
-    total = summed(recv)
-    tail = total[N_Y * ROWS :]
-    for d in range(N_Y):
-        out[d] = jnp.concatenate([total[d * ROWS : (d + 1) * ROWS], tail], axis=0).astype(BF16)
-
-
-def y_kernel(recv, out):
+def plane_kernel(recv, out):
     rounded = summed(recv).astype(BF16)
     for d in range(N_LINE):
         out[d] = rounded
@@ -281,10 +277,9 @@
     recv = swap(send)
     s_far = across(scaled)
     partial, act = call(
-        partial_kernel, [VMEM] * 4, (sds((N_X, f_in + TAIL, TILE)), sds((TILE, f_out)))
+        partial_kernel, [VMEM] * 4, (sds((N_Y * N_X, ROWS + TAIL, TILE)), sds((TILE, f_out)))
     )(keep, grad, recv, act)
-    from_x = exchange(partial, "x")
-    from_x, s_far = lax.optimization_barrier((from_x, s_far))
+    from_plane = exchange(partial, PLANE)
     zl = lax.axis_index("zl").astype(jnp.int32).reshape(1)
     pair = sds((N_X, 2 * width, TILE))
     stay, up, down = call(
@@ -293,12 +288,11 @@
         (pair,) * 3,
         [pltpu.VMEM((N_FEAT, width, TILE), F32)],
     )(core, zl, recv, s_far, scaled, adj, back)
-    from_x, stay, up, down = lax.optimization_barrier((from_x, stay, up, down))
-    from_y = exchange(call(x_kernel, [VMEM], sds((N_Y, ROWS + TAIL, TILE)))(from_x), "y")
-    from_line = exchange(call(y_kernel, [VMEM], sds((N_LINE, ROWS + TAIL, TILE)))(from_y), LINE)
     f_low = lax.ppermute(up, "zl", [(i, (i + 1) % 3) for i in range(3)])
     f_high = lax.ppermute(down, "zl", [(i, (i + 2) % 3) for i in range(3)])
-    from_line, f_low, f_high = lax.optimization_barrier((from_line, f_low, f_high))
+    from_plane, f_low, f_high = lax.optimization_barrier((from_plane, f_low, f_high))
+    to_line = call(plane_kernel, [VMEM], sds((N_LINE, ROWS + TAIL, TILE)))(from_plane)
+    from_line = exchange(to_line, LINE)
     to_y, bias_sum = call(
         lambda *refs: line_kernel(scale, *refs),
         [VMEM],

time: 126 us -> 128 us (1.016)
  blocking collectives: 63.5 us -> 65.8 us
  waiting for transfers between devices: 16.3 us -> 15 us
    ppermute x1, starting transfers between devices: 2.86 us -> 5.22 us  [local(): f_high = lax.ppermute(down, 'zl', [(i, (i + 2) % 3) for i in range(3)])]
    all_to_all x4, blocking collectives: 63.5 us -> 65.8 us  [exchange(): return lax.all_to_all(x, axis, split_axis=0, concat_axis=0, tiled=False)]
    all_to_all x2 -> x1, starting transfers between devices: 9.25 us -> 11.2 us  [exchange(): return lax.all_to_all(x, axis, split_axis=0, concat_axis=0, tiled=False)]
    all_to_all x2 -> x1, waiting for transfers between devices: 6.25 us -> 4.68 us  [exchange(): return lax.all_to_all(x, axis, split_axis=0, concat_axis=0, tiled=False)]
    ppermute x1, starting transfers between devices: 3.32 us -> 1.92 us  [local(): f_low = lax.ppermute(up, 'zl', [(i, (i + 1) % 3) for i in range(3)])]
  transfers between devices with their start and end apart: 9 -> 8, of which waited for: 7 -> 6; matrix products, arithmetic and copies ran while one was open for 0% -> 0% of each run, Pallas kernels for 2% -> 2%
where the time goes in v7:
time: 128 us; the launch traced here: 127 us
  blocking collectives  65.8 us (51%)
  starting transfers between devices  37.3 us (29%)
  waiting for transfers between devices  15 us (12%)
  Pallas kernels  8.23 us (6%)
    all_to_all x4, blocking collectives, exchange(): return lax.all_to_all(x, axis, split_axis=0, concat_axis=0, tiled=False)  65.8 us
    ppermute x3, starting transfers between devices, swap(): return lax.ppermute(x, 'c', [(0, 1), (1, 0)])  14.1 us
    all_to_all x1, starting transfers between devices, exchange(): return lax.all_to_all(x, axis, split_axis=0, concat_axis=0, tiled=False)  11.2 us
    ppermute x2, waiting for transfers between devices, across(): return lax.ppermute(x, AXES, pairs)  5.98 us
    ppermute x1, starting transfers between devices, local(): f_high = lax.ppermute(down, 'zl', [(i, (i + 2) % 3) for i in range(3)])  5.22 us
    ppermute x2, starting transfers between devices, across(): return lax.ppermute(x, AXES, pairs)  4.9 us
    all_to_all x1, waiting for transfers between devices, exchange(): return lax.all_to_all(x, axis, split_axis=0, concat_axis=0, tiled=False)  4.68 us
  transfers between devices with their start and end apart: 8, of which 6 were waited for; matrix products, arithmetic and copies ran while one was open for 0% of the time, Pallas kernels for 2%

profile of v7, /device:TPU:1, one launch (start us, length us, event | category | flops | bytes accessed | tf_op | source)
XLA Modules:
  0.0 127.1 jit_solution(13142480743531083372)
XLA Ops:
  0.6 0.9 shard_map.101
  1.6 20.9 %all_to_all.25 = bf16[24,24,128]{2,1,0:T(8,128)(2,1)S(1)} all-to-all(bf16[24,24,128]{2,1,0:T(8,128)(2,1)S(1)} %shard_map.101), channel_id=1, replica_groups=mesh['y'=8,'zh'=4,'x'=4,'zl'=3,'c'=2] {'x','zl','c'}, dimensions={0} | all-to-all | bytes 294912 | tf_op jit(solution)/shard_map/all_to_all | solution.py:228
  22.5 3.0 %collective-permute-start.1 = (bf16[576,128]{1,0:T(8,128)(2,1)S(1)}, bf16[576,128]{1,0:T(8,128)(2,1)S(1)}, u32[]{:S(2)}, u32[]{:S(2)}) collective-permute-start(bf16[576,128]{1,0:T(8,128)(2,1)S(1)} %bitcast.9), channel_id=1, source_target_pairs={{1,2},{3,4},{5,6},{7,8},{9,10},{11,12},{13,14},{15,16},{17,18},{19... | collective-permute-start | bytes 442376 | tf_op jit(solution)/shard_map/ppermute | solution.py:234
  25.5 1.9 %collective-permute-start = (bf16[576,128]{1,0:T(8,128)(2,1)S(1)}, bf16[576,128]{1,0:T(8,128)(2,1)S(1)}, u32[]{:S(2)}, u32[]{:S(2)}) collective-permute-start(bf16[576,128]{1,0:T(8,128)(2,1)S(1)} %bitcast.10), channel_id=1, source_target_pairs={{0,1},{1,0},{2,3},{3,2},{4,5},{5,4},{6,7},{7,6},{8,9},{9,8},{10,11... | collective-permute-start | bytes 442376 | tf_op jit(solution)/shard_map/ppermute | solution.py:237
  27.4 1.4 %shard_map.102 = (bf16[128,384]{1,0:T(8,128)(2,1)S(1)}, bf16[576,512]{1,0:T(8,128)(2,1)S(1)}, bf16[576,512]{1,0:T(8,128)(2,1)S(1)}, f32[1,512]{1,0:T(1,128)S(1)}, bf16[128,512]{1,0:T(8,128)(2,1)S(1)}) custom-call(s32[1]{0:T(128)} %bitcast.3.tile, bf16[3072,384]{1,0:T(8,128)(2,1)} %adjacency.1, bf16[576,512]{1,0:T(8,128)(2,1)} %refs_0_.1, ...), custom_call_target="tpu_custom_call" | custom-call | tf_op jit(solution)/shard_map/pallas_call | solution.py:258
  28.8 1.1 collective-permute-done.1.far
  29.9 0.0 collective-permute-done.near
  30.0 1.2 shard_map.103
  31.1 1.9 %collective-permute-start.2 = (bf16[1664,128]{1,0:T(8,128)(2,1)S(1)}, bf16[1664,128]{1,0:T(8,128)(2,1)S(1)}, u32[]{:S(2)}, u32[]{:S(2)}) collective-permute-start(bf16[1664,128]{1,0:T(8,128)(2,1)S(1)} %get-tuple-element.53), channel_id=1, source_target_pairs={{0,1},{1,0},{2,3},{3,2},{4,5},{5,4},{6,7},{7,6},{8,9},{9,8},{10,11... | collective-permute-start | bytes 1277960 | tf_op jit(solution)/shard_map/ppermute | solution.py:237
  33.1 1.7 %collective-permute-done.2.recv = bf16[1664,128]{1,0:T(8,128)(2,1)S(1)} collective-permute-done((bf16[1664,128]{1,0:T(8,128)(2,1)S(1)}, bf16[1664,128]{1,0:T(8,128)(2,1)S(1)}, u32[]{:S(2)}, u32[]{:S(2)}) %collective-permute-start.2) | collective-permute-done | bytes 426016 | tf_op jit(solution)/shard_map/ppermute | solution.py:237
  34.8 1.2 shard_map.104
  36.0 11.2 %all-to-all-start.1 = ((bf16[32,80,128]{2,1,0:T(8,128)(2,1)}), bf16[32,80,128]{2,1,0:T(8,128)(2,1)S(1)}, u32[]{:S(2)}, u32[]{:S(2)}) async-start(bf16[32,80,128]{2,1,0:T(8,128)(2,1)} %get-tuple-element.56), calls=%async_computation.1 | async-start | bytes 1310720 | tf_op jit(solution)/shard_map/all_to_all | solution.py:228
  47.1 1.9 %collective-permute-start.3 = (bf16[576,128]{1,0:T(8,128)(2,1)S(1)}, bf16[576,128]{1,0:T(8,128)(2,1)S(1)}, u32[]{:S(2)}, u32[]{:S(2)}) collective-permute-start(bf16[576,128]{1,0:T(8,128)(2,1)S(1)} %get-tuple-element.57.own), channel_id=1, source_target_pairs={{1,2},{3,4},{5,6},{7,8},{9,10},{11,12},{13,14},{15,16},{17,18},{19... | collective-permute-start | bytes 442376 | tf_op jit(solution)/shard_map/ppermute | solution.py:234
  49.1 4.8 %collective-permute-done.3.far = bf16[576,128]{1,0:T(8,128)(2,1)S(1)} collective-permute-done((bf16[576,128]{1,0:T(8,128)(2,1)S(1)}, bf16[576,128]{1,0:T(8,128)(2,1)S(1)}, u32[]{:S(2)}, u32[]{:S(2)}) %collective-permute-start.3) | collective-permute-done | bytes 147488 | tf_op jit(solution)/shard_map/ppermute | solution.py:234
  53.9 0.3 shard_map.105
  54.2 1.9 %collective-permute-start.4 = (bf16[4,48,128]{2,1,0:T(8,128)(2,1)S(1)}, bf16[4,48,128]{2,1,0:T(8,128)(2,1)S(1)}, u32[]{:S(2)}, u32[]{:S(2)}) collective-permute-start(bf16[4,48,128]{2,1,0:T(8,128)(2,1)S(1)} %get-tuple-element.59), channel_id=1, source_target_pairs={{0,2},{2,4},{4,0},{1,3},{3,5},{5,1},{6,8},{8,10},{10,6},{7,9},{9,1... | collective-permute-start | bytes 147464 | tf_op jit(solution)/shard_map/ppermute | solution.py:291
  56.1 5.2 %collective-permute-start.5 = (bf16[4,48,128]{2,1,0:T(8,128)(2,1)S(1)}, bf16[4,48,128]{2,1,0:T(8,128)(2,1)S(1)}, u32[]{:S(2)}, u32[]{:S(2)}) collective-permute-start(bf16[4,48,128]{2,1,0:T(8,128)(2,1)S(1)} %get-tuple-element.60), channel_id=1, source_target_pairs={{0,4},{2,0},{4,2},{1,5},{3,1},{5,3},{6,10},{8,6},{10,8},{7,11},{9,... | collective-permute-start | bytes 147464 | tf_op jit(solution)/shard_map/ppermute | solution.py:292
  61.3 0.0 collective-permute-done.4.low
  61.4 2.0 %collective-permute-done.5.high = bf16[4,48,128]{2,1,0:T(8,128)(2,1)S(1)} collective-permute-done((bf16[4,48,128]{2,1,0:T(8,128)(2,1)S(1)}, bf16[4,48,128]{2,1,0:T(8,128)(2,1)S(1)}, u32[]{:S(2)}, u32[]{:S(2)}) %collective-permute-start.5) | collective-permute-done | bytes 49184 | tf_op jit(solution)/shard_map/ppermute | solution.py:292
  63.4 4.7 %all-to-all-done.1.recv = bf16[32,80,128]{2,1,0:T(8,128)(2,1)S(1)} async-done(((bf16[32,80,128]{2,1,0:T(8,128)(2,1)}), bf16[32,80,128]{2,1,0:T(8,128)(2,1)S(1)}, u32[]{:S(2)}, u32[]{:S(2)}) %all-to-all-start.1) | async-done | bytes 655392 | tf_op jit(solution)/shard_map/all_to_all | solution.py:228
  68.1 0.1 shard_map.106
  68.2 19.4 %all_to_all.26.refs_0_ = bf16[12,80,128]{2,1,0:T(8,128)(2,1)S(1)} all-to-all(bf16[12,80,128]{2,1,0:T(8,128)(2,1)S(1)} %shard_map.106), channel_id=1, replica_groups=mesh['y'=8,'zh'=4,'x'=4,'zl'=3,'c'=2] {'zh','zl'}, dimensions={0} | all-to-all | bytes 491520 | tf_op jit(solution)/shard_map/all_to_all | solution.py:228
  87.6 0.6 shard_map.107
  88.2 14.3 %all_to_all.27 = bf16[8,72,128]{2,1,0:T(8,128)(2,1)S(1)} all-to-all(bf16[8,72,128]{2,1,0:T(8,128)(2,1)S(1)} %get-tuple-element.62), channel_id=1, replica_groups=mesh['y'=8,'zh'=4,'x'=4,'zl'=3,'c'=2] {'y'}, dimensions={0} | all-to-all | bytes 294912 | tf_op jit(solution)/shard_map/all_to_all | solution.py:228
  102.4 0.1 shard_map.108
  102.5 11.2 %all_to_all.28.block = bf16[4,720,128]{2,1,0:T(8,128)(2,1)S(1)} all-to-all(bf16[4,720,128]{2,1,0:T(8,128)(2,1)S(1)} %shard_map.108), channel_id=1, replica_groups=mesh['y'=8,'zh'=4,'x'=4,'zl'=3,'c'=2] {'x'}, dimensions={0} | all-to-all | bytes 1474560 | tf_op jit(solution)/shard_map/all_to_all | solution.py:228
  113.8 10.3 %collective-permute-start.6 = (bf16[4,720,128]{2,1,0:T(8,128)(2,1)S(1)}, bf16[4,720,128]{2,1,0:T(8,128)(2,1)S(1)}, u32[]{:S(2)}, u32[]{:S(2)}) collective-permute-start(bf16[4,720,128]{2,1,0:T(8,128)(2,1)S(1)} %all_to_all.28.block), channel_id=1, source_target_pairs={{0,1},{1,0},{2,3},{3,2},{4,5},{5,4},{6,7},{7,6},{8,9},{9,8},{10,11... | collective-permute-start | bytes 2211848 | tf_op jit(solution)/shard_map/ppermute | solution.py:237
  124.0 1.2 shard_map.109
  125.3 0.6 collective-permute-done.6.block
  125.9 1.2 shard_map.110
Async XLA Ops:
  22.5 7.5 %collective-permute-start.1 = (bf16[576,128]{1,0:T(8,128)(2,1)S(1)}, bf16[576,128]{1,0:T(8,128)(2,1)S(1)}, u32[]{:S(2)}, u32[]{:S(2)}) collective-permute-start(bf16[576,128]{1,0:T(8,128)(2,1)S(1)} %bitcast.9), channel_id=1, source_target_pairs={{1,2},{3,4},{5,6},{7,8},{9,10},{11,12},{13,14},{15,16},{17,18},{19... | collective-permute-start | bytes 442376 | tf_op jit(solution)/shard_map/ppermute | solution.py:234
  25.5 4.5 %collective-permute-start = (bf16[576,128]{1,0:T(8,128)(2,1)S(1)}, bf16[576,128]{1,0:T(8,128)(2,1)S(1)}, u32[]{:S(2)}, u32[]{:S(2)}) collective-permute-start(bf16[576,128]{1,0:T(8,128)(2,1)S(1)} %bitcast.10), channel_id=1, source_target_pairs={{0,1},{1,0},{2,3},{3,2},{4,5},{5,4},{6,7},{7,6},{8,9},{9,8},{10,11... | collective-permute-start | bytes 442376 | tf_op jit(solution)/shard_map/ppermute | solution.py:237
  31.1 3.7 %collective-permute-start.2 = (bf16[1664,128]{1,0:T(8,128)(2,1)S(1)}, bf16[1664,128]{1,0:T(8,128)(2,1)S(1)}, u32[]{:S(2)}, u32[]{:S(2)}) collective-permute-start(bf16[1664,128]{1,0:T(8,128)(2,1)S(1)} %get-tuple-element.53), channel_id=1, source_target_pairs={{0,1},{1,0},{2,3},{3,2},{4,5},{5,4},{6,7},{7,6},{8,9},{9,8},{10,11... | collective-permute-start | bytes 1277960 | tf_op jit(solution)/shard_map/ppermute | solution.py:237
  36.0 32.1 %all-to-all-start.1 = ((bf16[32,80,128]{2,1,0:T(8,128)(2,1)}), bf16[32,80,128]{2,1,0:T(8,128)(2,1)S(1)}, u32[]{:S(2)}, u32[]{:S(2)}) async-start(bf16[32,80,128]{2,1,0:T(8,128)(2,1)} %get-tuple-element.56), calls=%async_computation.1 | async-start | bytes 1310720 | tf_op jit(solution)/shard_map/all_to_all | solution.py:228
  47.1 6.8 %collective-permute-start.3 = (bf16[576,128]{1,0:T(8,128)(2,1)S(1)}, bf16[576,128]{1,0:T(8,128)(2,1)S(1)}, u32[]{:S(2)}, u32[]{:S(2)}) collective-permute-start(bf16[576,128]{1,0:T(8,128)(2,1)S(1)} %get-tuple-element.57.own), channel_id=1, source_target_pairs={{1,2},{3,4},{5,6},{7,8},{9,10},{11,12},{13,14},{15,16},{17,18},{19... | collective-permute-start | bytes 442376 | tf_op jit(solution)/shard_map/ppermute | solution.py:234
  54.2 7.2 %collective-permute-start.4 = (bf16[4,48,128]{2,1,0:T(8,128)(2,1)S(1)}, bf16[4,48,128]{2,1,0:T(8,128)(2,1)S(1)}, u32[]{:S(2)}, u32[]{:S(2)}) collective-permute-start(bf16[4,48,128]{2,1,0:T(8,128)(2,1)S(1)} %get-tuple-element.59), channel_id=1, source_target_pairs={{0,2},{2,4},{4,0},{1,3},{3,5},{5,1},{6,8},{8,10},{10,6},{7,9},{9,1... | collective-permute-start | bytes 147464 | tf_op jit(solution)/shard_map/ppermute | solution.py:291
  56.1 7.3 %collective-permute-start.5 = (bf16[4,48,128]{2,1,0:T(8,128)(2,1)S(1)}, bf16[4,48,128]{2,1,0:T(8,128)(2,1)S(1)}, u32[]{:S(2)}, u32[]{:S(2)}) collective-permute-start(bf16[4,48,128]{2,1,0:T(8,128)(2,1)S(1)} %get-tuple-element.60), channel_id=1, source_target_pairs={{0,4},{2,0},{4,2},{1,5},{3,1},{5,3},{6,10},{8,6},{10,8},{7,11},{9,... | collective-permute-start | bytes 147464 | tf_op jit(solution)/shard_map/ppermute | solution.py:292
  113.8 12.1 %collective-permute-start.6 = (bf16[4,720,128]{2,1,0:T(8,128)(2,1)S(1)}, bf16[4,720,128]{2,1,0:T(8,128)(2,1)S(1)}, u32[]{:S(2)}, u32[]{:S(2)}) collective-permute-start(bf16[4,720,128]{2,1,0:T(8,128)(2,1)S(1)} %all_to_all.28.block), channel_id=1, source_target_pairs={{0,1},{1,0},{2,3},{3,2},{4,5},{5,4},{6,7},{7,6},{8,9},{9,8},{10,11... | collective-permute-start | bytes 2211848 | tf_op jit(solution)/shard_map/ppermute | solution.py:237

commit v8 on v6

--- a/solution.py
+++ b/solution.py
@@ -104,8 +104,7 @@
     send[576 + 4 * TILE :] = scale
 
 
-def partial_kernel(keep, grad, recv, act, out, act_out):
-    act_out[...] = act[...]
+def partial_kernel(keep, grad, recv, out):
     f_in = keep.shape[0]
     rows = [recv[f_in + b * TILE : f_in + (b + 1) * TILE] for b in range(N_X)]
     g = jnp.concatenate([grad[...], jnp.concatenate(rows, axis=1)], axis=0)
@@ -124,7 +123,8 @@
     return total
 
 
-def x_kernel(recv, out):
+def x_kernel(recv, act, out, act_out):
+    act_out[...] = act[...]
     total = summed(recv)
     tail = total[N_Y * ROWS :]
     for d in range(N_Y):
@@ -280,11 +280,14 @@
     )(core, near, far, own, *held)
     recv = swap(send)
     s_far = across(scaled)
-    partial, act = call(
-        partial_kernel, [VMEM] * 4, (sds((N_X, f_in + TAIL, TILE)), sds((TILE, f_out)))
-    )(keep, grad, recv, act)
+    partial = call(partial_kernel, [VMEM] * 3, sds((N_X, f_in + TAIL, TILE)))(keep, grad, recv)
     from_x = exchange(partial, "x")
-    from_x, s_far = lax.optimization_barrier((from_x, s_far))
+    to_y, act = call(
+        x_kernel, [VMEM] * 2, (sds((N_Y, ROWS + TAIL, TILE)), sds((TILE, f_out)))
+    )(from_x, act)
+    from_y = exchange(to_y, "y")
+    from_y, s_far = lax.optimization_barrier((from_y, s_far))
+    from_line = exchange(call(y_kernel, [VMEM], sds((N_LINE, ROWS + TAIL, TILE)))(from_y), LINE)
     zl = lax.axis_index("zl").astype(jnp.int32).reshape(1)
     pair = sds((N_X, 2 * width, TILE))
     stay, up, down = call(
@@ -293,9 +296,6 @@
         (pair,) * 3,
         [pltpu.VMEM((N_FEAT, width, TILE), F32)],
     )(core, zl, recv, s_far, scaled, adj, back)
-    from_x, stay, up, down = lax.optimization_barrier((from_x, stay, up, down))
-    from_y = exchange(call(x_kernel, [VMEM], sds((N_Y, ROWS + TAIL, TILE)))(from_x), "y")
-    from_line = exchange(call(y_kernel, [VMEM], sds((N_LINE, ROWS + TAIL, TILE)))(from_y), LINE)
     f_low = lax.ppermute(up, "zl", [(i, (i + 1) % 3) for i in range(3)])
     f_high = lax.ppermute(down, "zl", [(i, (i + 2) % 3) for i in range(3)])
     from_line, f_low, f_high = lax.optimization_barrier((from_line, f_low, f_high))

time: 126 us -> 129 us (1.024)
  starting transfers between devices: 36.1 us -> 44.8 us
  blocking collectives: 63.5 us -> 59.3 us
  waiting for transfers between devices: 16.3 us -> 14.8 us
    all_to_all x2, starting transfers between devices: 9.25 us -> 18.4 us  [exchange(): return lax.all_to_all(x, axis, split_axis=0, concat_axis=0, tiled=False)]
    all_to_all x2, waiting for transfers between devices: 6.25 us -> 0.47 us  [exchange(): return lax.all_to_all(x, axis, split_axis=0, concat_axis=0, tiled=False)]
    all_to_all x4, blocking collectives: 63.5 us -> 59.3 us  [exchange(): return lax.all_to_all(x, axis, split_axis=0, concat_axis=0, tiled=False)]
    ppermute x1, waiting for transfers between devices: 2.29 us -> 4.76 us  [local(): f_high = lax.ppermute(down, 'zl', [(i, (i + 2) % 3) for i in range(3)])]
    ppermute x2, waiting for transfers between devices: 5.43 us -> 7.26 us  [across(): return lax.ppermute(x, AXES, pairs)]
  transfers between devices with their start and end apart: 9 -> 9, of which waited for: 7 -> 6; matrix products, arithmetic and copies ran while one was open for 0% -> 0% of each run, Pallas kernels for 2% -> 2%
where the time goes in v8:
time: 129 us; the launch traced here: 128 us
  blocking collectives  59.3 us (46%)
  starting transfers between devices  44.8 us (35%)
  waiting for transfers between devices  14.8 us (11%)
  Pallas kernels  8.76 us (7%)
    all_to_all x4, blocking collectives, exchange(): return lax.all_to_all(x, axis, split_axis=0, concat_axis=0, tiled=False)  59.3 us
    all_to_all x2, starting transfers between devices, exchange(): return lax.all_to_all(x, axis, split_axis=0, concat_axis=0, tiled=False)  18.4 us
    ppermute x3, starting transfers between devices, swap(): return lax.ppermute(x, 'c', [(0, 1), (1, 0)])  15.3 us
    ppermute x2, waiting for transfers between devices, across(): return lax.ppermute(x, AXES, pairs)  7.26 us
    ppermute x2, starting transfers between devices, across(): return lax.ppermute(x, AXES, pairs)  4.88 us
    ppermute x1, waiting for transfers between devices, local(): f_high = lax.ppermute(down, 'zl', [(i, (i + 2) % 3) for i in range(3)])  4.76 us
    ppermute x1, starting transfers between devices, local(): f_low = lax.ppermute(up, 'zl', [(i, (i + 1) % 3) for i in range(3)])  3.33 us
    ppermute x1, starting transfers between devices, local(): f_high = lax.ppermute(down, 'zl', [(i, (i + 2) % 3) for i in range(3)])  2.86 us
  transfers between devices with their start and end apart: 9, of which 6 were waited for; matrix products, arithmetic and copies ran while one was open for 0% of the time, Pallas kernels for 2%

profile of v8, /device:TPU:1, one launch (start us, length us, event | category | flops | bytes accessed | tf_op | source)
XLA Modules:
  0.0 128.4 jit_solution(7395531307559458186)
XLA Ops:
  0.6 0.9 shard_map.101
  1.6 20.9 %all_to_all.30 = bf16[24,24,128]{2,1,0:T(8,128)(2,1)S(1)} all-to-all(bf16[24,24,128]{2,1,0:T(8,128)(2,1)S(1)} %shard_map.101), channel_id=1, replica_groups=mesh['y'=8,'zh'=4,'x'=4,'zl'=3,'c'=2] {'x','zl','c'}, dimensions={0} | all-to-all | bytes 294912 | tf_op jit(solution)/shard_map/all_to_all | solution.py:232
  22.5 3.0 %collective-permute-start.1 = (bf16[576,128]{1,0:T(8,128)(2,1)S(1)}, bf16[576,128]{1,0:T(8,128)(2,1)S(1)}, u32[]{:S(2)}, u32[]{:S(2)}) collective-permute-start(bf16[576,128]{1,0:T(8,128)(2,1)S(1)} %bitcast.9), channel_id=1, source_target_pairs={{1,2},{3,4},{5,6},{7,8},{9,10},{11,12},{13,14},{15,16},{17,18},{19... | collective-permute-start | bytes 442376 | tf_op jit(solution)/shard_map/ppermute | solution.py:238
  25.5 1.9 %collective-permute-start = (bf16[576,128]{1,0:T(8,128)(2,1)S(1)}, bf16[576,128]{1,0:T(8,128)(2,1)S(1)}, u32[]{:S(2)}, u32[]{:S(2)}) collective-permute-start(bf16[576,128]{1,0:T(8,128)(2,1)S(1)} %bitcast.10), channel_id=1, source_target_pairs={{0,1},{1,0},{2,3},{3,2},{4,5},{5,4},{6,7},{7,6},{8,9},{9,8},{10,11... | collective-permute-start | bytes 442376 | tf_op jit(solution)/shard_map/ppermute | solution.py:241
  27.4 1.4 %shard_map.102 = (bf16[128,384]{1,0:T(8,128)(2,1)S(1)}, bf16[576,512]{1,0:T(8,128)(2,1)S(1)}, bf16[576,512]{1,0:T(8,128)(2,1)S(1)}, f32[1,512]{1,0:T(1,128)S(1)}, bf16[128,512]{1,0:T(8,128)(2,1)S(1)}) custom-call(s32[1]{0:T(128)} %bitcast.3.tile, bf16[3072,384]{1,0:T(8,128)(2,1)} %adjacency.1, bf16[576,512]{1,0:T(8,128)(2,1)} %refs_0_.1, ...), custom_call_target="tpu_custom_call" | custom-call | tf_op jit(solution)/shard_map/pallas_call | solution.py:262
  28.8 1.1 collective-permute-done.1.far
  29.9 0.0 collective-permute-done.near
  30.0 1.2 shard_map.103
  31.1 1.9 %collective-permute-start.2 = (bf16[1664,128]{1,0:T(8,128)(2,1)S(1)}, bf16[1664,128]{1,0:T(8,128)(2,1)S(1)}, u32[]{:S(2)}, u32[]{:S(2)}) collective-permute-start(bf16[1664,128]{1,0:T(8,128)(2,1)S(1)} %get-tuple-element.55), channel_id=1, source_target_pairs={{0,1},{1,0},{2,3},{3,2},{4,5},{5,4},{6,7},{7,6},{8,9},{9,8},{10,11... | collective-permute-start | bytes 1277960 | tf_op jit(solution)/shard_map/ppermute | solution.py:241
  33.1 1.7 %collective-permute-done.2.recv = bf16[1664,128]{1,0:T(8,128)(2,1)S(1)} collective-permute-done((bf16[1664,128]{1,0:T(8,128)(2,1)S(1)}, bf16[1664,128]{1,0:T(8,128)(2,1)S(1)}, u32[]{:S(2)}, u32[]{:S(2)}) %collective-permute-start.2) | collective-permute-done | bytes 426016 | tf_op jit(solution)/shard_map/ppermute | solution.py:241
  34.8 0.3 shard_map.104
  35.1 13.1 %all_to_all.31.recv = bf16[4,584,128]{2,1,0:T(8,128)(2,1)S(1)} all-to-all(bf16[4,584,128]{2,1,0:T(8,128)(2,1)S(1)} %shard_map.104), channel_id=1, replica_groups=mesh['y'=8,'zh'=4,'x'=4,'zl'=3,'c'=2] {'x'}, dimensions={0} | all-to-all | bytes 1196032 | tf_op jit(solution)/shard_map/all_to_all | solution.py:232
  48.3 0.8 shard_map.105
  49.0 10.3 %all-to-all-start.2 = ((bf16[8,80,128]{2,1,0:T(8,128)(2,1)}), bf16[8,80,128]{2,1,0:T(8,128)(2,1)S(1)}, u32[]{:S(2)}, u32[]{:S(2)}) async-start(bf16[8,80,128]{2,1,0:T(8,128)(2,1)} %get-tuple-element.58), calls=%async_computation.2 | async-start | bytes 327680 | tf_op jit(solution)/shard_map/all_to_all | solution.py:232
  59.3 1.9 %collective-permute-start.3 = (bf16[576,128]{1,0:T(8,128)(2,1)S(1)}, bf16[576,128]{1,0:T(8,128)(2,1)S(1)}, u32[]{:S(2)}, u32[]{:S(2)}) collective-permute-start(bf16[576,128]{1,0:T(8,128)(2,1)S(1)} %get-tuple-element.59.own), channel_id=1, source_target_pairs={{1,2},{3,4},{5,6},{7,8},{9,10},{11,12},{13,14},{15,16},{17,18},{19... | collective-permute-start | bytes 442376 | tf_op jit(solution)/shard_map/ppermute | solution.py:238
  61.2 6.1 %collective-permute-done.3.far = bf16[576,128]{1,0:T(8,128)(2,1)S(1)} collective-permute-done((bf16[576,128]{1,0:T(8,128)(2,1)S(1)}, bf16[576,128]{1,0:T(8,128)(2,1)S(1)}, u32[]{:S(2)}, u32[]{:S(2)}) %collective-permute-start.3) | collective-permute-done | bytes 147488 | tf_op jit(solution)/shard_map/ppermute | solution.py:238
  67.3 0.0 all-to-all-done.2.recv
  67.4 0.7 shard_map.106
  68.1 8.1 %all-to-all-start.3 = ((bf16[12,80,128]{2,1,0:T(8,128)(2,1)}), bf16[12,80,128]{2,1,0:T(8,128)(2,1)S(1)}, u32[]{:S(2)}, u32[]{:S(2)}) async-start(bf16[12,80,128]{2,1,0:T(8,128)(2,1)} %shard_map.106), calls=%async_computation.3 | async-start | bytes 491520 | tf_op jit(solution)/shard_map/all_to_all | solution.py:232
  76.2 0.3 shard_map.107
  76.5 3.3 %collective-permute-start.4 = (bf16[4,48,128]{2,1,0:T(8,128)(2,1)S(1)}, bf16[4,48,128]{2,1,0:T(8,128)(2,1)S(1)}, u32[]{:S(2)}, u32[]{:S(2)}) collective-permute-start(bf16[4,48,128]{2,1,0:T(8,128)(2,1)S(1)} %get-tuple-element.63), channel_id=1, source_target_pairs={{0,2},{2,4},{4,0},{1,3},{3,5},{5,1},{6,8},{8,10},{10,6},{7,9},{9,1... | collective-permute-start | bytes 147464 | tf_op jit(solution)/shard_map/ppermute | solution.py:299
  79.9 2.9 %collective-permute-start.5 = (bf16[4,48,128]{2,1,0:T(8,128)(2,1)S(1)}, bf16[4,48,128]{2,1,0:T(8,128)(2,1)S(1)}, u32[]{:S(2)}, u32[]{:S(2)}) collective-permute-start(bf16[4,48,128]{2,1,0:T(8,128)(2,1)S(1)} %get-tuple-element.64), channel_id=1, source_target_pairs={{0,4},{2,0},{4,2},{1,5},{3,1},{5,3},{6,10},{8,6},{10,8},{7,11},{9,... | collective-permute-start | bytes 147464 | tf_op jit(solution)/shard_map/ppermute | solution.py:300
  82.7 0.0 collective-permute-done.4.low
  82.7 4.8 %collective-permute-done.5.high = bf16[4,48,128]{2,1,0:T(8,128)(2,1)S(1)} collective-permute-done((bf16[4,48,128]{2,1,0:T(8,128)(2,1)S(1)}, bf16[4,48,128]{2,1,0:T(8,128)(2,1)S(1)}, u32[]{:S(2)}, u32[]{:S(2)}) %collective-permute-start.5) | collective-permute-done | bytes 49184 | tf_op jit(solution)/shard_map/ppermute | solution.py:300
  87.5 0.4 all-to-all-done.3.refs_0_
  87.9 0.6 shard_map.108
  88.5 14.3 %all_to_all.32 = bf16[8,72,128]{2,1,0:T(8,128)(2,1)S(1)} all-to-all(bf16[8,72,128]{2,1,0:T(8,128)(2,1)S(1)} %get-tuple-element.66), channel_id=1, replica_groups=mesh['y'=8,'zh'=4,'x'=4,'zl'=3,'c'=2] {'y'}, dimensions={0} | all-to-all | bytes 294912 | tf_op jit(solution)/shard_map/all_to_all | solution.py:232
  102.9 0.1 shard_map.109
  103.0 10.9 %all_to_all.33.block = bf16[4,720,128]{2,1,0:T(8,128)(2,1)S(1)} all-to-all(bf16[4,720,128]{2,1,0:T(8,128)(2,1)S(1)} %shard_map.109), channel_id=1, replica_groups=mesh['y'=8,'zh'=4,'x'=4,'zl'=3,'c'=2] {'x'}, dimensions={0} | all-to-all | bytes 1474560 | tf_op jit(solution)/shard_map/all_to_all | solution.py:232
  113.9 11.5 %collective-permute-start.6 = (bf16[4,720,128]{2,1,0:T(8,128)(2,1)S(1)}, bf16[4,720,128]{2,1,0:T(8,128)(2,1)S(1)}, u32[]{:S(2)}, u32[]{:S(2)}) collective-permute-start(bf16[4,720,128]{2,1,0:T(8,128)(2,1)S(1)} %all_to_all.33.block), channel_id=1, source_target_pairs={{0,1},{1,0},{2,3},{3,2},{4,5},{5,4},{6,7},{7,6},{8,9},{9,8},{10,11... | collective-permute-start | bytes 2211848 | tf_op jit(solution)/shard_map/ppermute | solution.py:241
  125.4 1.2 shard_map.110
  126.6 0.6 collective-permute-done.6.block
  127.2 1.2 shard_map.111
Async XLA Ops:
  22.5 7.5 %collective-permute-start.1 = (bf16[576,128]{1,0:T(8,128)(2,1)S(1)}, bf16[576,128]{1,0:T(8,128)(2,1)S(1)}, u32[]{:S(2)}, u32[]{:S(2)}) collective-permute-start(bf16[576,128]{1,0:T(8,128)(2,1)S(1)} %bitcast.9), channel_id=1, source_target_pairs={{1,2},{3,4},{5,6},{7,8},{9,10},{11,12},{13,14},{15,16},{17,18},{19... | collective-permute-start | bytes 442376 | tf_op jit(solution)/shard_map/ppermute | solution.py:238
  25.5 4.5 %collective-permute-start = (bf16[576,128]{1,0:T(8,128)(2,1)S(1)}, bf16[576,128]{1,0:T(8,128)(2,1)S(1)}, u32[]{:S(2)}, u32[]{:S(2)}) collective-permute-start(bf16[576,128]{1,0:T(8,128)(2,1)S(1)} %bitcast.10), channel_id=1, source_target_pairs={{0,1},{1,0},{2,3},{3,2},{4,5},{5,4},{6,7},{7,6},{8,9},{9,8},{10,11... | collective-permute-start | bytes 442376 | tf_op jit(solution)/shard_map/ppermute | solution.py:241
  31.1 3.7 %collective-permute-start.2 = (bf16[1664,128]{1,0:T(8,128)(2,1)S(1)}, bf16[1664,128]{1,0:T(8,128)(2,1)S(1)}, u32[]{:S(2)}, u32[]{:S(2)}) collective-permute-start(bf16[1664,128]{1,0:T(8,128)(2,1)S(1)} %get-tuple-element.55), channel_id=1, source_target_pairs={{0,1},{1,0},{2,3},{3,2},{4,5},{5,4},{6,7},{7,6},{8,9},{9,8},{10,11... | collective-permute-start | bytes 1277960 | tf_op jit(solution)/shard_map/ppermute | solution.py:241
  49.0 18.3 %all-to-all-start.2 = ((bf16[8,80,128]{2,1,0:T(8,128)(2,1)}), bf16[8,80,128]{2,1,0:T(8,128)(2,1)S(1)}, u32[]{:S(2)}, u32[]{:S(2)}) async-start(bf16[8,80,128]{2,1,0:T(8,128)(2,1)} %get-tuple-element.58), calls=%async_computation.2 | async-start | bytes 327680 | tf_op jit(solution)/shard_map/all_to_all | solution.py:232
  59.3 8.0 %collective-permute-start.3 = (bf16[576,128]{1,0:T(8,128)(2,1)S(1)}, bf16[576,128]{1,0:T(8,128)(2,1)S(1)}, u32[]{:S(2)}, u32[]{:S(2)}) collective-permute-start(bf16[576,128]{1,0:T(8,128)(2,1)S(1)} %get-tuple-element.59.own), channel_id=1, source_target_pairs={{1,2},{3,4},{5,6},{7,8},{9,10},{11,12},{13,14},{15,16},{17,18},{19... | collective-permute-start | bytes 442376 | tf_op jit(solution)/shard_map/ppermute | solution.py:238
  68.1 19.9 %all-to-all-start.3 = ((bf16[12,80,128]{2,1,0:T(8,128)(2,1)}), bf16[12,80,128]{2,1,0:T(8,128)(2,1)S(1)}, u32[]{:S(2)}, u32[]{:S(2)}) async-start(bf16[12,80,128]{2,1,0:T(8,128)(2,1)} %shard_map.106), calls=%async_computation.3 | async-start | bytes 491520 | tf_op jit(solution)/shard_map/all_to_all | solution.py:232
  76.5 6.2 %collective-permute-start.4 = (bf16[4,48,128]{2,1,0:T(8,128)(2,1)S(1)}, bf16[4,48,128]{2,1,0:T(8,128)(2,1)S(1)}, u32[]{:S(2)}, u32[]{:S(2)}) collective-permute-start(bf16[4,48,128]{2,1,0:T(8,128)(2,1)S(1)} %get-tuple-element.63), channel_id=1, source_target_pairs={{0,2},{2,4},{4,0},{1,3},{3,5},{5,1},{6,8},{8,10},{10,6},{7,9},{9,1... | collective-permute-start | bytes 147464 | tf_op jit(solution)/shard_map/ppermute | solution.py:299
  79.9 7.6 %collective-permute-start.5 = (bf16[4,48,128]{2,1,0:T(8,128)(2,1)S(1)}, bf16[4,48,128]{2,1,0:T(8,128)(2,1)S(1)}, u32[]{:S(2)}, u32[]{:S(2)}) collective-permute-start(bf16[4,48,128]{2,1,0:T(8,128)(2,1)S(1)} %get-tuple-element.64), channel_id=1, source_target_pairs={{0,4},{2,0},{4,2},{1,5},{3,1},{5,3},{6,10},{8,6},{10,8},{7,11},{9,... | collective-permute-start | bytes 147464 | tf_op jit(solution)/shard_map/ppermute | solution.py:300
  113.9 13.3 %collective-permute-start.6 = (bf16[4,720,128]{2,1,0:T(8,128)(2,1)S(1)}, bf16[4,720,128]{2,1,0:T(8,128)(2,1)S(1)}, u32[]{:S(2)}, u32[]{:S(2)}) collective-permute-start(bf16[4,720,128]{2,1,0:T(8,128)(2,1)S(1)} %all_to_all.33.block), channel_id=1, source_target_pairs={{0,1},{1,0},{2,3},{3,2},{4,5},{5,4},{6,7},{7,6},{8,9},{9,8},{10,11... | collective-permute-start | bytes 2211848 | tf_op jit(solution)/shard_map/ppermute | solution.py:241

commit v9 on v6

--- a/solution.py
+++ b/solution.py
@@ -13,11 +13,13 @@
 GRAPH = ("y", "zh")
 FEAT = ("x", "zl", "c")
 LINE = ("zh", "zl")
+PLANE = ("y", "zl")
 N_X = 4
 N_Y = 8
 N_LINE = 12
 N_FEAT = 24
 ROWS = 72
+THIRD = 24
 TAIL = 8
 SMEM = pl.BlockSpec(memory_space=pltpu.SMEM)
 ANY = pl.BlockSpec(memory_space=pl.ANY)
@@ -79,19 +81,28 @@
     return jnp.where(first, f, n), jnp.where(first, n, f)
 
 
+def early_kernel(own, adj, ws, bias, inner, degree, pre):
+    a = adj[...]
+    degree[...] = 1.0 + dot(jnp.ones((8, 3 * TILE), BF16), a, 1, 1)
+    x = own[...]
+    inner[...] = dot(x, a[:, lanes(1)], 1, 1)
+    pre[...] = dot(x, ws[...], 0, 0) + bias[...]
+
+
 def forward_kernel(
-    core, near, far, own, adj, ws, wn, bias, cot, act, grad, keep, send, back, scaled
+    core, near, far, own, adj, ws, wn, cot, inner, degree, pre_self,
+    act, grad, keep, send, back, scaled,
 ):
-    a = adj[...]
-    degree = (1.0 + dot(jnp.ones((8, 3 * TILE), BF16), a, 1, 1))[:1]
-    low, high = sides(core, far[...], near[...])
-    m = (band((low, own[...], high), a) / degree).astype(BF16)
-    x = own[...]
-    pre = dot(x, ws[...], 0, 0) + dot(m, wn[...], 0, 0) + bias[...]
+    count = degree[:1]
+    edges = jnp.concatenate([adj[:, lanes(0)], adj[:, lanes(2)]], axis=1)
+    tiles = jnp.concatenate(sides(core, far[...], near[...]), axis=1)
+    m = ((inner[...] + dot(tiles, edges, 1, 1)) / count).astype(BF16)
+    pre = pre_self[...] + dot(m, wn[...], 0, 0)
     s = 1.0 / (1.0 + jnp.exp(-pre))
     act[...] = (pre * s).astype(BF16)
     g = (cot[...].astype(F32) * s * (1.0 + pre * (1.0 - s))).astype(BF16)
     grad[...] = g
+    x = own[...]
     first = core[0] == 0
     keep[...] = jnp.where(first, x, m)
     send[:576] = jnp.where(first, m, x)
@@ -99,7 +110,7 @@
         send[576 + b * TILE : 576 + (b + 1) * TILE] = g[:, lanes(b)]
     back[...] = dot(ws[...], g, 1, 1).astype(BF16)
     rounded = dot(wn[...], g, 1, 1).astype(BF16).astype(F32)
-    scale = (rounded / degree).astype(BF16)
+    scale = (rounded / count).astype(BF16)
     scaled[...] = scale
     send[576 + 4 * TILE :] = scale
 
@@ -132,16 +143,19 @@
 
 
 def y_kernel(recv, out):
-    rounded = summed(recv).astype(BF16)
-    for d in range(N_LINE):
-        out[d] = rounded
+    total = summed(recv)
+    tail = total[ROWS:]
+    for zl in range(3):
+        rounded = jnp.concatenate([total[zl * THIRD : (zl + 1) * THIRD], tail], axis=0).astype(BF16)
+        for zh in range(4):
+            out[3 * zh + zl] = rounded
 
 
 def line_kernel(scale, recv, out, bias):
     total = summed(recv) * scale
-    bias[...] = jnp.concatenate([total[ROWS + b : ROWS + b + 1] for b in range(N_X)], axis=1)
-    rounded = total[:ROWS].astype(BF16)
-    for d in range(N_Y):
+    bias[...] = jnp.concatenate([total[THIRD + b : THIRD + b + 1] for b in range(N_X)], axis=1)
+    rounded = total[:THIRD].astype(BF16)
+    for d in range(3 * N_Y):
         out[d] = rounded
 
 
@@ -271,13 +285,18 @@
         ),
         [dma((5,))],
     )(tile, *map(pinned, (adjacency, w_self, w_neigh, bias_out.reshape(1, f_out), cotangent)))
-    near, far, held = lax.optimization_barrier((near, far, held))
-    adj = held[0]
+    adj, ws, wn, bias, cot = held
+    early = call(
+        early_kernel,
+        [VMEM] * 4,
+        (sds((f_in, TILE), F32), sds((8, TILE), F32), sds((TILE, f_out), F32)),
+    )(own, adj, ws, bias)
+    near, far, early = lax.optimization_barrier((near, far, early))
     act, grad, keep, send, back, scaled = call(
         forward_kernel,
-        [SMEM] + [VMEM] * 8,
+        [SMEM] + [VMEM] * 10,
         (sds((TILE, f_out)), sds((TILE, f_out)), wide, sds((2 * f_in + f_out, TILE)), wide, wide),
-    )(core, near, far, own, *held)
+    )(core, near, far, own, adj, ws, wn, cot, *early)
     recv = swap(send)
     s_far = across(scaled)
     partial, act = call(
@@ -295,16 +314,15 @@
     )(core, zl, recv, s_far, scaled, adj, back)
     from_x, stay, up, down = lax.optimization_barrier((from_x, stay, up, down))
     from_y = exchange(call(x_kernel, [VMEM], sds((N_Y, ROWS + TAIL, TILE)))(from_x), "y")
-    from_line = exchange(call(y_kernel, [VMEM], sds((N_LINE, ROWS + TAIL, TILE)))(from_y), LINE)
+    from_line = exchange(call(y_kernel, [VMEM], sds((N_LINE, THIRD + TAIL, TILE)))(from_y), LINE)
     f_low = lax.ppermute(up, "zl", [(i, (i + 1) % 3) for i in range(3)])
     f_high = lax.ppermute(down, "zl", [(i, (i + 2) % 3) for i in range(3)])
-    from_line, f_low, f_high = lax.optimization_barrier((from_line, f_low, f_high))
-    to_y, bias_sum = call(
+    to_plane, bias_sum = call(
         lambda *refs: line_kernel(scale, *refs),
         [VMEM],
-        (sds((N_Y, ROWS, TILE)), sds((1, f_out), F32)),
+        (sds((3 * N_Y, THIRD, TILE)), sds((1, f_out), F32)),
     )(from_line)
-    column = exchange(to_y, "y").reshape(f_in, TILE)
+    column = exchange(to_plane, PLANE).reshape(f_in, TILE)
     to_x = call(join_kernel, [SMEM] + [VMEM] * 4, sds((N_X, f_in + 6 * width, TILE)))(
         zl, column, stay, f_low, f_high
     )

time: 126 us -> 124 us (0.984)
  blocking collectives: 63.5 us -> 68.3 us
  starting transfers between devices: 36.1 us -> 32.6 us
  waiting for transfers between devices: 16.3 us -> 13.7 us
    all_to_all x4, blocking collectives: 63.5 us -> 68.3 us  [exchange(): return lax.all_to_all(x, axis, split_axis=0, concat_axis=0, tiled=False)]
    all_to_all x2, starting transfers between devices: 9.25 us -> 7.47 us  [exchange(): return lax.all_to_all(x, axis, split_axis=0, concat_axis=0, tiled=False)]
    ppermute x3, starting transfers between devices: 15.2 us -> 13.5 us  [swap(): return lax.ppermute(x, 'c', [(0, 1), (1, 0)])]
    all_to_all x2, waiting for transfers between devices: 6.25 us -> 4.56 us  [exchange(): return lax.all_to_all(x, axis, split_axis=0, concat_axis=0, tiled=False)]
where the time goes in v9:
time: 124 us
  blocking collectives  68.3 us (55%)
  starting transfers between devices  32.6 us (26%)
  waiting for transfers between devices  13.7 us (11%)
  Pallas kernels  8.49 us (7%)
    all_to_all x4, blocking collectives, exchange(): return lax.all_to_all(x, axis, split_axis=0, concat_axis=0, tiled=False)  68.3 us
    ppermute x3, starting transfers between devices, swap(): return lax.ppermute(x, 'c', [(0, 1), (1, 0)])  13.5 us
    all_to_all x2, starting transfers between devices, exchange(): return lax.all_to_all(x, axis, split_axis=0, concat_axis=0, tiled=False)  7.47 us
    ppermute x2, starting transfers between devices, across(): return lax.ppermute(x, AXES, pairs)  5.42 us
    ppermute x2, waiting for transfers between devices, across(): return lax.ppermute(x, AXES, pairs)  5.1 us
    all_to_all x2, waiting for transfers between devices, exchange(): return lax.all_to_all(x, axis, split_axis=0, concat_axis=0, tiled=False)  4.56 us
    ppermute x1, starting transfers between devices, local(): f_high = lax.ppermute(down, 'zl', [(i, (i + 2) % 3) for i in range(3)])  3.1 us
    ppermute x1, starting transfers between devices, local(): f_low = lax.ppermute(up, 'zl', [(i, (i + 1) % 3) for i in range(3)])  3.08 us
  transfers between devices with their start and end apart: 9, of which 7 were waited for; matrix products, arithmetic and copies ran while one was open for 0% of the time, Pallas kernels for 2%

profile of v9, /device:TPU:1, one launch (start us, length us, event | category | flops | bytes accessed | tf_op | source)
XLA Modules:
  0.0 123.8 jit_solution(10654633958339265853)
XLA Ops:
  0.6 0.9 shard_map.101
  1.6 20.9 %all_to_all.30 = bf16[24,24,128]{2,1,0:T(8,128)(2,1)S(1)} all-to-all(bf16[24,24,128]{2,1,0:T(8,128)(2,1)S(1)} %shard_map.101), channel_id=1, replica_groups=mesh['y'=8,'zh'=4,'x'=4,'zl'=3,'c'=2] {'x','zl','c'}, dimensions={0} | all-to-all | bytes 294912 | tf_op jit(solution)/shard_map/all_to_all | solution.py:246
  22.5 3.0 %collective-permute-start.1 = (bf16[576,128]{1,0:T(8,128)(2,1)S(1)}, bf16[576,128]{1,0:T(8,128)(2,1)S(1)}, u32[]{:S(2)}, u32[]{:S(2)}) collective-permute-start(bf16[576,128]{1,0:T(8,128)(2,1)S(1)} %bitcast.9), channel_id=1, source_target_pairs={{1,2},{3,4},{5,6},{7,8},{9,10},{11,12},{13,14},{15,16},{17,18},{19... | collective-permute-start | bytes 442376 | tf_op jit(solution)/shard_map/ppermute | solution.py:252
  25.5 1.9 %collective-permute-start = (bf16[576,128]{1,0:T(8,128)(2,1)S(1)}, bf16[576,128]{1,0:T(8,128)(2,1)S(1)}, u32[]{:S(2)}, u32[]{:S(2)}) collective-permute-start(bf16[576,128]{1,0:T(8,128)(2,1)S(1)} %bitcast.10), channel_id=1, source_target_pairs={{0,1},{1,0},{2,3},{3,2},{4,5},{5,4},{6,7},{7,6},{8,9},{9,8},{10,11... | collective-permute-start | bytes 442376 | tf_op jit(solution)/shard_map/ppermute | solution.py:255
  27.4 1.4 %shard_map.102 = (bf16[128,384]{1,0:T(8,128)(2,1)S(1)}, bf16[576,512]{1,0:T(8,128)(2,1)S(1)}, bf16[576,512]{1,0:T(8,128)(2,1)S(1)}, f32[1,512]{1,0:T(1,128)S(1)}, bf16[128,512]{1,0:T(8,128)(2,1)S(1)}) custom-call(s32[1]{0:T(128)} %bitcast.3.tile, bf16[3072,384]{1,0:T(8,128)(2,1)} %adjacency.1, bf16[576,512]{1,0:T(8,128)(2,1)} %refs_0_.1, ...), custom_call_target="tpu_custom_call" | custom-call | tf_op jit(solution)/shard_map/pallas_call | solution.py:276
  28.8 0.3 shard_map.103
  29.1 0.8 collective-permute-done.1.far
  29.9 0.0 collective-permute-done.near
  30.0 1.0 shard_map.104
  31.0 1.9 %collective-permute-start.2 = (bf16[1664,128]{1,0:T(8,128)(2,1)S(1)}, bf16[1664,128]{1,0:T(8,128)(2,1)S(1)}, u32[]{:S(2)}, u32[]{:S(2)}) collective-permute-start(bf16[1664,128]{1,0:T(8,128)(2,1)S(1)} %get-tuple-element.58), channel_id=1, source_target_pairs={{0,1},{1,0},{2,3},{3,2},{4,5},{5,4},{6,7},{7,6},{8,9},{9,8},{10,11... | collective-permute-start | bytes 1277960 | tf_op jit(solution)/shard_map/ppermute | solution.py:255
  32.9 1.7 %collective-permute-done.2.recv = bf16[1664,128]{1,0:T(8,128)(2,1)S(1)} collective-permute-done((bf16[1664,128]{1,0:T(8,128)(2,1)S(1)}, bf16[1664,128]{1,0:T(8,128)(2,1)S(1)}, u32[]{:S(2)}, u32[]{:S(2)}) %collective-permute-start.2) | collective-permute-done | bytes 426016 | tf_op jit(solution)/shard_map/ppermute | solution.py:255
  34.7 1.1 shard_map.105
  35.8 3.6 %all-to-all-start.1 = ((bf16[4,584,128]{2,1,0:T(8,128)(2,1)}), bf16[4,584,128]{2,1,0:T(8,128)(2,1)S(1)}, u32[]{:S(2)}, u32[]{:S(2)}) async-start(bf16[4,584,128]{2,1,0:T(8,128)(2,1)} %get-tuple-element.61), calls=%async_computation.1 | async-start | bytes 1196032 | tf_op jit(solution)/shard_map/all_to_all | solution.py:246
  39.4 2.4 %collective-permute-start.3 = (bf16[576,128]{1,0:T(8,128)(2,1)S(1)}, bf16[576,128]{1,0:T(8,128)(2,1)S(1)}, u32[]{:S(2)}, u32[]{:S(2)}) collective-permute-start(bf16[576,128]{1,0:T(8,128)(2,1)S(1)} %get-tuple-element.62.own), channel_id=1, source_target_pairs={{1,2},{3,4},{5,6},{7,8},{9,10},{11,12},{13,14},{15,16},{17,18},{19... | collective-permute-start | bytes 442376 | tf_op jit(solution)/shard_map/ppermute | solution.py:252
  41.9 4.3 %collective-permute-done.3.far = bf16[576,128]{1,0:T(8,128)(2,1)S(1)} collective-permute-done((bf16[576,128]{1,0:T(8,128)(2,1)S(1)}, bf16[576,128]{1,0:T(8,128)(2,1)S(1)}, u32[]{:S(2)}, u32[]{:S(2)}) %collective-permute-start.3) | collective-permute-done | bytes 147488 | tf_op jit(solution)/shard_map/ppermute | solution.py:252
  46.2 3.4 %all-to-all-done.1.recv = bf16[4,584,128]{2,1,0:T(8,128)(2,1)S(1)} async-done(((bf16[4,584,128]{2,1,0:T(8,128)(2,1)}), bf16[4,584,128]{2,1,0:T(8,128)(2,1)S(1)}, u32[]{:S(2)}, u32[]{:S(2)}) %all-to-all-start.1) | async-done | bytes 598048 | tf_op jit(solution)/shard_map/all_to_all | solution.py:246
  49.5 0.3 shard_map.106
  49.9 0.1 shard_map.107
  49.9 21.3 %all_to_all.31.recv = bf16[8,80,128]{2,1,0:T(8,128)(2,1)S(1)} all-to-all(bf16[8,80,128]{2,1,0:T(8,128)(2,1)S(1)} %shard_map.107), channel_id=1, replica_groups=mesh['y'=8,'zh'=4,'x'=4,'zl'=3,'c'=2] {'y'}, dimensions={0} | all-to-all | bytes 327680 | tf_op jit(solution)/shard_map/all_to_all | solution.py:246
  71.2 15.2 %all_to_all.32.refs_0_ = bf16[12,32,128]{2,1,0:T(8,128)(2,1)S(1)} all-to-all(bf16[12,32,128]{2,1,0:T(8,128)(2,1)S(1)} %shard_map.108), channel_id=1, replica_groups=mesh['y'=8,'zh'=4,'x'=4,'zl'=3,'c'=2] {'zh','zl'}, dimensions={0} | all-to-all | bytes 196608 | tf_op jit(solution)/shard_map/all_to_all | solution.py:246
  86.5 0.7 shard_map.109
  87.1 3.8 %all-to-all-start.4 = ((bf16[24,24,128]{2,1,0:T(8,128)(2,1)}), bf16[24,24,128]{2,1,0:T(8,128)(2,1)S(1)}, u32[]{:S(2)}, u32[]{:S(2)}) async-start(bf16[24,24,128]{2,1,0:T(8,128)(2,1)} %get-tuple-element.70), calls=%async_computation.4 | async-start | bytes 294912 | tf_op jit(solution)/shard_map/all_to_all | solution.py:246
  91.0 3.1 %collective-permute-start.4 = (bf16[4,48,128]{2,1,0:T(8,128)(2,1)S(1)}, bf16[4,48,128]{2,1,0:T(8,128)(2,1)S(1)}, u32[]{:S(2)}, u32[]{:S(2)}) collective-permute-start(bf16[4,48,128]{2,1,0:T(8,128)(2,1)S(1)} %get-tuple-element.72), channel_id=1, source_target_pairs={{0,2},{2,4},{4,0},{1,3},{3,5},{5,1},{6,8},{8,10},{10,6},{7,9},{9,1... | collective-permute-start | bytes 147464 | tf_op jit(solution)/shard_map/ppermute | solution.py:318
  94.1 3.1 %collective-permute-start.5 = (bf16[4,48,128]{2,1,0:T(8,128)(2,1)S(1)}, bf16[4,48,128]{2,1,0:T(8,128)(2,1)S(1)}, u32[]{:S(2)}, u32[]{:S(2)}) collective-permute-start(bf16[4,48,128]{2,1,0:T(8,128)(2,1)S(1)} %get-tuple-element.73), channel_id=1, source_target_pairs={{0,4},{2,0},{4,2},{1,5},{3,1},{5,3},{6,10},{8,6},{10,8},{7,11},{9,... | collective-permute-start | bytes 147464 | tf_op jit(solution)/shard_map/ppermute | solution.py:319
  97.2 0.0 collective-permute-done.4.low
  97.2 1.7 %collective-permute-done.5.high = bf16[4,48,128]{2,1,0:T(8,128)(2,1)S(1)} collective-permute-done((bf16[4,48,128]{2,1,0:T(8,128)(2,1)S(1)}, bf16[4,48,128]{2,1,0:T(8,128)(2,1)S(1)}, u32[]{:S(2)}, u32[]{:S(2)}) %collective-permute-start.5) | collective-permute-done | bytes 49184 | tf_op jit(solution)/shard_map/ppermute | solution.py:319
  98.9 1.2 all-to-all-done.4
  100.1 0.1 shard_map.110
  100.2 10.9 %all_to_all.33.block = bf16[4,720,128]{2,1,0:T(8,128)(2,1)S(1)} all-to-all(bf16[4,720,128]{2,1,0:T(8,128)(2,1)S(1)} %shard_map.110), channel_id=1, replica_groups=mesh['y'=8,'zh'=4,'x'=4,'zl'=3,'c'=2] {'x'}, dimensions={0} | all-to-all | bytes 1474560 | tf_op jit(solution)/shard_map/all_to_all | solution.py:246
  111.1 9.7 %collective-permute-start.6 = (bf16[4,720,128]{2,1,0:T(8,128)(2,1)S(1)}, bf16[4,720,128]{2,1,0:T(8,128)(2,1)S(1)}, u32[]{:S(2)}, u32[]{:S(2)}) collective-permute-start(bf16[4,720,128]{2,1,0:T(8,128)(2,1)S(1)} %all_to_all.33.block), channel_id=1, source_target_pairs={{0,1},{1,0},{2,3},{3,2},{4,5},{5,4},{6,7},{7,6},{8,9},{9,8},{10,11... | collective-permute-start | bytes 2211848 | tf_op jit(solution)/shard_map/ppermute | solution.py:255
  120.8 1.2 %shard_map.111 = (f32[576,512]{1,0:T(8,128)}, f32[576,512]{1,0:T(8,128)}, f32[24,3072]{1,0:T(8,128)}) custom-call(s32[1]{0:T(128)} %bitcast.core, bf16[4,720,128]{2,1,0:T(8,128)(2,1)S(1)} %all_to_all.33.block), custom_call_target="tpu_custom_call" | custom-call | tf_op jit(solution)/shard_map/pallas_call | solution.py:338
  122.0 0.6 collective-permute-done.6.block
  122.6 1.2 shard_map.112
  (1 shorter events, 0.0 us)
Async XLA Ops:
  22.5 7.5 %collective-permute-start.1 = (bf16[576,128]{1,0:T(8,128)(2,1)S(1)}, bf16[576,128]{1,0:T(8,128)(2,1)S(1)}, u32[]{:S(2)}, u32[]{:S(2)}) collective-permute-start(bf16[576,128]{1,0:T(8,128)(2,1)S(1)} %bitcast.9), channel_id=1, source_target_pairs={{1,2},{3,4},{5,6},{7,8},{9,10},{11,12},{13,14},{15,16},{17,18},{19... | collective-permute-start | bytes 442376 | tf_op jit(solution)/shard_map/ppermute | solution.py:252
  25.5 4.5 %collective-permute-start = (bf16[576,128]{1,0:T(8,128)(2,1)S(1)}, bf16[576,128]{1,0:T(8,128)(2,1)S(1)}, u32[]{:S(2)}, u32[]{:S(2)}) collective-permute-start(bf16[576,128]{1,0:T(8,128)(2,1)S(1)} %bitcast.10), channel_id=1, source_target_pairs={{0,1},{1,0},{2,3},{3,2},{4,5},{5,4},{6,7},{7,6},{8,9},{9,8},{10,11... | collective-permute-start | bytes 442376 | tf_op jit(solution)/shard_map/ppermute | solution.py:255
  31.0 3.7 %collective-permute-start.2 = (bf16[1664,128]{1,0:T(8,128)(2,1)S(1)}, bf16[1664,128]{1,0:T(8,128)(2,1)S(1)}, u32[]{:S(2)}, u32[]{:S(2)}) collective-permute-start(bf16[1664,128]{1,0:T(8,128)(2,1)S(1)} %get-tuple-element.58), channel_id=1, source_target_pairs={{0,1},{1,0},{2,3},{3,2},{4,5},{5,4},{6,7},{7,6},{8,9},{9,8},{10,11... | collective-permute-start | bytes 1277960 | tf_op jit(solution)/shard_map/ppermute | solution.py:255
  35.8 13.8 %all-to-all-start.1 = ((bf16[4,584,128]{2,1,0:T(8,128)(2,1)}), bf16[4,584,128]{2,1,0:T(8,128)(2,1)S(1)}, u32[]{:S(2)}, u32[]{:S(2)}) async-start(bf16[4,584,128]{2,1,0:T(8,128)(2,1)} %get-tuple-element.61), calls=%async_computation.1 | async-start | bytes 1196032 | tf_op jit(solution)/shard_map/all_to_all | solution.py:246
  39.4 6.7 %collective-permute-start.3 = (bf16[576,128]{1,0:T(8,128)(2,1)S(1)}, bf16[576,128]{1,0:T(8,128)(2,1)S(1)}, u32[]{:S(2)}, u32[]{:S(2)}) collective-permute-start(bf16[576,128]{1,0:T(8,128)(2,1)S(1)} %get-tuple-element.62.own), channel_id=1, source_target_pairs={{1,2},{3,4},{5,6},{7,8},{9,10},{11,12},{13,14},{15,16},{17,18},{19... | collective-permute-start | bytes 442376 | tf_op jit(solution)/shard_map/ppermute | solution.py:252
  87.1 12.9 %all-to-all-start.4 = ((bf16[24,24,128]{2,1,0:T(8,128)(2,1)}), bf16[24,24,128]{2,1,0:T(8,128)(2,1)S(1)}, u32[]{:S(2)}, u32[]{:S(2)}) async-start(bf16[24,24,128]{2,1,0:T(8,128)(2,1)} %get-tuple-element.70), calls=%async_computation.4 | async-start | bytes 294912 | tf_op jit(solution)/shard_map/all_to_all | solution.py:246
  91.0 6.2 %collective-permute-start.4 = (bf16[4,48,128]{2,1,0:T(8,128)(2,1)S(1)}, bf16[4,48,128]{2,1,0:T(8,128)(2,1)S(1)}, u32[]{:S(2)}, u32[]{:S(2)}) collective-permute-start(bf16[4,48,128]{2,1,0:T(8,128)(2,1)S(1)} %get-tuple-element.72), channel_id=1, source_target_pairs={{0,2},{2,4},{4,0},{1,3},{3,5},{5,1},{6,8},{8,10},{10,6},{7,9},{9,1... | collective-permute-start | bytes 147464 | tf_op jit(solution)/shard_map/ppermute | solution.py:318
  94.1 4.8 %collective-permute-start.5 = (bf16[4,48,128]{2,1,0:T(8,128)(2,1)S(1)}, bf16[4,48,128]{2,1,0:T(8,128)(2,1)S(1)}, u32[]{:S(2)}, u32[]{:S(2)}) collective-permute-start(bf16[4,48,128]{2,1,0:T(8,128)(2,1)S(1)} %get-tuple-element.73), channel_id=1, source_target_pairs={{0,4},{2,0},{4,2},{1,5},{3,1},{5,3},{6,10},{8,6},{10,8},{7,11},{9,... | collective-permute-start | bytes 147464 | tf_op jit(solution)/shard_map/ppermute | solution.py:319
  111.1 11.5 %collective-permute-start.6 = (bf16[4,720,128]{2,1,0:T(8,128)(2,1)S(1)}, bf16[4,720,128]{2,1,0:T(8,128)(2,1)S(1)}, u32[]{:S(2)}, u32[]{:S(2)}) collective-permute-start(bf16[4,720,128]{2,1,0:T(8,128)(2,1)S(1)} %all_to_all.33.block), channel_id=1, source_target_pairs={{0,1},{1,0},{2,3},{3,2},{4,5},{5,4},{6,7},{7,6},{8,9},{9,8},{10,11... | collective-permute-start | bytes 2211848 | tf_op jit(solution)/shard_map/ppermute | solution.py:255

commit v10 on v9

--- a/solution.py
+++ b/solution.py
@@ -13,7 +13,7 @@
 GRAPH = ("y", "zh")
 FEAT = ("x", "zl", "c")
 LINE = ("zh", "zl")
-PLANE = ("y", "zl")
+BLOCK = ("x", "zl")
 N_X = 4
 N_Y = 8
 N_LINE = 12
@@ -155,39 +155,34 @@
     total = summed(recv) * scale
     bias[...] = jnp.concatenate([total[THIRD + b : THIRD + b + 1] for b in range(N_X)], axis=1)
     rounded = total[:THIRD].astype(BF16)
-    for d in range(3 * N_Y):
+    for d in range(N_Y):
         out[d] = rounded
 
 
-def feat_kernel(core, zl, recv, far, own, adj, back, stay, up, down, parts):
+def feat_kernel(core, recv, far, own, adj, back, out):
     low, high = sides(core, far[...], recv[recv.shape[0] - own.shape[0] :])
     total = back[...].astype(F32) + band((low, own[...], high), adj[...])
-    width = parts.shape[1]
-    for i in range(N_FEAT):
-        parts[i] = total[i * width : (i + 1) * width]
-    for shift, out in enumerate((stay, up, down)):
-        at = 2 * lax.rem(zl[0] + shift, 3)
-        for d in range(N_X):
-            pair = jnp.concatenate([parts[6 * d + at], parts[6 * d + at + 1]], axis=0)
-            out[d] = pair.astype(BF16)
-
-
-def join_kernel(zl, grads, stay, low, high, out):
-    f_in = grads.shape[0]
-    pair = stay.shape[1]
+    pair = out.shape[1]
+    for d in range(N_LINE):
+        out[d] = total[d * pair : (d + 1) * pair].astype(BF16)
+
+
+def join_kernel(grads, feats, out):
+    rows = grads.shape[0]
     whole = grads[...]
-    place = zl[0]
-    for d in range(N_X):
-        out[d, :f_in] = whole
-        for p in range(3):
-            far = jnp.where(place == (p + 1) % 3, low[d], high[d])
-            out[d, f_in + p * pair : f_in + (p + 1) * pair] = jnp.where(place == p, stay[d], far)
+    for d in range(N_LINE):
+        out[d, :rows] = whole
+        out[d, rows:] = feats[d]
 
 
 def halves(block, held, copies):
-    for d in range(N_X):
-        held[:, lanes(d)] = block[d, : held.shape[0]].astype(F32)
-        copies(d)
+    for x in range(N_X):
+        for zl in range(3):
+            rows = block[3 * x + zl, : N_Y * THIRD].astype(F32)
+            for y in range(N_Y):
+                at = y * ROWS + zl * THIRD
+                held[at : at + THIRD, lanes(x)] = rows[y * THIRD : (y + 1) * THIRD]
+        copies(x)
 
 
 def send_half(held, sems, first, yes, no):
@@ -210,19 +205,14 @@
 
 def columns(core, source, block, gf, part, sems):
     width = part.shape[1]
-    f_in = block.shape[1] - 6 * width
     first = core == 0
     copies = []
-    for d in range(N_X):
-        rows = block[d, f_in:].astype(F32)
-        for p in range(3):
-            k = 3 * d + p
-            even = rows[2 * p * width : (2 * p + 1) * width]
-            odd = rows[(2 * p + 1) * width : (2 * p + 2) * width]
-            at = pl.ds(pl.multiple_of((2 * k + source) * TILE, TILE), TILE)
-            part[k] = jnp.where(first, even, odd)
-            copies.append(pltpu.make_async_copy(part.at[k], gf.at[:, at], sems.at[k]))
-            copies[-1].start()
+    for d in range(N_LINE):
+        rows = block[d, N_Y * THIRD :].astype(F32)
+        at = pl.ds(pl.multiple_of((2 * d + source) * TILE, TILE), TILE)
+        part[d] = jnp.where(first, rows[:width], rows[width:])
+        copies.append(pltpu.make_async_copy(part.at[d], gf.at[:, at], sems.at[d]))
+        copies[-1].start()
     return copies
 
 
@@ -304,29 +294,20 @@
     )(keep, grad, recv, act)
     from_x = exchange(partial, "x")
     from_x, s_far = lax.optimization_barrier((from_x, s_far))
-    zl = lax.axis_index("zl").astype(jnp.int32).reshape(1)
-    pair = sds((N_X, 2 * width, TILE))
-    stay, up, down = call(
-        feat_kernel,
-        [SMEM] * 2 + [VMEM] * 5,
-        (pair,) * 3,
-        [pltpu.VMEM((N_FEAT, width, TILE), F32)],
-    )(core, zl, recv, s_far, scaled, adj, back)
-    from_x, stay, up, down = lax.optimization_barrier((from_x, stay, up, down))
+    feats = call(feat_kernel, [SMEM] + [VMEM] * 5, sds((N_LINE, 2 * width, TILE)))(
+        core, recv, s_far, scaled, adj, back
+    )
+    from_x, feats = lax.optimization_barrier((from_x, feats))
     from_y = exchange(call(x_kernel, [VMEM], sds((N_Y, ROWS + TAIL, TILE)))(from_x), "y")
     from_line = exchange(call(y_kernel, [VMEM], sds((N_LINE, THIRD + TAIL, TILE)))(from_y), LINE)
-    f_low = lax.ppermute(up, "zl", [(i, (i + 1) % 3) for i in range(3)])
-    f_high = lax.ppermute(down, "zl", [(i, (i + 2) % 3) for i in range(3)])
-    to_plane, bias_sum = call(
+    to_y_again, bias_sum = call(
         lambda *refs: line_kernel(scale, *refs),
         [VMEM],
-        (sds((3 * N_Y, THIRD, TILE)), sds((1, f_out), F32)),
+        (sds((N_Y, THIRD, TILE)), sds((1, f_out), F32)),
     )(from_line)
-    column = exchange(to_plane, PLANE).reshape(f_in, TILE)
-    to_x = call(join_kernel, [SMEM] + [VMEM] * 4, sds((N_X, f_in + 6 * width, TILE)))(
-        zl, column, stay, f_low, f_high
-    )
-    block = exchange(to_x, "x")
+    column = exchange(to_y_again, "y").reshape(N_Y * THIRD, TILE)
+    to_block = call(join_kernel, [VMEM] * 2, sds((N_LINE, N_Y * THIRD + 2 * width, TILE)))(column, feats)
+    block = exchange(to_block, BLOCK)
     other = swap(block)
     whole = sds((width, n_rows), F32)
     room = [

time: 124 us -> 124 us (level)
  blocking collectives: 68.3 us -> 80.8 us
  starting transfers between devices: 32.6 us -> 22.4 us
  waiting for transfers between devices: 13.7 us -> 10.8 us
    all_to_all x4 -> x5, blocking collectives: 68.3 us -> 80.8 us  [exchange(): return lax.all_to_all(x, axis, split_axis=0, concat_axis=0, tiled=False)]
    ppermute x2 -> x0, starting transfers between devices: 6.18 us -> none  [the longest x1 3.1 us: local(): f_high = lax.ppermute(down, 'zl', [(i, (i + 2) % 3) for i in range(3)])]
    all_to_all x2 -> x1, starting transfers between devices: 7.47 us -> 3.64 us  [exchange(): return lax.all_to_all(x, axis, split_axis=0, concat_axis=0, tiled=False)]
    ppermute x2 -> x0, waiting for transfers between devices: 1.72 us -> none  [the longest x1 1.71 us: local(): f_high = lax.ppermute(down, 'zl', [(i, (i + 2) % 3) for i in range(3)])]
    all_to_all x2 -> x1, waiting for transfers between devices: 4.56 us -> 3.37 us  [exchange(): return lax.all_to_all(x, axis, split_axis=0, concat_axis=0, tiled=False)]
  transfers between devices with their start and end apart: 9 -> 6, of which waited for: 7 -> 5; matrix products, arithmetic and copies ran while one was open for 0% -> 0% of each run, Pallas kernels for 2% -> 2%
where the time goes in v10:
time: 124 us; the launch traced here: 123 us
  blocking collectives  80.8 us (65%)
  starting transfers between devices  22.4 us (18%)
  waiting for transfers between devices  10.8 us (9%)
  Pallas kernels  8.37 us (7%)
    all_to_all x5, blocking collectives, exchange(): return lax.all_to_all(x, axis, split_axis=0, concat_axis=0, tiled=False)  80.8 us
    ppermute x3, starting transfers between devices, swap(): return lax.ppermute(x, 'c', [(0, 1), (1, 0)])  13.4 us
    ppermute x2, starting transfers between devices, across(): return lax.ppermute(x, AXES, pairs)  5.42 us
    ppermute x2, waiting for transfers between devices, across(): return lax.ppermute(x, AXES, pairs)  5.1 us
    all_to_all x1, starting transfers between devices, exchange(): return lax.all_to_all(x, axis, split_axis=0, concat_axis=0, tiled=False)  3.64 us
    all_to_all x1, waiting for transfers between devices, exchange(): return lax.all_to_all(x, axis, split_axis=0, concat_axis=0, tiled=False)  3.37 us
  transfers between devices with their start and end apart: 6, of which 5 were waited for; matrix products, arithmetic and copies ran while one was open for 0% of the time, Pallas kernels for 2%

profile of v10, /device:TPU:1, one launch (start us, length us, event | category | flops | bytes accessed | tf_op | source)
XLA Modules:
  0.0 123.1 jit_solution(7082179414124114065)
XLA Ops:
  0.6 0.9 shard_map.101
  1.6 20.9 %all_to_all.30 = bf16[24,24,128]{2,1,0:T(8,128)(2,1)S(1)} all-to-all(bf16[24,24,128]{2,1,0:T(8,128)(2,1)S(1)} %shard_map.101), channel_id=1, replica_groups=mesh['y'=8,'zh'=4,'x'=4,'zl'=3,'c'=2] {'x','zl','c'}, dimensions={0} | all-to-all | bytes 294912 | tf_op jit(solution)/shard_map/all_to_all | solution.py:236
  22.5 3.0 %collective-permute-start.1 = (bf16[576,128]{1,0:T(8,128)(2,1)S(1)}, bf16[576,128]{1,0:T(8,128)(2,1)S(1)}, u32[]{:S(2)}, u32[]{:S(2)}) collective-permute-start(bf16[576,128]{1,0:T(8,128)(2,1)S(1)} %bitcast.8), channel_id=1, source_target_pairs={{1,2},{3,4},{5,6},{7,8},{9,10},{11,12},{13,14},{15,16},{17,18},{19... | collective-permute-start | bytes 442376 | tf_op jit(solution)/shard_map/ppermute | solution.py:242
  25.5 1.9 %collective-permute-start = (bf16[576,128]{1,0:T(8,128)(2,1)S(1)}, bf16[576,128]{1,0:T(8,128)(2,1)S(1)}, u32[]{:S(2)}, u32[]{:S(2)}) collective-permute-start(bf16[576,128]{1,0:T(8,128)(2,1)S(1)} %bitcast.9), channel_id=1, source_target_pairs={{0,1},{1,0},{2,3},{3,2},{4,5},{5,4},{6,7},{7,6},{8,9},{9,8},{10,11... | collective-permute-start | bytes 442376 | tf_op jit(solution)/shard_map/ppermute | solution.py:245
  27.4 1.4 %shard_map.102 = (bf16[128,384]{1,0:T(8,128)(2,1)S(1)}, bf16[576,512]{1,0:T(8,128)(2,1)S(1)}, bf16[576,512]{1,0:T(8,128)(2,1)S(1)}, f32[1,512]{1,0:T(1,128)S(1)}, bf16[128,512]{1,0:T(8,128)(2,1)S(1)}) custom-call(s32[1]{0:T(128)} %bitcast.3.tile, bf16[3072,384]{1,0:T(8,128)(2,1)} %adjacency.1, bf16[576,512]{1,0:T(8,128)(2,1)} %refs_0_.1, ...), custom_call_target="tpu_custom_call" | custom-call | tf_op jit(solution)/shard_map/pallas_call | solution.py:266
  28.8 0.3 shard_map.103
  29.1 0.8 collective-permute-done.1.far
  29.9 0.0 collective-permute-done.near
  30.0 1.0 shard_map.104
  31.0 1.9 %collective-permute-start.2 = (bf16[1664,128]{1,0:T(8,128)(2,1)S(1)}, bf16[1664,128]{1,0:T(8,128)(2,1)S(1)}, u32[]{:S(2)}, u32[]{:S(2)}) collective-permute-start(bf16[1664,128]{1,0:T(8,128)(2,1)S(1)} %get-tuple-element.53), channel_id=1, source_target_pairs={{0,1},{1,0},{2,3},{3,2},{4,5},{5,4},{6,7},{7,6},{8,9},{9,8},{10,11... | collective-permute-start | bytes 1277960 | tf_op jit(solution)/shard_map/ppermute | solution.py:245
  32.9 1.7 %collective-permute-done.2.recv = bf16[1664,128]{1,0:T(8,128)(2,1)S(1)} collective-permute-done((bf16[1664,128]{1,0:T(8,128)(2,1)S(1)}, bf16[1664,128]{1,0:T(8,128)(2,1)S(1)}, u32[]{:S(2)}, u32[]{:S(2)}) %collective-permute-start.2) | collective-permute-done | bytes 426016 | tf_op jit(solution)/shard_map/ppermute | solution.py:245
  34.7 1.1 shard_map.105
  35.8 3.6 %all-to-all-start.1 = ((bf16[4,584,128]{2,1,0:T(8,128)(2,1)}), bf16[4,584,128]{2,1,0:T(8,128)(2,1)S(1)}, u32[]{:S(2)}, u32[]{:S(2)}) async-start(bf16[4,584,128]{2,1,0:T(8,128)(2,1)} %get-tuple-element.56), calls=%async_computation.1 | async-start | bytes 1196032 | tf_op jit(solution)/shard_map/all_to_all | solution.py:236
  39.4 2.4 %collective-permute-start.3 = (bf16[576,128]{1,0:T(8,128)(2,1)S(1)}, bf16[576,128]{1,0:T(8,128)(2,1)S(1)}, u32[]{:S(2)}, u32[]{:S(2)}) collective-permute-start(bf16[576,128]{1,0:T(8,128)(2,1)S(1)} %get-tuple-element.57.own), channel_id=1, source_target_pairs={{1,2},{3,4},{5,6},{7,8},{9,10},{11,12},{13,14},{15,16},{17,18},{19... | collective-permute-start | bytes 442376 | tf_op jit(solution)/shard_map/ppermute | solution.py:242
  41.9 4.3 %collective-permute-done.3.far = bf16[576,128]{1,0:T(8,128)(2,1)S(1)} collective-permute-done((bf16[576,128]{1,0:T(8,128)(2,1)S(1)}, bf16[576,128]{1,0:T(8,128)(2,1)S(1)}, u32[]{:S(2)}, u32[]{:S(2)}) %collective-permute-start.3) | collective-permute-done | bytes 147488 | tf_op jit(solution)/shard_map/ppermute | solution.py:242
  46.2 3.4 %all-to-all-done.1.recv = bf16[4,584,128]{2,1,0:T(8,128)(2,1)S(1)} async-done(((bf16[4,584,128]{2,1,0:T(8,128)(2,1)}), bf16[4,584,128]{2,1,0:T(8,128)(2,1)S(1)}, u32[]{:S(2)}, u32[]{:S(2)}) %all-to-all-start.1) | async-done | bytes 598048 | tf_op jit(solution)/shard_map/all_to_all | solution.py:236
  49.5 0.3 shard_map.106.feats
  49.8 0.1 shard_map.107
  49.9 21.3 %all_to_all.31.recv = bf16[8,80,128]{2,1,0:T(8,128)(2,1)S(1)} all-to-all(bf16[8,80,128]{2,1,0:T(8,128)(2,1)S(1)} %shard_map.107), channel_id=1, replica_groups=mesh['y'=8,'zh'=4,'x'=4,'zl'=3,'c'=2] {'y'}, dimensions={0} | all-to-all | bytes 327680 | tf_op jit(solution)/shard_map/all_to_all | solution.py:236
  71.2 15.2 %all_to_all.32.refs_0_ = bf16[12,32,128]{2,1,0:T(8,128)(2,1)S(1)} all-to-all(bf16[12,32,128]{2,1,0:T(8,128)(2,1)S(1)} %shard_map.108), channel_id=1, replica_groups=mesh['y'=8,'zh'=4,'x'=4,'zl'=3,'c'=2] {'zh','zl'}, dimensions={0} | all-to-all | bytes 196608 | tf_op jit(solution)/shard_map/all_to_all | solution.py:236
  86.4 0.6 shard_map.109
  87.0 9.4 %all_to_all.33 = bf16[8,24,128]{2,1,0:T(8,128)(2,1)S(1)} all-to-all(bf16[8,24,128]{2,1,0:T(8,128)(2,1)S(1)} %get-tuple-element.62), channel_id=1, replica_groups=mesh['y'=8,'zh'=4,'x'=4,'zl'=3,'c'=2] {'y'}, dimensions={0} | all-to-all | bytes 98304 | tf_op jit(solution)/shard_map/all_to_all | solution.py:236
  96.4 0.1 shard_map.110
  96.5 14.0 %all_to_all.34.block = bf16[12,240,128]{2,1,0:T(8,128)(2,1)S(1)} all-to-all(bf16[12,240,128]{2,1,0:T(8,128)(2,1)S(1)} %shard_map.110), channel_id=1, replica_groups=mesh['y'=8,'zh'=4,'x'=4,'zl'=3,'c'=2] {'x','zl'}, dimensions={0} | all-to-all | bytes 1474560 | tf_op jit(solution)/shard_map/all_to_all | solution.py:236
  110.5 9.5 %collective-permute-start.4 = (bf16[12,240,128]{2,1,0:T(8,128)(2,1)S(1)}, bf16[12,240,128]{2,1,0:T(8,128)(2,1)S(1)}, u32[]{:S(2)}, u32[]{:S(2)}) collective-permute-start(bf16[12,240,128]{2,1,0:T(8,128)(2,1)S(1)} %all_to_all.34.block), channel_id=1, source_target_pairs={{0,1},{1,0},{2,3},{3,2},{4,5},{5,4},{6,7},{7,6},{8,9},{9,8},{10,11... | collective-permute-start | bytes 2211848 | tf_op jit(solution)/shard_map/ppermute | solution.py:245
  120.0 1.2 %shard_map.111 = (f32[576,512]{1,0:T(8,128)}, f32[576,512]{1,0:T(8,128)}, f32[24,3072]{1,0:T(8,128)}) custom-call(s32[1]{0:T(128)} %bitcast.core, bf16[12,240,128]{2,1,0:T(8,128)(2,1)S(1)} %all_to_all.34.block), custom_call_target="tpu_custom_call" | custom-call | tf_op jit(solution)/shard_map/pallas_call | solution.py:319
  121.3 0.6 collective-permute-done.4.block
  121.9 1.2 %shard_map.112 = (f32[576,512]{1,0:T(8,128)}, f32[576,512]{1,0:T(8,128)}, f32[24,3072]{1,0:T(8,128)}) custom-call(s32[1]{0:T(128)} %bitcast.core, bf16[12,240,128]{2,1,0:T(8,128)(2,1)S(1)} %collective-permute-done.4.block, f32[576,512]{1,0:T(8,128)} %get-tuple-element.64.gs_in, ...), custom_call_target="tpu_custom_call", output_to_operand_aliasing={{0}: (2, {}), {1}: (3, {}), {2}: (4, {})} | custom-call | tf_op jit(solution)/shard_map/pallas_call | solution.py:322
  (1 shorter events, 0.0 us)
Async XLA Ops:
  22.5 7.5 %collective-permute-start.1 = (bf16[576,128]{1,0:T(8,128)(2,1)S(1)}, bf16[576,128]{1,0:T(8,128)(2,1)S(1)}, u32[]{:S(2)}, u32[]{:S(2)}) collective-permute-start(bf16[576,128]{1,0:T(8,128)(2,1)S(1)} %bitcast.8), channel_id=1, source_target_pairs={{1,2},{3,4},{5,6},{7,8},{9,10},{11,12},{13,14},{15,16},{17,18},{19... | collective-permute-start | bytes 442376 | tf_op jit(solution)/shard_map/ppermute | solution.py:242
  25.5 4.5 %collective-permute-start = (bf16[576,128]{1,0:T(8,128)(2,1)S(1)}, bf16[576,128]{1,0:T(8,128)(2,1)S(1)}, u32[]{:S(2)}, u32[]{:S(2)}) collective-permute-start(bf16[576,128]{1,0:T(8,128)(2,1)S(1)} %bitcast.9), channel_id=1, source_target_pairs={{0,1},{1,0},{2,3},{3,2},{4,5},{5,4},{6,7},{7,6},{8,9},{9,8},{10,11... | collective-permute-start | bytes 442376 | tf_op jit(solution)/shard_map/ppermute | solution.py:245
  31.0 3.7 %collective-permute-start.2 = (bf16[1664,128]{1,0:T(8,128)(2,1)S(1)}, bf16[1664,128]{1,0:T(8,128)(2,1)S(1)}, u32[]{:S(2)}, u32[]{:S(2)}) collective-permute-start(bf16[1664,128]{1,0:T(8,128)(2,1)S(1)} %get-tuple-element.53), channel_id=1, source_target_pairs={{0,1},{1,0},{2,3},{3,2},{4,5},{5,4},{6,7},{7,6},{8,9},{9,8},{10,11... | collective-permute-start | bytes 1277960 | tf_op jit(solution)/shard_map/ppermute | solution.py:245
  35.8 13.8 %all-to-all-start.1 = ((bf16[4,584,128]{2,1,0:T(8,128)(2,1)}), bf16[4,584,128]{2,1,0:T(8,128)(2,1)S(1)}, u32[]{:S(2)}, u32[]{:S(2)}) async-start(bf16[4,584,128]{2,1,0:T(8,128)(2,1)} %get-tuple-element.56), calls=%async_computation.1 | async-start | bytes 1196032 | tf_op jit(solution)/shard_map/all_to_all | solution.py:236
  39.4 6.7 %collective-permute-start.3 = (bf16[576,128]{1,0:T(8,128)(2,1)S(1)}, bf16[576,128]{1,0:T(8,128)(2,1)S(1)}, u32[]{:S(2)}, u32[]{:S(2)}) collective-permute-start(bf16[576,128]{1,0:T(8,128)(2,1)S(1)} %get-tuple-element.57.own), channel_id=1, source_target_pairs={{1,2},{3,4},{5,6},{7,8},{9,10},{11,12},{13,14},{15,16},{17,18},{19... | collective-permute-start | bytes 442376 | tf_op jit(solution)/shard_map/ppermute | solution.py:242
  110.5 11.4 %collective-permute-start.4 = (bf16[12,240,128]{2,1,0:T(8,128)(2,1)S(1)}, bf16[12,240,128]{2,1,0:T(8,128)(2,1)S(1)}, u32[]{:S(2)}, u32[]{:S(2)}) collective-permute-start(bf16[12,240,128]{2,1,0:T(8,128)(2,1)S(1)} %all_to_all.34.block), channel_id=1, source_target_pairs={{0,1},{1,0},{2,3},{3,2},{4,5},{5,4},{6,7},{7,6},{8,9},{9,8},{10,11... | collective-permute-start | bytes 2211848 | tf_op jit(solution)/shard_map/ppermute | solution.py:245

commit v11 on v10

--- a/solution.py
+++ b/solution.py
@@ -293,13 +293,12 @@
         partial_kernel, [VMEM] * 4, (sds((N_X, f_in + TAIL, TILE)), sds((TILE, f_out)))
     )(keep, grad, recv, act)
     from_x = exchange(partial, "x")
-    from_x, s_far = lax.optimization_barrier((from_x, s_far))
     feats = call(feat_kernel, [SMEM] + [VMEM] * 5, sds((N_LINE, 2 * width, TILE)))(
         core, recv, s_far, scaled, adj, back
     )
-    from_x, feats = lax.optimization_barrier((from_x, feats))
     from_y = exchange(call(x_kernel, [VMEM], sds((N_Y, ROWS + TAIL, TILE)))(from_x), "y")
     from_line = exchange(call(y_kernel, [VMEM], sds((N_LINE, THIRD + TAIL, TILE)))(from_y), LINE)
+    from_line, feats = lax.optimization_barrier((from_line, feats))
     to_y_again, bias_sum = call(
         lambda *refs: line_kernel(scale, *refs),
         [VMEM],

time: 124 us -> 125 us (level)
  starting transfers between devices: 22.4 us -> 26.4 us
  waiting for transfers between devices: 10.8 us -> 8.13 us
    ppermute x3, starting transfers between devices: 13.4 us -> 8.95 us  [swap(): return lax.ppermute(x, 'c', [(0, 1), (1, 0)])]
    ppermute x2, starting transfers between devices: 5.42 us -> 9.65 us  [across(): return lax.ppermute(x, AXES, pairs)]
    all_to_all x1, starting transfers between devices: 3.64 us -> 7.84 us  [exchange(): return lax.all_to_all(x, axis, split_axis=0, concat_axis=0, tiled=False)]
    all_to_all x1, waiting for transfers between devices: 3.37 us -> 0.01 us  [exchange(): return lax.all_to_all(x, axis, split_axis=0, concat_axis=0, tiled=False)]
  transfers between devices with their start and end apart: 6 -> 6, of which waited for: 5 -> 4; matrix products, arithmetic and copies ran while one was open for 0% -> 0% of each run, Pallas kernels for 2% -> 3%
where the time goes in v11:
time: 125 us; the launch traced here: 124 us
  blocking collectives  80.2 us (64%)
  starting transfers between devices  26.4 us (21%)
  Pallas kernels  8.79 us (7%)
  waiting for transfers between devices  8.13 us (7%)
    all_to_all x5, blocking collectives, exchange(): return lax.all_to_all(x, axis, split_axis=0, concat_axis=0, tiled=False)  80.2 us
    ppermute x2, starting transfers between devices, across(): return lax.ppermute(x, AXES, pairs)  9.65 us
    ppermute x3, starting transfers between devices, swap(): return lax.ppermute(x, 'c', [(0, 1), (1, 0)])  8.95 us
    all_to_all x1, starting transfers between devices, exchange(): return lax.all_to_all(x, axis, split_axis=0, concat_axis=0, tiled=False)  7.84 us
    ppermute x2, waiting for transfers between devices, across(): return lax.ppermute(x, AXES, pairs)  5.82 us
  transfers between devices with their start and end apart: 6, of which 4 were waited for; matrix products, arithmetic and copies ran while one was open for 0% of the time, Pallas kernels for 3%

profile of v11, /device:TPU:1, one launch (start us, length us, event | category | flops | bytes accessed | tf_op | source)
XLA Modules:
  0.0 124.3 jit_solution(10414147816726668320)
XLA Ops:
  0.6 0.9 shard_map.101
  1.6 20.9 %all_to_all.30 = bf16[24,24,128]{2,1,0:T(8,128)(2,1)S(1)} all-to-all(bf16[24,24,128]{2,1,0:T(8,128)(2,1)S(1)} %shard_map.101), channel_id=1, replica_groups=mesh['y'=8,'zh'=4,'x'=4,'zl'=3,'c'=2] {'x','zl','c'}, dimensions={0} | all-to-all | bytes 294912 | tf_op jit(solution)/shard_map/all_to_all | solution.py:236
  22.5 3.0 %collective-permute-start.1 = (bf16[576,128]{1,0:T(8,128)(2,1)S(1)}, bf16[576,128]{1,0:T(8,128)(2,1)S(1)}, u32[]{:S(2)}, u32[]{:S(2)}) collective-permute-start(bf16[576,128]{1,0:T(8,128)(2,1)S(1)} %bitcast.8), channel_id=1, source_target_pairs={{1,2},{3,4},{5,6},{7,8},{9,10},{11,12},{13,14},{15,16},{17,18},{19... | collective-permute-start | bytes 442376 | tf_op jit(solution)/shard_map/ppermute | solution.py:242
  25.5 1.9 %collective-permute-start = (bf16[576,128]{1,0:T(8,128)(2,1)S(1)}, bf16[576,128]{1,0:T(8,128)(2,1)S(1)}, u32[]{:S(2)}, u32[]{:S(2)}) collective-permute-start(bf16[576,128]{1,0:T(8,128)(2,1)S(1)} %bitcast.9), channel_id=1, source_target_pairs={{0,1},{1,0},{2,3},{3,2},{4,5},{5,4},{6,7},{7,6},{8,9},{9,8},{10,11... | collective-permute-start | bytes 442376 | tf_op jit(solution)/shard_map/ppermute | solution.py:245
  27.4 1.4 %shard_map.102 = (bf16[128,384]{1,0:T(8,128)(2,1)S(1)}, bf16[576,512]{1,0:T(8,128)(2,1)S(1)}, bf16[576,512]{1,0:T(8,128)(2,1)S(1)}, f32[1,512]{1,0:T(1,128)S(1)}, bf16[128,512]{1,0:T(8,128)(2,1)S(1)}) custom-call(s32[1]{0:T(128)} %bitcast.3.tile, bf16[3072,384]{1,0:T(8,128)(2,1)} %adjacency.1, bf16[576,512]{1,0:T(8,128)(2,1)} %refs_0_.1, ...), custom_call_target="tpu_custom_call" | custom-call | tf_op jit(solution)/shard_map/pallas_call | solution.py:266
  28.8 0.3 shard_map.103
  29.1 0.8 collective-permute-done.1.far
  29.9 0.0 collective-permute-done.near
  30.0 1.0 shard_map.104
  31.0 1.9 %collective-permute-start.2 = (bf16[1664,128]{1,0:T(8,128)(2,1)S(1)}, bf16[1664,128]{1,0:T(8,128)(2,1)S(1)}, u32[]{:S(2)}, u32[]{:S(2)}) collective-permute-start(bf16[1664,128]{1,0:T(8,128)(2,1)S(1)} %get-tuple-element.51), channel_id=1, source_target_pairs={{0,1},{1,0},{2,3},{3,2},{4,5},{5,4},{6,7},{7,6},{8,9},{9,8},{10,11... | collective-permute-start | bytes 1277960 | tf_op jit(solution)/shard_map/ppermute | solution.py:245
  32.9 1.7 %collective-permute-done.2.recv = bf16[1664,128]{1,0:T(8,128)(2,1)S(1)} collective-permute-done((bf16[1664,128]{1,0:T(8,128)(2,1)S(1)}, bf16[1664,128]{1,0:T(8,128)(2,1)S(1)}, u32[]{:S(2)}, u32[]{:S(2)}) %collective-permute-start.2) | collective-permute-done | bytes 426016 | tf_op jit(solution)/shard_map/ppermute | solution.py:245
  34.7 0.9 shard_map.105
  35.6 13.1 %all_to_all.31.recv = bf16[4,584,128]{2,1,0:T(8,128)(2,1)S(1)} all-to-all(bf16[4,584,128]{2,1,0:T(8,128)(2,1)S(1)} %get-tuple-element.54), channel_id=1, replica_groups=mesh['y'=8,'zh'=4,'x'=4,'zl'=3,'c'=2] {'x'}, dimensions={0} | all-to-all | bytes 1196032 | tf_op jit(solution)/shard_map/all_to_all | solution.py:236
  48.7 0.1 shard_map.106
  48.8 18.5 %all_to_all.32.recv = bf16[8,80,128]{2,1,0:T(8,128)(2,1)S(1)} all-to-all(bf16[8,80,128]{2,1,0:T(8,128)(2,1)S(1)} %shard_map.106), channel_id=1, replica_groups=mesh['y'=8,'zh'=4,'x'=4,'zl'=3,'c'=2] {'y'}, dimensions={0} | all-to-all | bytes 327680 | tf_op jit(solution)/shard_map/all_to_all | solution.py:236
  67.3 0.7 shard_map.107
  67.9 7.8 %all-to-all-start.3 = ((bf16[12,32,128]{2,1,0:T(8,128)(2,1)}), bf16[12,32,128]{2,1,0:T(8,128)(2,1)S(1)}, u32[]{:S(2)}, u32[]{:S(2)}) async-start(bf16[12,32,128]{2,1,0:T(8,128)(2,1)} %shard_map.107), calls=%async_computation.3 | async-start | bytes 196608 | tf_op jit(solution)/shard_map/all_to_all | solution.py:236
  75.8 6.7 %collective-permute-start.3 = (bf16[576,128]{1,0:T(8,128)(2,1)S(1)}, bf16[576,128]{1,0:T(8,128)(2,1)S(1)}, u32[]{:S(2)}, u32[]{:S(2)}) collective-permute-start(bf16[576,128]{1,0:T(8,128)(2,1)S(1)} %get-tuple-element.55.own), channel_id=1, source_target_pairs={{1,2},{3,4},{5,6},{7,8},{9,10},{11,12},{13,14},{15,16},{17,18},{19... | collective-permute-start | bytes 442376 | tf_op jit(solution)/shard_map/ppermute | solution.py:242
  82.5 5.0 %collective-permute-done.3.far = bf16[576,128]{1,0:T(8,128)(2,1)S(1)} collective-permute-done((bf16[576,128]{1,0:T(8,128)(2,1)S(1)}, bf16[576,128]{1,0:T(8,128)(2,1)S(1)}, u32[]{:S(2)}, u32[]{:S(2)}) %collective-permute-start.3) | collective-permute-done | bytes 147488 | tf_op jit(solution)/shard_map/ppermute | solution.py:242
  87.5 0.3 shard_map.108.feats
  87.8 0.0 all-to-all-done.3.refs_0_
  87.8 0.6 shard_map.109
  88.4 9.4 %all_to_all.33 = bf16[8,24,128]{2,1,0:T(8,128)(2,1)S(1)} all-to-all(bf16[8,24,128]{2,1,0:T(8,128)(2,1)S(1)} %get-tuple-element.58), channel_id=1, replica_groups=mesh['y'=8,'zh'=4,'x'=4,'zl'=3,'c'=2] {'y'}, dimensions={0} | all-to-all | bytes 98304 | tf_op jit(solution)/shard_map/all_to_all | solution.py:236
  97.8 0.1 shard_map.110
  97.9 18.2 %all_to_all.34.block = bf16[12,240,128]{2,1,0:T(8,128)(2,1)S(1)} all-to-all(bf16[12,240,128]{2,1,0:T(8,128)(2,1)S(1)} %shard_map.110), channel_id=1, replica_groups=mesh['y'=8,'zh'=4,'x'=4,'zl'=3,'c'=2] {'x','zl'}, dimensions={0} | all-to-all | bytes 1474560 | tf_op jit(solution)/shard_map/all_to_all | solution.py:236
  116.1 5.1 %collective-permute-start.4 = (bf16[12,240,128]{2,1,0:T(8,128)(2,1)S(1)}, bf16[12,240,128]{2,1,0:T(8,128)(2,1)S(1)}, u32[]{:S(2)}, u32[]{:S(2)}) collective-permute-start(bf16[12,240,128]{2,1,0:T(8,128)(2,1)S(1)} %all_to_all.34.block), channel_id=1, source_target_pairs={{0,1},{1,0},{2,3},{3,2},{4,5},{5,4},{6,7},{7,6},{8,9},{9,8},{10,11... | collective-permute-start | bytes 2211848 | tf_op jit(solution)/shard_map/ppermute | solution.py:245
  121.2 1.2 %shard_map.111 = (f32[576,512]{1,0:T(8,128)}, f32[576,512]{1,0:T(8,128)}, f32[24,3072]{1,0:T(8,128)}) custom-call(s32[1]{0:T(128)} %bitcast.core, bf16[12,240,128]{2,1,0:T(8,128)(2,1)S(1)} %all_to_all.34.block), custom_call_target="tpu_custom_call" | custom-call | tf_op jit(solution)/shard_map/pallas_call | solution.py:318
  122.5 0.6 collective-permute-done.4.block
  123.0 1.2 shard_map.112
Async XLA Ops:
  22.5 7.5 %collective-permute-start.1 = (bf16[576,128]{1,0:T(8,128)(2,1)S(1)}, bf16[576,128]{1,0:T(8,128)(2,1)S(1)}, u32[]{:S(2)}, u32[]{:S(2)}) collective-permute-start(bf16[576,128]{1,0:T(8,128)(2,1)S(1)} %bitcast.8), channel_id=1, source_target_pairs={{1,2},{3,4},{5,6},{7,8},{9,10},{11,12},{13,14},{15,16},{17,18},{19... | collective-permute-start | bytes 442376 | tf_op jit(solution)/shard_map/ppermute | solution.py:242
  25.5 4.5 %collective-permute-start = (bf16[576,128]{1,0:T(8,128)(2,1)S(1)}, bf16[576,128]{1,0:T(8,128)(2,1)S(1)}, u32[]{:S(2)}, u32[]{:S(2)}) collective-permute-start(bf16[576,128]{1,0:T(8,128)(2,1)S(1)} %bitcast.9), channel_id=1, source_target_pairs={{0,1},{1,0},{2,3},{3,2},{4,5},{5,4},{6,7},{7,6},{8,9},{9,8},{10,11... | collective-permute-start | bytes 442376 | tf_op jit(solution)/shard_map/ppermute | solution.py:245
  31.0 3.7 %collective-permute-start.2 = (bf16[1664,128]{1,0:T(8,128)(2,1)S(1)}, bf16[1664,128]{1,0:T(8,128)(2,1)S(1)}, u32[]{:S(2)}, u32[]{:S(2)}) collective-permute-start(bf16[1664,128]{1,0:T(8,128)(2,1)S(1)} %get-tuple-element.51), channel_id=1, source_target_pairs={{0,1},{1,0},{2,3},{3,2},{4,5},{5,4},{6,7},{7,6},{8,9},{9,8},{10,11... | collective-permute-start | bytes 1277960 | tf_op jit(solution)/shard_map/ppermute | solution.py:245
  67.9 19.8 %all-to-all-start.3 = ((bf16[12,32,128]{2,1,0:T(8,128)(2,1)}), bf16[12,32,128]{2,1,0:T(8,128)(2,1)S(1)}, u32[]{:S(2)}, u32[]{:S(2)}) async-start(bf16[12,32,128]{2,1,0:T(8,128)(2,1)} %shard_map.107), calls=%async_computation.3 | async-start | bytes 196608 | tf_op jit(solution)/shard_map/all_to_all | solution.py:236
  75.8 11.7 %collective-permute-start.3 = (bf16[576,128]{1,0:T(8,128)(2,1)S(1)}, bf16[576,128]{1,0:T(8,128)(2,1)S(1)}, u32[]{:S(2)}, u32[]{:S(2)}) collective-permute-start(bf16[576,128]{1,0:T(8,128)(2,1)S(1)} %get-tuple-element.55.own), channel_id=1, source_target_pairs={{1,2},{3,4},{5,6},{7,8},{9,10},{11,12},{13,14},{15,16},{17,18},{19... | collective-permute-start | bytes 442376 | tf_op jit(solution)/shard_map/ppermute | solution.py:242
  116.1 6.9 %collective-permute-start.4 = (bf16[12,240,128]{2,1,0:T(8,128)(2,1)S(1)}, bf16[12,240,128]{2,1,0:T(8,128)(2,1)S(1)}, u32[]{:S(2)}, u32[]{:S(2)}) collective-permute-start(bf16[12,240,128]{2,1,0:T(8,128)(2,1)S(1)} %all_to_all.34.block), channel_id=1, source_target_pairs={{0,1},{1,0},{2,3},{3,2},{4,5},{5,4},{6,7},{7,6},{8,9},{9,8},{10,11... | collective-permute-start | bytes 2211848 | tf_op jit(solution)/shard_map/ppermute | solution.py:245
